TPU v7x, 32 devices: a whole 2x2x4 slice. The times are simulated.
32 devices in a mesh: dp: 8 (over z, y), mp: 4 (over x, core).
Axes of the slice: x: 2, y: 2, z: 4, core: 2. Of those that a mesh axis runs over, the one named last changes fastest.
Arguments:
- tokens: bfloat16 [32, 412, 768], P('dp'), may hold values from -6 to 6
- cotangent: bfloat16 [32, 512, 768], P('dp'), may hold values from -6 to 6
- segment_ids: int32 [32, 412], P('dp'), may hold values from 0 to 3, never falling along the last dimension, each value on 1 to 206 neighbouring positions
- prompt_ids: int32 [100], replicated, may hold values from 0 to 32127
- rel_buckets: int32 [1023], replicated, may hold values from 0 to 31
- table: bfloat16 [32128, 768], P('dp'), may hold values from -6 to 6
- prompt_delta: float32 [76800], P('dp'), may hold values from -6 to 6
- norm1_gain: float32 [768], replicated, may hold values from 0.25 to 1.75
- w_query: bfloat16 [768, 768], P(None, 'mp'), may hold values from -0.0546875 to 0.0546875
- w_key: bfloat16 [768, 768], P(None, 'mp'), may hold values from -0.21875 to 0.21875
- w_value: bfloat16 [768, 768], P(None, 'mp'), may hold values from -0.21875 to 0.21875
- w_output: bfloat16 [768, 768], P('mp'), may hold values from -0.3125 to 0.3125
- rel_bias: float32 [32, 12], P(None, 'mp'), may hold values from -4 to 4
- norm2_gain: float32 [768], replicated, may hold values from 0.25 to 1.75
- w_inner: bfloat16 [768, 3072], P(None, 'mp'), may hold values from -0.21875 to 0.21875
- w_outer: bfloat16 [3072, 768], P('mp'), may hold values from -0.109375 to 0.109375
Outputs:
- out: bfloat16 [32, 512, 768], P('dp')
- grad_tokens: bfloat16 [32, 412, 768], P('dp')
- grad_prompt: float32 [76800], P('dp')
- grad_norm1: float32 [768], P('dp')
- grad_query: float32 [768, 768], P('dp', 'mp')
- grad_key: float32 [768, 768], P('dp', 'mp')
- grad_value: float32 [768, 768], P('dp', 'mp')
- grad_output: float32 [768, 768], P('mp', 'dp')
- grad_rel: float32 [32, 12], P('dp', 'mp')
- grad_norm2: float32 [768], P('dp')
- grad_inner: float32 [768, 3072], P('dp', 'mp')
- grad_outer: float32 [3072, 768], P('mp', 'dp')
Inputs may be any that keep to these rules, and one draw needn't show every extreme that they name: `segment_ids`: in each pack the ids never fall and every id from 0 to 3 holds 1 to 206 rows; some id holds exactly 206.
All inputs are finite; a program needn't handle non-finite values.
Results may differ from a plain program's by a relative error of at most 0.025.
Values may be sent and summed in bfloat16 or wider, within the bound.
No kernel may reach another device: no remote copies, remote signals or barrier semaphores. Data moves between devices by JAX's collectives and lax.ppermute only.
A program may use at most 128 MiB of HBM per device.

v0:
```python
import functools

import jax
import jax.numpy as jnp
from jax import lax
from jax.experimental import pallas as pl
from jax.experimental.pallas import tpu as pltpu
from jax.sharding import PartitionSpec as P

epsilon = 1e-06
blocked = -1000000000.0
highest = lax.Precision.HIGHEST
low = jnp.bfloat16
wide = jnp.float32
root_half = 0.7071067811865476
inv_root_tau = 0.3989422804014327


def nn(left, right):
    return lax.dot_general(left, right, (((1,), (0,)), ((), ())), preferred_element_type=wide)


def nt(left, right):
    return lax.dot_general(left, right, (((1,), (1,)), ((), ())), preferred_element_type=wide)


def tn(left, right):
    return lax.dot_general(left, right, (((0,), (0,)), ((), ())), preferred_element_type=wide)


def params(mebibytes):
    return pltpu.CompilerParams(vmem_limit_bytes=mebibytes * 1024 * 1024)


def in_hbm(shape, dtype):
    return pltpu.HBM(shape, dtype)


def kernel_call(kernel, micros, vmem=16, near=(), least=400000, **rest):
    cost = pl.CostEstimate(flops=0, bytes_accessed=int(micros * 3.6e6), transcendentals=0)
    call = pl.pallas_call(kernel, cost_estimate=cost, compiler_params=params(vmem), **rest)

    def run(*args):
        return call(
            *[
                pltpu.with_memory_space_constraint(v, pltpu.HBM) if (v.size >= least or v.ndim == 4) and i not in near else v
                for i, v in enumerate(args)
            ]
        )

    return run


def swap(value, axis, bit):
    count = lax.axis_size(axis)
    return lax.ppermute(value, axis, [(i, i ^ bit) for i in range(count)])


def bits_of(count):
    return [1 << i for i in range(count.bit_length() - 1)]


def rms_norm(values, gain):
    return values * lax.rsqrt(jnp.mean(values * values, axis=-1, keepdims=True) + epsilon) * gain


def norm_back(upstream, gain, values):
    scale = lax.rsqrt(jnp.mean(values * values, axis=-1, keepdims=True) + epsilon)
    scaled = upstream * gain
    inner = jnp.mean(scaled * values, axis=-1, keepdims=True)
    grad = scale * scaled - values * (scale * scale * scale * inner)
    return grad, jnp.sum(upstream * values * scale, axis=0, keepdims=True)


def bias_kernel(line_ref, grid_ref):
    rows = grid_ref.shape[1]
    spread = jnp.broadcast_to(line_ref[0], (rows, 2 * rows))
    grid_ref[0] = pltpu.roll(spread, 0, 1, stride=1, stride_axis=0)[:, :rows]


def bias_grid_of(line):
    heads, _, double = line.shape
    rows = double // 2
    return kernel_call(
        bias_kernel, 2,
        grid=(heads,),
        in_specs=[pl.BlockSpec((1, 1, double), lambda h: (h, 0, 0))],
        out_specs=pl.BlockSpec((1, rows, rows), lambda h: (h, 0, 0)),
        out_shape=jax.ShapeDtypeStruct((heads, rows, rows), wide),
        name="bias_grid",
    )(line)


def diag_kernel(grid_ref, line_ref):
    packs, _, rows, _ = grid_ref.shape
    lanes = 128
    count = rows // lanes
    blocks = []
    for block in range(2 * count):
        total = jnp.zeros((lanes, lanes), wide)
        for band in range(count):
            column = (block + band) % (2 * count)
            if column < count:
                for pack in range(packs):
                    total = total + grid_ref[
                        pack, 0, band * lanes : (band + 1) * lanes, column * lanes : (column + 1) * lanes
                    ].astype(wide)
        blocks.append(total)
    held = jnp.concatenate(blocks, axis=1)
    total = held[:8]
    for slab in range(1, lanes // 8):
        total = total + pltpu.roll(held[8 * slab : 8 * slab + 8], 2 * rows - 8 * slab, 1)
    line = total[0:1]
    for row in range(1, 8):
        line = line + pltpu.roll(total[row : row + 1], 2 * rows - row, 1)
    line_ref[0] = line


def diagonal_sums(grid):
    packs, heads, rows, _ = grid.shape
    return kernel_call(
        diag_kernel, 3,
        grid=(heads,),
        in_specs=[pl.BlockSpec((packs, 1, rows, rows), lambda h: (0, h, 0, 0))],
        out_specs=pl.BlockSpec((1, 1, 2 * rows), lambda h: (h, 0, 0)),
        out_shape=in_hbm((heads, 1, 2 * rows), wide),
        name="diagonal_sums",
    )(grid)


def shifted_text_kernel(tokens_ref, gain_ref, weight_ref, *refs):
    rows_ref, normed_ref, joined_ref, wide_ref = refs[-4:]
    rows = rows_ref.shape[1]
    prompt_len = rows - tokens_ref.shape[1]
    wide_ref[:prompt_len, :] = jnp.zeros((prompt_len, wide_ref.shape[1]), wide)
    wide_ref[prompt_len:, :] = tokens_ref[0].astype(wide)
    values = wide_ref[...]
    rows_ref[0] = values.astype(low)
    normed = rms_norm(values, gain_ref[...]).astype(low)
    normed_ref[0] = normed
    joined_ref[0] = nt(normed, weight_ref[...]).astype(low)


def text_projections(first, count, rows, tokens, gain, weight, kept):
    packs, text, model = tokens.shape
    triple = weight.shape[0]
    fixed = lambda p: (0, 0)
    moving = lambda p: (first + p, 0, 0)
    return kernel_call(
        shifted_text_kernel, 1.2 * count,
        grid=(count,),
        in_specs=[
            pl.BlockSpec((1, text, model), moving),
            pl.BlockSpec((1, model), fixed),
            pl.BlockSpec((triple, model), fixed),
        ]
        + [pl.BlockSpec(memory_space=pl.ANY)] * len(kept),
        out_specs=[
            pl.BlockSpec((1, rows, model), moving),
            pl.BlockSpec((1, rows, model), moving),
            pl.BlockSpec((1, rows, triple), moving),
        ],
        out_shape=[
            in_hbm((packs, rows, model), low),
            in_hbm((packs, rows, model), low),
            in_hbm((packs, rows, triple), low),
        ],
        scratch_shapes=[pltpu.VMEM((rows, model), wide)],
        input_output_aliases={3 + i: i for i in range(len(kept))},
        name="text_projections",
    )(tokens, gain, weight, *kept)


def prompt_kernel(place_ref, pieces_ref, gain_ref, weight_ref, rows_in, normed_in, joined_in, rows_out, normed_out, joined_out,
                  prompt_ref, rows_ref, normed_ref, joined_ref, load_sems, save_sems):
    count, part, _ = pieces_ref.shape
    packs = rows_ref.shape[0]
    top = count * part
    held = (rows_ref, normed_ref, joined_ref)
    loads = [
        pltpu.make_async_copy(source.at[:, pl.ds(0, top)], target, load_sems.at[i])
        for i, (source, target) in enumerate(zip((rows_in, normed_in, joined_in), held))
    ]
    for copy in loads:
        copy.start()
    for k in range(count):
        start = pl.multiple_of(jnp.bitwise_xor(place_ref[0], k) * part, part)
        prompt_ref[pl.ds(start, part), :] = pieces_ref[k]
    prompt = prompt_ref[...]
    normed = rms_norm(prompt.astype(wide), gain_ref[...]).astype(low)
    joined = nt(normed, weight_ref[...]).astype(low)
    saves = []
    for i, (value, target) in enumerate(zip((prompt, normed, joined), (rows_out, normed_out, joined_out))):
        loads[i].wait()
        for pack in range(packs):
            held[i][pack] = held[i][pack] + value
        copy = pltpu.make_async_copy(held[i], target.at[:, pl.ds(0, top)], save_sems.at[i])
        copy.start()
        saves.append(copy)
    for copy in saves:
        copy.wait()


def add_prompt(place, pieces, gain, weight, rows, normed, joined):
    packs, _, model = rows.shape
    triple = weight.shape[0]
    count, part, _ = pieces.shape
    top = count * part
    inside = pl.BlockSpec(memory_space=pltpu.VMEM)
    anywhere = pl.BlockSpec(memory_space=pl.ANY)
    return kernel_call(
        prompt_kernel, 2.5,
        in_specs=[pl.BlockSpec(memory_space=pltpu.SMEM)] + [inside] * 3 + [anywhere] * 3,
        out_specs=[anywhere] * 3,
        out_shape=[
            in_hbm(rows.shape, low),
            in_hbm(normed.shape, low),
            in_hbm(joined.shape, low),
        ],
        scratch_shapes=[
            pltpu.VMEM((top, model), low),
            pltpu.VMEM((packs, top, model), low),
            pltpu.VMEM((packs, top, model), low),
            pltpu.VMEM((packs, top, triple), low),
            pltpu.SemaphoreType.DMA((3,)),
            pltpu.SemaphoreType.DMA((3,)),
        ],
        input_output_aliases={4: 0, 5: 1, 6: 2},
        name="add_prompt",
    )(place, pieces, gain, weight, rows, normed, joined)


def look_up_kernel(ids_ref, table_any, placed_ref, out_ref, blocks_ref, total_ref, sems):
    part = out_ref.shape[0]
    limit = table_any.shape[0]
    copies, inside = [], []
    for row in range(part):
        local = jnp.clip(ids_ref[row], 0, limit - 1)
        inside.append(local)
        start = pl.multiple_of(jnp.left_shift(jnp.right_shift(local, 4), 4), 16)
        copies.append(
            pltpu.make_async_copy(table_any.at[pl.ds(start, 16)], blocks_ref.at[row], sems.at[row])
        )
    for copy in copies:
        copy.start()
    for copy in copies:
        copy.wait()
    position = lax.broadcasted_iota(jnp.int32, blocks_ref.shape[1:], 0)
    for row in range(part):
        own = inside[row] == ids_ref[row]
        chosen = (position == jnp.bitwise_and(inside[row], 15)) & own
        found = jnp.sum(jnp.where(chosen, blocks_ref[row].astype(wide), 0.0), axis=0, keepdims=True)
        total_ref[row : row + 1, :] = placed_ref[row : row + 1, :] + found
    out_ref[...] = total_ref[...].astype(low)


def look_up_rows(ids, table, placed):
    part, model = placed.shape
    inside = pl.BlockSpec(memory_space=pltpu.VMEM)
    return kernel_call(
        look_up_kernel, 2.5,
        in_specs=[pl.BlockSpec(memory_space=pltpu.SMEM), pl.BlockSpec(memory_space=pl.ANY), inside],
        out_specs=inside,
        out_shape=jax.ShapeDtypeStruct((part, model), low),
        scratch_shapes=[
            pltpu.VMEM((part, 16, model), low),
            pltpu.VMEM((part, model), wide),
            pltpu.SemaphoreType.DMA((part,)),
        ],
        name="look_up",
    )(ids, table, placed)


def attention_step_kernel(
    prompt_len, heads, first, last, step, core_ref, joined_any, bias_ref, seg_rows_ref, seg_cols_ref, w_out_ref, *refs,
):
    turns = list(range(first, last + 1))
    refs = list(refs)
    if last == 1:
        got_ref, refs = refs[0], refs[1:]
    joined_ref, probs_ref, mixed_ref, load_sems, save_sems = refs[-5:]
    outs = refs[-5 - 2 * len(turns) - 1 : -5]
    flat_refs, probs_outs, mixed_any = outs[: len(turns)], outs[len(turns) : -1], outs[-1]
    rows = joined_ref.shape[1]
    half = rows // 2
    width = w_out_ref.shape[0]
    size = width // heads
    loads = [
        pltpu.make_async_copy(joined_any.at[step - turn], joined_ref.at[i], load_sems.at[i])
        for i, turn in enumerate(turns)
    ]
    for copy in loads:
        copy.start()
    saves = []
    col_pos = lax.broadcasted_iota(jnp.int32, (half, rows), 1)
    for i, turn in enumerate(turns):
        pack = step - turn
        mine = jnp.bitwise_xor(core_ref[0], 1 - turn)
        start = pl.multiple_of(mine * half, half)
        here = pl.ds(start, half)
        row_pos = start + lax.broadcasted_iota(jnp.int32, (half, rows), 0)
        allowed = (
            (row_pos < prompt_len)
            | (col_pos < prompt_len)
            | (seg_rows_ref[here, pack : pack + 1] == seg_cols_ref[pack : pack + 1, :])
        )
        loads[i].wait()
        queries = joined_ref[i, here, :width]
        mixed = []
        for head in range(heads):
            keys = joined_ref[i, :, width + head * size : width + (head + 1) * size]
            values = joined_ref[i, :, 2 * width + head * size : 2 * width + (head + 1) * size]
            scores = nt(queries[:, head * size : (head + 1) * size], keys) + bias_ref[head, here, :]
            scores = jnp.where(allowed, scores, blocked)
            top = jnp.max(scores, axis=-1, keepdims=True)
            raised = jnp.exp(scores - top)
            total = jnp.sum(raised, axis=-1, keepdims=True)
            probs = (raised * (1.0 / total)).astype(low)
            probs_ref[i, head] = probs
            copy = pltpu.make_async_copy(
                probs_ref.at[i, head], probs_outs[i].at[0, head], save_sems.at[i * (heads + 1) + head]
            )
            copy.start()
            saves.append(copy)
            mixed.append(nn(probs, values).astype(low))
        mixed = jnp.concatenate(mixed, axis=1)
        mixed_ref[i] = mixed
        copy = pltpu.make_async_copy(
            mixed_ref.at[i], mixed_any.at[pack, here], save_sems.at[i * (heads + 1) + heads]
        )
        copy.start()
        saves.append(copy)
        share = nn(mixed, w_out_ref[...])
        if turn == 1:
            share = share + got_ref[...].astype(wide)
        flat_refs[i][...] = share.astype(low)
    for copy in saves:
        copy.wait()


def attention_step(step, packs, prompt_len, core, joined, bias, seg_rows, seg_cols, w_out, got, mixed_all):
    _, rows, triple = joined.shape
    heads = bias.shape[0]
    width, model = w_out.shape
    half = rows // 2
    first, last = (0 if step < packs else 1), (1 if step > 0 else 0)
    steps = last - first + 1
    inside = pl.BlockSpec(memory_space=pltpu.VMEM)
    anywhere = pl.BlockSpec(memory_space=pl.ANY)
    in_specs = [pl.BlockSpec(memory_space=pltpu.SMEM), anywhere] + [inside] * 4
    args = [core, joined, bias, seg_rows, seg_cols, w_out]
    if last == 1:
        in_specs.append(inside)
        args.append(got)
    aliases = {}
    if mixed_all is not None:
        aliases = {len(args): 2 * steps}
        in_specs.append(anywhere)
        args.append(mixed_all)
    outs = kernel_call(
        functools.partial(attention_step_kernel, prompt_len, heads, first, last, step), 5, near=(2,), vmem=24,
        in_specs=in_specs,
        out_specs=[inside] * steps + [anywhere] * (steps + 1),
        out_shape=[jax.ShapeDtypeStruct((half, model), low)] * steps
        + [in_hbm((1, heads, half, rows), low)] * steps
        + [in_hbm((packs, rows, width), low)],
        scratch_shapes=[
            pltpu.VMEM((steps, rows, triple), low),
            pltpu.VMEM((steps, heads, half, rows), low),
            pltpu.VMEM((steps, half, width), low),
            pltpu.SemaphoreType.DMA((steps,)),
            pltpu.SemaphoreType.DMA((steps * (heads + 1),)),
        ],
        input_output_aliases=aliases,
        name="attention_step",
    )(*args)
    send, probs_send = (outs[0], outs[steps]) if first == 0 else (None, None)
    pair, probs_own = (outs[steps - 1], outs[2 * steps - 1]) if last == 1 else (None, None)
    return send, pair, probs_send, probs_own, outs[-1]


def feed_step_kernel(first, last, step, place_ref, rows_any, cot_any, gain_ref, *refs):
    refs = list(refs)
    turns = list(range(first, last + 1))
    sums = [refs[2 * i : 2 * i + 2] for i in range(len(turns))]
    refs = refs[2 * len(turns) :]
    if last == 1:
        got_ref, refs = refs[0], refs[1:]
    w_in_any, w_out_any, in_a, in_b, out_a, out_b = refs[:6]
    (rows_ref, cot_ref, normed_ref, active_ref, hidden_ref, result_ref, w_in_ref, w_out_ref,
     load_sems, save_sems) = refs[-10:]
    outs = refs[-10 - (3 + (1 if first == 0 else 0) + (4 if last == 1 else 0)) : -10]
    saved, rest = outs[:3], outs[3:]
    if first == 0:
        send_ref, rest = rest[0], rest[1:]
    if last == 1:
        middle_ref, grad_ref, gain_grad_ref, results_any = rest
    half = rows_ref.shape[0] // len(turns)
    half_rows = in_a.shape[0]
    core, side, part = place_ref[0], place_ref[1], place_ref[2]
    near = pl.ds(pl.multiple_of(part * half_rows, half_rows), half_rows)
    away = pl.ds(pl.multiple_of((1 - part) * half_rows, half_rows), half_rows)

    def block(turn):
        mine = jnp.bitwise_xor(core, 1 - turn)
        return step - turn, pl.ds(pl.multiple_of(mine * half, half), half)

    def span(index):
        return pl.ds(index * half, half)

    row_loads = [
        pltpu.make_async_copy(rows_any.at[*block(turn)], rows_ref.at[span(i)], load_sems.at[i])
        for i, turn in enumerate(turns)
    ]
    cot_loads = [
        pltpu.make_async_copy(cot_any.at[*block(turn)], cot_ref.at[span(i)], load_sems.at[2 + i])
        for i, turn in enumerate(turns)
    ]
    in_loads = [
        pltpu.make_async_copy(w_in_any, w_in_ref.at[side], load_sems.at[4]),
        pltpu.make_async_copy(in_a, w_in_ref.at[1 - side, near], load_sems.at[5]),
        pltpu.make_async_copy(in_b, w_in_ref.at[1 - side, away], load_sems.at[6]),
    ]
    out_loads = [
        pltpu.make_async_copy(w_out_any, w_out_ref.at[side], load_sems.at[7]),
        pltpu.make_async_copy(out_a, w_out_ref.at[1 - side, near], load_sems.at[8]),
        pltpu.make_async_copy(out_b, w_out_ref.at[1 - side, away], load_sems.at[9]),
    ]
    for copy in row_loads[::-1] + in_loads + cot_loads[::-1] + out_loads:
        copy.start()
    saves, kept = [], {}

    def save(index, place, source, target):
        copy = pltpu.make_async_copy(
            source, target.at[*block(turns[index])], save_sems.at[2 * place + index]
        )
        copy.start()
        saves.append(copy)

    def prepare(index):
        row_loads[index].wait()
        pair_ref, far_ref = sums[index]
        middle = rows_ref[span(index), :].astype(wide) + (
            pair_ref[...].astype(wide) + far_ref[...].astype(wide)
        )
        scale = lax.rsqrt(jnp.mean(middle * middle, axis=-1, keepdims=True) + epsilon)
        normed_ref[span(index), :] = (middle * scale * gain_ref[...]).astype(low)
        kept[index] = [middle, scale, None, None]
        save(index, 0, normed_ref.at[span(index)], saved[0])

    def expand(index, quarter):
        rows_at = span(index)
        inner = nn(normed_ref[rows_at, :], w_in_ref[quarter])
        share = 0.5 + 0.5 * lax.erf(inner * root_half)
        active = (inner * share).astype(low)
        slope = share + inner * (jnp.exp(-0.5 * inner * inner) * inv_root_tau)
        if quarter == 0 and index == len(turns) - 1:
            for copy in cot_loads + out_loads:
                copy.wait()
        hidden = (nt(cot_ref[rows_at, :], w_out_ref[quarter]) * slope).astype(low)
        active_ref[quarter, rows_at, :] = active
        hidden_ref[quarter, rows_at, :] = hidden
        feed_share = nn(active, w_out_ref[quarter])
        back_share = nt(hidden, w_in_ref[quarter])
        if quarter == 0:
            kept[index][2:] = [feed_share, back_share]
        else:
            kept[index][2] = kept[index][2] + feed_share
            kept[index][3] = kept[index][3] + back_share
            save(index, 1, active_ref.at[side, rows_at], saved[1])
            save(index, 2, hidden_ref.at[side, rows_at], saved[2])

    def finish_own(index):
        middle, scale, feed, back = kept[index]
        result_ref[...] = (middle + (feed + got_ref[:half, :].astype(wide))).astype(low)
        copy = pltpu.make_async_copy(result_ref, results_any.at[step - 1], save_sems.at[6])
        copy.start()
        saves.append(copy)
        upstream = back + got_ref[half:, :].astype(wide)
        scaled = upstream * gain_ref[...]
        inner = jnp.mean(scaled * middle, axis=-1, keepdims=True)
        grad = cot_ref[span(index), :].astype(wide) + scale * scaled - middle * (
            scale * scale * scale * inner
        )
        middle_ref[...] = grad
        grad_ref[...] = grad.astype(low)
        gain_grad_ref[...] = jnp.sum(upstream * middle * scale, axis=0, keepdims=True)

    def send_far(index):
        send_ref[:half, :] = kept[index][2].astype(low)
        send_ref[half:, :] = kept[index][3].astype(low)

    order = list(range(len(turns)))[::-1]
    prepare(order[0])
    for copy in in_loads:
        copy.wait()
    expand(order[0], 0)
    if len(order) == 2:
        prepare(order[1])
    expand(order[0], 1)
    if len(order) == 2:
        expand(order[1], 0)
    if last == 1:
        finish_own(order[0])
    if len(order) == 2:
        expand(order[1], 1)
    if first == 0:
        send_far(order[-1])
    for copy in saves:
        copy.wait()


def feed_step(step, packs, place, rows, cot, gain, sums, far_sums, own_pair, own_far, got,
              w_in, w_out, in_halves, out_halves, kept, results):
    _, row_count, model = rows.shape
    hidden = w_in.shape[1]
    half = row_count // 2
    first, last = (0 if step < packs else 1), (1 if step > 0 else 0)
    steps = last - first + 1
    inside = pl.BlockSpec(memory_space=pltpu.VMEM)
    anywhere = pl.BlockSpec(memory_space=pl.ANY)
    args = [place, rows, cot, gain]
    in_specs = [pl.BlockSpec(memory_space=pltpu.SMEM), anywhere, anywhere, inside]
    flats = ([sums, far_sums] if first == 0 else []) + ([own_pair, own_far, got] if last == 1 else [])
    args += flats
    in_specs += [inside] * len(flats)
    args += [w_in, w_out, *in_halves, *out_halves]
    in_specs += [anywhere] * 6
    aliases = {}
    if kept is not None:
        in_specs += [anywhere] * 3
        aliases = {len(args) + i: i for i in range(3)}
        args += list(kept)
    out_specs = [anywhere] * 3
    out_shape = [
        in_hbm((packs, row_count, model), low),
        in_hbm((packs, row_count, hidden), low),
        in_hbm((packs, row_count, hidden), low),
    ]
    if first == 0:
        out_specs.append(inside)
        out_shape.append(jax.ShapeDtypeStruct((row_count, model), low))
    if last == 1:
        if results is not None:
            in_specs.append(anywhere)
            aliases[len(args)] = len(out_shape) + 3
            args.append(results)
        out_specs += [inside] * 3 + [anywhere]
        out_shape += [
            in_hbm((half, model), wide),
            (jax.ShapeDtypeStruct if step < packs else in_hbm)((half, model), low),
            jax.ShapeDtypeStruct((1, model), wide),
            in_hbm((packs, half, model), low),
        ]
    outs = kernel_call(
        functools.partial(feed_step_kernel, first, last, step), 4 + 4 * steps, vmem=26,
        in_specs=in_specs,
        out_specs=out_specs,
        scratch_shapes=[
            pltpu.VMEM((steps * half, model), low),
            pltpu.VMEM((steps * half, model), low),
            pltpu.VMEM((steps * half, model), low),
            pltpu.VMEM((2, steps * half, hidden), low),
            pltpu.VMEM((2, steps * half, hidden), low),
            pltpu.VMEM((half, model), low),
            pltpu.VMEM((2, model, hidden), low),
            pltpu.VMEM((2, hidden, model), low),
            pltpu.SemaphoreType.DMA((10,)),
            pltpu.SemaphoreType.DMA((7,)),
        ],
        out_shape=out_shape,
        input_output_aliases=aliases,
        name="feed_step",
    )(*args)
    sent = outs[3] if first == 0 else None
    own = list(outs[-4:]) if last == 1 else [None] * 4
    return outs[:3], sent, own


def attention_back_kernel(
    heads, prompt_len, has_back, has_prev, core_ref, *refs,
):
    refs = list(refs)
    if has_back:
        own_ref, far_ref, w_out_ref, probs_own_ref, probs_far_ref, joined_ref = refs[:6]
        refs = refs[6:]
    w_joined_ref = refs.pop(0)
    if has_prev:
        prev_ref, got_ref, values_ref, grad_ref, gain_ref, gain_in_ref, head_in_ref = refs[:7]
        refs = refs[7:]
        if not has_back:
            other_gain_ref, refs = refs[0], refs[1:]
    outs = refs[-((5 if has_back else 0) + (3 if has_prev else 0)):]
    if has_prev:
        pair_ref, gain_out_ref, head_out_ref = outs[:3]
        outs = outs[3:]
        pair = (nn(prev_ref[...], w_joined_ref[...]) + got_ref[...].astype(wide)).astype(low)
        pair_ref[...] = pair
        top = head_in_ref.shape[0]
        values, upstream = values_ref[0].astype(wide), pair.astype(wide)
        grad, share = norm_back(upstream, gain_ref[...], values)
        gain_sum = gain_in_ref[...] + share
        gain_out_ref[...] = gain_sum
        grad = grad[:top] + jnp.where(core_ref[1] == 0, grad_ref[...], 0.0)
        head_sum = head_in_ref[...] + jnp.where(core_ref[0] == 0, grad, 0.0)
        if has_back:
            head_out_ref[...] = head_sum
        else:
            groups, group_rows, _ = head_out_ref.shape
            rows = prompt_len // groups
            head_out_ref[...] = jnp.zeros(head_out_ref.shape, low)
            for group in range(groups):
                head_out_ref[group, :rows, :] = head_sum[group * rows : (group + 1) * rows].astype(low)
                head_out_ref[group, rows : rows + 1, :] = gain_sum.astype(low)
                head_out_ref[group, rows + 1 : rows + 2, :] = other_gain_ref[...].astype(low)
    if not has_back:
        return
    send_ref, own_grads_ref, grads_ref, scores_ref, whole_ref = outs
    rows = joined_ref.shape[1]
    half = rows // 2
    width = w_out_ref.shape[0]
    size = width // heads
    core = core_ref[0]
    starts = [pl.multiple_of(core * half, half), pl.multiple_of((1 - core) * half, half)]
    ups, asks, asked = [], [], [[], []]
    for side, ref in enumerate((own_ref, far_ref)):
        whole_ref[0, pl.ds(starts[side], half), :] = ref[...]
        ups.append(nt(ref[...], w_out_ref[...]).astype(low))
        asks.append(joined_ref[0, pl.ds(starts[side], half), :width])
    grad_keys, grad_values = [], []
    for head in range(heads):
        cols = slice(head * size, (head + 1) * size)
        keys = joined_ref[0, :, width + head * size : width + (head + 1) * size]
        values = joined_ref[0, :, 2 * width + head * size : 2 * width + (head + 1) * size]
        grad_key, grad_value = None, None
        for side, probs_ref in enumerate((probs_own_ref, probs_far_ref)):
            probs = probs_ref[0, head]
            upstream = ups[side][:, cols]
            grad_probs = nt(upstream, values)
            spread = probs.astype(wide)
            inner = jnp.sum(spread * grad_probs, axis=-1, keepdims=True)
            grad_scores = (spread * (grad_probs - inner)).astype(low)
            scores_ref[0, head, pl.ds(starts[side], half), :] = grad_scores
            value_share = tn(upstream, probs)
            key_share = tn(asks[side][:, cols], grad_scores)
            grad_value = value_share if grad_value is None else grad_value + value_share
            grad_key = key_share if grad_key is None else grad_key + key_share
            asked[side].append(nn(grad_scores, keys))
        grad_values.append(grad_value.T)
        grad_keys.append(grad_key.T)
    rest = jnp.concatenate(grad_keys + grad_values, axis=1).astype(low)
    grads_ref[0, :, width:] = rest
    for side in range(2):
        grads_ref[0, pl.ds(starts[side], half), :width] = jnp.concatenate(asked[side], axis=1).astype(low)
    own_grads_ref[...] = grads_ref[0, pl.ds(starts[0], half), :]
    send_ref[...] = nn(grads_ref[0, pl.ds(starts[1], half), :], w_joined_ref[...]).astype(low)


def attention_back_step(step, packs, heads, prompt_len, other_gain, core, own, far, w_out, probs_own, probs_far, joined, w_joined,
                        prev, got, values, grad, gain, gain_sum, head_sum, kept):
    _, rows, triple = joined.shape
    width, model = w_out.shape
    half = rows // 2
    has_back, has_prev = step < packs, step > 0
    fixed = lambda t, c: (0, 0)
    flat = pl.BlockSpec((half, model), fixed)
    anywhere = pl.BlockSpec(memory_space=pl.ANY)
    in_specs, args, out_specs, out_shape, aliases = [], [core], [], [], {}
    if has_back:
        in_specs += [
            flat,
            flat,
            pl.BlockSpec((width, model), fixed),
            pl.BlockSpec((1, heads, half, rows), lambda t, c: (0, 0, 0, 0)),
            pl.BlockSpec((1, heads, half, rows), lambda t, c: (0, 0, 0, 0)),
            pl.BlockSpec((1, rows, triple), lambda t, c: (step, 0, 0)),
        ]
        args += [own, far, w_out, probs_own, probs_far, joined]
    in_specs.append(pl.BlockSpec((triple, model), fixed))
    args.append(w_joined)
    if has_prev:
        line = pl.BlockSpec((1, model), fixed)
        head = pl.BlockSpec(head_sum.shape, fixed)
        in_specs += [
            pl.BlockSpec((half, triple), fixed),
            flat,
            pl.BlockSpec((1, half, model), lambda t, c: (step - 1, c[0], 0)),
            head,
            line,
            line,
            head,
        ]
        args += [prev, got, values, grad, gain, gain_sum, head_sum]
        if has_back:
            head_out = in_hbm(head_sum.shape, wide)
        else:
            in_specs.append(line)
            args.append(other_gain)
            groups = Small.groups
            small = (groups, -(-(prompt_len // groups + 3) // 16) * 16, model)
            head, head_out = pl.BlockSpec(small, lambda t, c: (0, 0, 0)), jax.ShapeDtypeStruct(small, low)
        out_specs += [flat, line, head]
        out_shape += [
            jax.ShapeDtypeStruct((half, model), low),
            jax.ShapeDtypeStruct((1, model), wide),
            head_out,
        ]
    if has_back:
        if kept is not None:
            in_specs += [anywhere] * 3
            aliases = {len(args) + i: len(out_shape) + 2 + i for i in range(3)}
            args += list(kept)
        out_specs += [
            flat,
            pl.BlockSpec((half, triple), fixed),
            pl.BlockSpec((1, rows, triple), lambda t, c: (step, 0, 0)),
            pl.BlockSpec((1, heads, rows, rows), lambda t, c: (step, 0, 0, 0)),
            pl.BlockSpec((1, rows, model), lambda t, c: (step, 0, 0)),
        ]
        out_shape += [
            jax.ShapeDtypeStruct((half, model), low),
            in_hbm((half, triple), low),
            in_hbm((packs, rows, triple), low),
            in_hbm((packs, heads, rows, rows), low),
            in_hbm((packs, rows, model), low),
        ]
    outs = list(
        kernel_call(
            functools.partial(attention_back_kernel, heads, prompt_len, has_back, has_prev), 6,
            least=1000 if step == packs - 1 else 400000,
            grid_spec=pltpu.PrefetchScalarGridSpec(
                num_scalar_prefetch=1, grid=(1,), in_specs=in_specs, out_specs=out_specs
            ),
            out_shape=out_shape,
            input_output_aliases=aliases,
                name="attention_back_step",
        )(*args)
    )
    done, outs = (outs[:3], outs[3:]) if has_prev else ((None,) * 3, outs)
    send, own_grads, *kept = outs if has_back else (None, None)
    return done, send, own_grads, kept


def finish_kernel(packs, core_ref, rows_any, gain_ref, *refs):
    out_ref, rows_ref, sems = refs[-3:]
    half = rows_ref.shape[1]
    start = pl.multiple_of(core_ref[0] * half, half)
    copies = [
        pltpu.make_async_copy(rows_any.at[pack, pl.ds(start, half)], rows_ref.at[i], sems.at[i])
        for i, pack in enumerate(packs)
    ]
    for copy in copies:
        copy.start()
    for i, copy in enumerate(copies):
        copy.wait()
        pair_ref, far_ref, grad_ref = refs[3 * i : 3 * i + 3]
        upstream = pair_ref[...].astype(wide) + far_ref[...].astype(wide)
        grad, _ = norm_back(upstream, gain_ref[...], rows_ref[i].astype(wide))
        out_ref[i] = (grad_ref[...] + grad).astype(low)


def finish(packs, core, rows, gain, parts):
    half, model = parts[0][0].shape
    inside = pl.BlockSpec(memory_space=pltpu.VMEM)
    return kernel_call(
        functools.partial(finish_kernel, packs), 1.5 * len(packs), vmem=24,
        in_specs=[pl.BlockSpec(memory_space=pltpu.SMEM), pl.BlockSpec(memory_space=pl.ANY), inside]
        + [inside] * (3 * len(packs)),
        out_specs=inside,
        out_shape=jax.ShapeDtypeStruct((len(packs), half, model), low),
        scratch_shapes=[
            pltpu.VMEM((len(packs), half, model), low),
            pltpu.SemaphoreType.DMA((len(packs),)),
        ],
        name="finish",
    )(core, rows, gain, *[v for part in parts for v in part])


def place_kernel(core_ref, own_ref, far_ref, out_ref, sems):
    packs, half, _ = own_ref.shape
    copies = []
    for pack in range(packs):
        for side, ref in enumerate((own_ref, far_ref)):
            start = pl.multiple_of(jnp.bitwise_xor(core_ref[0], side) * half, half)
            copies.append(
                pltpu.make_async_copy(
                    ref.at[pack], out_ref.at[pack, pl.ds(start, half)], sems.at[2 * pack + side]
                )
            )
    for copy in copies:
        copy.start()
    for copy in copies:
        copy.wait()


def place_halves(core, own, far):
    packs, half, model = own.shape
    inside = pl.BlockSpec(memory_space=pltpu.VMEM)
    return kernel_call(
        place_kernel, 2.5, vmem=24, least=1000,
        in_specs=[pl.BlockSpec(memory_space=pltpu.SMEM), inside, inside],
        out_specs=pl.BlockSpec(memory_space=pl.ANY),
        out_shape=in_hbm((packs, 2 * half, model), low),
        scratch_shapes=[pltpu.SemaphoreType.DMA((2 * packs,))],
        name="place_halves",
    )(core, own, far)


def weave_kernel(core_ref, *refs):
    out_ref, rows_ref, woven_ref = refs[-3:]
    half = rows_ref.shape[0] // 2
    text = out_ref.shape[0]
    pack = 0
    for own_ref, far_ref in zip(refs[:-3:2], refs[1:-3:2]):
        for i in range(own_ref.shape[0]):
            for side, ref in enumerate((own_ref, far_ref)):
                start = pl.multiple_of(jnp.bitwise_xor(core_ref[0], side) * half, half)
                rows_ref[pl.ds(start, half), :] = ref[i].astype(wide)
            woven_ref[:, pack, :] = rows_ref[2 * half - text :, :]
            pack += 1
    out_ref[...] = woven_ref[...].astype(low)


def weave_halves(core, pairs, text):
    packs = sum(own.shape[0] for own, _ in pairs)
    _, half, model = pairs[0][0].shape
    inside = pl.BlockSpec(memory_space=pltpu.VMEM)
    return kernel_call(
        weave_kernel, 4, vmem=32, least=1000,
        in_specs=[pl.BlockSpec(memory_space=pltpu.SMEM)] + [inside] * (2 * len(pairs)),
        out_specs=inside,
        out_shape=jax.ShapeDtypeStruct((text, packs, model), low),
        scratch_shapes=[pltpu.VMEM((2 * half, model), wide), pltpu.VMEM((text, packs, model), wide)],
        name="weave_halves",
    )(core, *[v for pair in pairs for v in pair])


def weight_kernel(pairs, split, where_ref, *refs):
    if split:
        keep_ref, send_ref, total_ref = refs[-3:]
    else:
        whole_ref, total_ref = refs[-2:]
    column = 0
    for i in range(pairs):
        right = refs[2 * i + 1][...]
        total_ref[:, column : column + right.shape[1]] = tn(refs[2 * i][...], right)
        column += right.shape[1]
    if not split:
        whole_ref[...] = total_ref[...].astype(low)
        return
    count, block, _ = keep_ref.shape
    side = jnp.bitwise_and(where_ref[0], 1)
    for i in range(count):
        for ref, chosen in ((keep_ref, side), (send_ref, 1 - side)):
            start = pl.multiple_of((2 * i + chosen) * block, 8)
            ref[i] = total_ref[pl.ds(start, block), :].astype(low)


def weight_shares(where, count, pairs, split):
    rows, model = pairs[0][0].shape
    widths = [right.shape[1] for _, right in pairs]
    turns, width = 2, sum(widths)
    block = model // count
    in_specs = []
    for n in widths:
        in_specs += [
            pl.BlockSpec((rows, model // turns), lambda t, w: (0, t)),
            pl.BlockSpec((rows, n), lambda t, w: (0, 0)),
        ]
    if split:
        out_specs = [pl.BlockSpec((count // 2 // turns, block, width), lambda t, w: (t, 0, 0))] * 2
        out_shape = [jax.ShapeDtypeStruct((count // 2, block, width), low)] * 2
    else:
        out_specs = pl.BlockSpec((model // turns, width), lambda t, w: (t, 0))
        out_shape = in_hbm((model, width), low)
    return kernel_call(
        functools.partial(weight_kernel, len(pairs), split), 6, vmem=26,
        grid_spec=pltpu.PrefetchScalarGridSpec(
            num_scalar_prefetch=1,
            grid=(turns,),
            in_specs=in_specs,
            out_specs=out_specs,
            scratch_shapes=[pltpu.VMEM((model // turns, width), wide)],
        ),
        out_shape=out_shape,
        name="weight_shares",
    )(where, *[value for pair in pairs for value in pair])


def fold_kernel(count, where_ref, *refs):
    ins, outs = refs[:count], refs[count:]
    group = outs[0].shape[0]
    for flip, out_ref in enumerate(outs):
        for piece in range(group):
            spot = jnp.bitwise_xor(where_ref[0], flip)
            spot = spot * group + piece if len(outs) == 4 else piece * 2 + spot
            total = ins[0][spot].astype(wide)
            for ref in ins[1:]:
                total = total + ref[spot].astype(wide)
            out_ref[piece] = total.astype(out_ref.dtype)


def fold(where, parts, cuts):
    whole, block, width = parts[0].shape
    shape = (whole // cuts, block, width)
    inside = pl.BlockSpec(memory_space=pltpu.VMEM)
    return kernel_call(
        functools.partial(fold_kernel, len(parts)), 1.5, vmem=24,
        in_specs=[pl.BlockSpec(memory_space=pltpu.SMEM)] + [inside] * len(parts),
        out_specs=[inside] * cuts,
        out_shape=[jax.ShapeDtypeStruct(shape, low)] * cuts,
        name="fold",
    )(where, *parts)


def unfold_kernel(count, cuts, *refs):
    ins, outs = refs[:count], refs[count:]
    total = ins[0][0].astype(wide)
    for ref in ins[1:]:
        total = total + ref[0].astype(wide)
    for (start, width, turned), out_ref in zip(cuts, outs):
        piece = total[:, start : start + width]
        out_ref[...] = piece.T if turned else piece


def unfold(parts, cuts):
    block = parts[0].shape[1]
    inside = pl.BlockSpec(memory_space=pltpu.VMEM)
    return kernel_call(
        functools.partial(unfold_kernel, len(parts), cuts), 1.5,
        in_specs=[inside] * len(parts),
        out_specs=[inside] * len(cuts),
        out_shape=[
            jax.ShapeDtypeStruct((width, block) if turned else (block, width), wide)
            for _, width, turned in cuts
        ],
        name="unfold",
    )(*parts)


def small_fold_kernel(has_rel, side_ref, mine_ref, got_ref, *refs):
    keep_ref, send_ref, total_ref = refs[-3:]
    groups, rows, _ = mine_ref.shape
    half = groups // 2
    total_ref[...] = mine_ref[...].astype(wide) + got_ref[...].astype(wide)
    if has_rel:
        rel_ref, spot = refs[0], refs[1]
        for group in range(groups):
            total_ref[group, spot[0], :] = rel_ref[0, :]
    keep_ref[...] = total_ref[pl.ds(side_ref[0] * half, half)].astype(low)
    send_ref[...] = total_ref[pl.ds((1 - side_ref[0]) * half, half)].astype(low)


def small_fold(side, mine, got, rel=None, spot=None):
    groups, rows, model = mine.shape
    inside, scalar = pl.BlockSpec(memory_space=pltpu.VMEM), pl.BlockSpec(memory_space=pltpu.SMEM)
    more = [] if rel is None else [rel, jnp.full((1,), spot, jnp.int32)]
    return kernel_call(
        functools.partial(small_fold_kernel, rel is not None), 1,
        in_specs=[scalar, inside, inside] + ([inside, scalar] if more else []),
        out_specs=[inside] * 2,
        out_shape=[jax.ShapeDtypeStruct((groups // 2, rows, model), low)] * 2,
        scratch_shapes=[pltpu.VMEM((groups, rows, model), wide)],
        name="small_fold",
    )(side, mine, got, *more)


def tie(*values):
    return lax.optimization_barrier(values)


def stages_of(count):
    bits = bits_of(count)
    rest = bits[1:][::-1]
    return [bits[:1]] + [rest[i : i + 2] for i in range(0, len(rest), 2)]


class Scatter:
    def __init__(self, keep, send, cuts):
        self.bits, self.cuts = bits_of(lax.axis_size("dp"))[1:], cuts
        self.parts = [keep, swap(send, "dp", 1)]

    def step(self):
        if self.cuts == 4:
            bit, self.bits = self.bits[-2], self.bits[:-2]
        else:
            bit, self.bits = self.bits[0], self.bits[1:]
        where = ((lax.axis_index("dp") // bit) % self.cuts).astype(jnp.int32).reshape(1)
        own, *sends = fold(where, self.parts, self.cuts)
        self.parts = [own] + [swap(v, "dp", bit * (flip + 1)) for flip, v in enumerate(sends)]

    def end(self, pieces):
        while self.bits:
            self.step()
        return unfold(self.parts, pieces)


def look_up(prompt_ids, table, prompt_delta):
    prompt_len = prompt_ids.shape[0]
    table_rows, model = table.shape
    groups = 2
    part = -(-prompt_len // (16 * groups)) * 16
    dp_index, mp_index = lax.axis_index("dp"), lax.axis_index("mp") % groups
    padded = jnp.pad(prompt_ids, (0, part * groups - prompt_len), constant_values=-1)
    ids = lax.dynamic_slice_in_dim(padded, mp_index * part, part)
    size, block = prompt_delta.shape[0], part * model
    line = jnp.pad(prompt_delta, (block, block))
    start = jnp.clip(block + mp_index * block - dp_index * size, 0, block + size)
    placed = lax.dynamic_slice_in_dim(line, start, block).reshape(part, model)
    local = jnp.where(ids < 0, -1, ids - dp_index * table_rows)
    if table_rows % 16 == 0:
        return look_up_rows(local, table, placed)
    selector = (local[:, None] == jnp.arange(table_rows, dtype=jnp.int32)[None, :]).astype(low)
    return (jnp.dot(selector, table, preferred_element_type=wide) + placed).astype(low)


def own_half(weight):
    part = lax.axis_index("dp") % 2
    halves = weight.reshape(2, weight.shape[0] // 2, weight.shape[1])
    return lax.dynamic_index_in_dim(halves, part, 0, keepdims=False)


class Small:
    groups = 4

    def __init__(self, total, prompt_len):
        self.total, self.share = total, prompt_len // self.groups
        self.mp_bits = bits_of(lax.axis_size("mp"))
        self.dp_bits = bits_of(lax.axis_size("dp"))[::-1]
        self.hops = 0
        self.hop_mp()

    def hop_mp(self):
        bit, self.mp_bits = self.mp_bits[0], self.mp_bits[1:]
        self.keep, self.got = self.total, swap(self.total, "mp", bit)

    def land(self):
        self.total = (self.keep.astype(wide) + self.got.astype(wide)).astype(low)

    def hop_dp(self, rel=None):
        bit, self.dp_bits = self.dp_bits[0], self.dp_bits[1:]
        if self.hops < 2:
            side = ((lax.axis_index("dp") // bit) % 2).astype(jnp.int32).reshape(1)
            if rel is not None:
                self.rel = rel
                rel = jnp.pad(rel.reshape(1, -1), ((0, 0), (0, self.keep.shape[2] - rel.size)))
            self.keep, send = small_fold(side, self.keep, self.got, rel, self.share + 2)
        else:
            self.land()
            self.keep = send = self.total
        self.hops += 1
        self.got = swap(send, "dp", bit)

    def results(self):
        while self.dp_bits:
            self.hop_dp()
        total = self.keep[0].astype(wide) + self.got[0].astype(wide)
        dp_count, dp_index = lax.axis_size("dp"), lax.axis_index("dp")
        share, model = self.share, total.shape[1]
        inside = dp_count // self.groups
        size = share * model // inside
        prompt_grad = lax.dynamic_slice_in_dim(total[:share].reshape(-1), (dp_index % inside) * size, size)
        width = model // dp_count
        gains = lax.dynamic_slice_in_dim(total[share : share + 2], dp_index * width, width, axis=1)
        piece = self.rel.size // dp_count
        rel_out = lax.dynamic_slice_in_dim(total[share + 2], dp_index * piece, piece)
        return prompt_grad, gains[0], gains[1], rel_out.reshape(-1, self.rel.shape[1])


def body(
    tokens, cotangent, segment_ids, prompt_ids, rel_buckets, table, prompt_delta, norm1_gain,
    w_query, w_key, w_value, w_output, rel_bias, norm2_gain, w_inner, w_outer,
):
    prompt_len = prompt_ids.shape[0]
    packs, rows, model = cotangent.shape
    bucket_count, heads = rel_bias.shape
    width = w_query.shape[1]
    groups = lax.axis_size("dp")
    mp_bits = bits_of(lax.axis_size("mp"))
    mp_index = lax.axis_index("mp").astype(jnp.int32)
    place = jnp.stack([mp_index % 2, (mp_index // 2) % 2, (lax.axis_index("dp") % 2).astype(jnp.int32)])
    gain1, gain2 = norm1_gain[None, :], norm2_gain[None, :]
    w_q, w_k, w_v = w_query.T, w_key.T, w_value.T

    in_near = swap(own_half(w_inner), "mp", 2)
    total = look_up(prompt_ids, table, prompt_delta)

    w_joined = jnp.concatenate([w_q, w_k, w_v], axis=0)
    bucket_hot = (
        rel_buckets[:, None] == jnp.arange(bucket_count, dtype=jnp.int32)[None, :]
    ).astype(wide)
    bucket_hot = jnp.pad(bucket_hot, ((0, 1), (0, 0)))
    turned = jnp.roll(bucket_hot, -(rows - 1), axis=0)
    bias_line = jnp.dot(turned, rel_bias, precision=highest).T
    marks = jnp.pad(segment_ids, ((0, 0), (prompt_len, 0)), constant_values=-1)
    seg_rows, seg_cols = marks.T, marks

    texts, half_packs = [], packs // 2
    for hop, bit in enumerate(bits_of(groups)):
        got = swap(total, "dp", bit)
        if hop == 0:
            bias = bias_grid_of(bias_line[:, None, :])
            got, bias, seg_rows, seg_cols = tie(got, bias, seg_rows, seg_cols)
        if hop == 1:
            texts = text_projections(0, half_packs, rows, tokens, gain1, w_joined, texts)
            got, *texts = tie(got, *texts)
        if hop == 2:
            texts = text_projections(half_packs, packs - half_packs, rows, tokens, gain1, w_joined, texts)
            got, *texts = tie(got, *texts)
            got, in_near = tie(got, in_near)
            in_away = swap(in_near, "dp", 1)
            out_near = swap(own_half(w_outer), "mp", 2)
        total = (total.astype(wide) + got.astype(wide)).astype(low)
    whole_rows, normed1, joined = texts
    pieces = jnp.stack([total, swap(total, "mp", 1)])
    whole_rows, normed1, joined = add_prompt(
        place[:1], pieces, gain1, w_joined, whole_rows, normed1, joined
    )

    pairs, fars, pairs_far, fars_far, probs_far, probs_own, mixed, got = [], [], [], [], [], [], None, None

    def attend(step):
        nonlocal mixed, got, place, in_away, out_near, out_away
        send, pair, probs_send, probs_pair, mixed = attention_step(
            step, packs, prompt_len, place, joined, bias, seg_rows, seg_cols, w_output, got, mixed
        )
        if step == 0:
            place, out_near, send = tie(place, out_near, send)
            out_away = swap(out_near, "dp", 1)
        else:
            place, pair = tie(place, pair)
        if step == 1:
            place, in_away = tie(place, in_away)
        if send is not None:
            probs_far.append(probs_send)
            got = swap(send, "mp", 1)
        if pair is not None:
            probs_own.append(probs_pair)
            pairs.append(pair)
            fars.append(swap(pair, "mp", 2))
            pairs_far.append(swap(pair, "mp", 1))
            fars_far.append(swap(fars[-1], "mp", 1))

    out_away = None

    def arrive(pack):
        nonlocal place
        place, fars[pack], pairs_far[pack], fars_far[pack] = tie(
            place, fars[pack], pairs_far[pack], fars_far[pack]
        )

    kept, sent, results, grads_wide, grads_low = None, None, None, [], []
    gain2_sum, none = 0.0, [None]
    back_kept, prev, got = None, None, None
    gain1_sum, head_sum = jnp.zeros((1, model), wide), jnp.zeros((128, model), wide)
    text_rows, pairs_back = [], []

    def feed(step):
        nonlocal kept, sent, results, gain2_sum, place
        kept, new_sent, done = feed_step(
            step, packs, place, whole_rows, cotangent, gain2,
            (pairs_far + none)[step], (fars_far + none)[step],
            (none + pairs)[step], (none + fars)[step], sent,
            w_inner, w_outer, (in_near, in_away), (out_near, out_away), kept, results,
        )
        if step < packs:
            place, new_sent = tie(place, new_sent)
            sent = swap(new_sent, "mp", 1)
        else:
            place, done[1] = tie(place, done[1])
        if step > 0:
            grads_wide.append(done[0])
            grads_low.append((done[1], swap(done[1], "mp", 1)))
            gain2_sum, results = gain2_sum + done[2], done[3]

    def back(step):
        nonlocal back_kept, prev, got, gain1_sum, head_sum, place
        live = step < packs
        done, send, own_grads, back_new = attention_back_step(
            step, packs, heads, prompt_len, gain2_sum, place, *(grads_low[step] if live else none * 2), w_output,
            probs_own[step] if live else None, probs_far[step] if live else None, joined, w_joined,
            prev, got, whole_rows, grads_wide[step - 1] if step else None, gain1, gain1_sum, head_sum,
            back_kept,
        )
        if live:
            place, send = tie(place, send)
            back_kept, prev, got = back_new, own_grads, swap(send, "mp", 1)
        if step > 0:
            pair, gain1_sum, head_sum = done
            pairs_back.append([pair, swap(pair, "mp", 2)])

    def end(*ended):
        nonlocal place
        rows_low = finish(ended, place, whole_rows, gain1, [(*pairs_back[p], grads_wide[p]) for p in ended])
        place, rows_low = tie(place, rows_low)
        text_rows.append((rows_low, swap(rows_low, "mp", 1)))

    def flat(value):
        return value.reshape(packs * rows, -1)

    for step in range(packs):
        attend(step)
    place, out_away = tie(place, out_away)
    arrive(0)
    feed(0)
    attend(packs)
    arrive(1)
    feed(1)
    for step in range(2, packs):
        arrive(step)
        feed(step)
        back(step - 2)
    feed(packs)
    normed2, active, hidden = kept
    where = lax.axis_index("dp").astype(jnp.int32).reshape(1)
    where, place = tie(where, place)
    feed_shares = weight_shares(
        where, groups, [(flat(normed2), flat(hidden)), (flat(cotangent), flat(active))], True
    )
    place, *feed_shares = tie(place, *feed_shares)
    feed_sum = Scatter(*feed_shares, 2)
    back(packs - 2)
    far_results = swap(results, "mp", 1)
    place, far_results, *pairs_back[0] = tie(place, far_results, *pairs_back[0])
    back(packs - 1)
    place, *pairs_back[1] = tie(place, *pairs_back[1])
    place, *feed_sum.parts = tie(place, *feed_sum.parts)
    feed_sum.step()
    grad_joined, scores, grad_rows = back_kept
    where, place = tie(where, place)
    tail_shares = weight_shares(
        where, groups, [(flat(normed1), flat(grad_joined)), (flat(grad_rows), flat(mixed))], True
    )
    place, *tail_shares = tie(place, *tail_shares)
    place, *feed_sum.parts = tie(place, *feed_sum.parts)
    feed_sum.step()
    tail = Scatter(*tail_shares, 4)
    side_one = (mp_index // 2) % 2 == 1
    gain2_sum = jnp.where(side_one, 0.0, gain2_sum)
    back(packs)
    place, head_sum = tie(place, head_sum)
    small = Small(head_sum, prompt_len)
    place, scores = tie(place, scores)
    line = diagonal_sums(scores)[:, 0, :]
    rel_share = jnp.einsum("ht,tb->bh", line, turned, precision=highest)
    small.land()
    small.hop_mp()
    place, rel_share = tie(place, rel_share)
    end(*range(packs - 1))
    out = place_halves(place, results, far_results)
    place, out, *tail.parts = tie(place, out, *tail.parts)
    tail.step()
    place, tail.parts[0], *feed_sum.parts = tie(place, tail.parts[0], *feed_sum.parts)
    hidden_width = w_inner.shape[1]
    inner_grad, outer_grad = feed_sum.end(((0, hidden_width, False), (hidden_width, hidden_width, False)))
    place, small.got, inner_grad = tie(place, small.got, inner_grad)
    small.hop_dp(rel_share)
    end(packs - 1)
    place, small.got = tie(place, small.got)
    small.hop_dp()
    text_rows[-1] = tie(*text_rows[-1])
    place, *tail.parts = tie(place, *tail.parts)
    grad_tokens = weave_halves(place, text_rows, rows - prompt_len)
    grad_tokens = jnp.transpose(grad_tokens, (1, 0, 2))
    query_grad, key_grad, value_grad, output_grad = tail.end(
        tuple((i * width, width, i == 3) for i in range(4))
    )
    prompt_grad, gain1_grad, gain2_grad, rel_grad = small.results()
    return (
        out, grad_tokens, prompt_grad, gain1_grad, query_grad, key_grad, value_grad, output_grad,
        rel_grad, gain2_grad, inner_grad, outer_grad.T,
    )


def solution(mesh):
    in_specs = (
        P("dp", None, None),
        P("dp", None, None),
        P("dp", None),
        P(),
        P(),
        P("dp", None),
        P("dp"),
        P(),
        P(None, "mp"),
        P(None, "mp"),
        P(None, "mp"),
        P("mp", None),
        P(None, "mp"),
        P(),
        P(None, "mp"),
        P("mp", None),
    )
    out_specs = (
        P("dp", None, None),
        P("dp", None, None),
        P("dp"),
        P("dp"),
        P("dp", "mp"),
        P("dp", "mp"),
        P("dp", "mp"),
        P("mp", "dp"),
        P("dp", "mp"),
        P("dp"),
        P("dp", "mp"),
        P("mp", "dp"),
    )
    return jax.shard_map(body, mesh=mesh, in_specs=in_specs, out_specs=out_specs, check_vma=False)
```

profile of v0, /device:TPU:0, one launch (start us, length us, event | category | flops | bytes accessed | tf_op | source)
XLA Modules:
  0.0 269.6 jit_solution(2874984844648262277)
XLA Ops:
  2.4 6.5 %look_up.1 = bf16[64,768]{1,0:T(8,128)(2,1)S(1)} custom-call(s32[64]{0:T(128)S(1)} %compare_select_fusion.ids_ref, bf16[4016,768]{1,0:T(8,128)(2,1)} %table_any.1, f32[64,768]{1,0:T(8,128)S(1)} %reshape.99.placed_ref), custom_call_target="tpu_custom_call" | custom-call | bytes 9000000 | tf_op jit(solution)/shard_map/look_up/pallas_call | solution.py:44
  20.1 4.3 %text_projections.2 = (bf16[4,512,768]{2,1,0:T(8,128)(2,1)}, bf16[4,512,768]{2,1,0:T(8,128)(2,1)}, bf16[4,512,576]{2,1,0:T(8,128)(2,1)}) custom-call(bf16[4,412,768]{2,1,0:T(8,128)(2,1)} %copy.78.tokens_ref, f32[1,768]{1,0:T(1,128)S(1)} %broadcast_in_dim.25.gain_ref.refs_11_.refs_5_, bf16[576,768]{1,0:T(8,128)(2,1)} %pad_maximum_fusion.weight_ref.refs_6_.refs_0_), custom_call_target="tpu_custom_call" | custom-call | bytes 8640000 | tf_op jit(solution)/shard_map/text_projections/pallas_call | solution.py:44
  26.9 4.8 %text_projections.3 = (bf16[4,512,768]{2,1,0:T(8,128)(2,1)}, bf16[4,512,768]{2,1,0:T(8,128)(2,1)}, bf16[4,512,576]{2,1,0:T(8,128)(2,1)}) custom-call(bf16[4,412,768]{2,1,0:T(8,128)(2,1)} %copy.78.tokens_ref, f32[1,768]{1,0:T(1,128)S(1)} %broadcast_in_dim.25.gain_ref.refs_11_.refs_5_, ...), custom_call_target="tpu_custom_call", output_to_operand_aliasing={{0}: (3, {}), {1}: (4, {}), {2}: (5, {})} | custom-call | bytes 8640000 | tf_op jit(solution)/shard_map/text_projections/pallas_call | solution.py:44
  42.7 5.6 %attention_step.6 = (bf16[256,768]{1,0:T(8,128)(2,1)S(1)}, bf16[256,768]{1,0:T(8,128)(2,1)S(1)}, bf16[1,3,256,512]{3,2,1,0:T(8,128)(2,1)}, bf16[1,3,256,512]{3,2,1,0:T(8,128)(2,1)}, bf16[4,512,192]{2,1,0:T(8,128)(2,1)}) custom-call(s32[3]{0:T(128)S(1)} %pad_add_fusion.core_ref.place_ref, ...), custom_call_target="tpu_custom_call", output_to_operand_aliasing={{4}: (7, {})} | custom-call | bytes 18000000 | tf_op jit(solution)/shard_map/attention_step/pallas_call | solution.py:44
  50.5 7.1 %collective-permute-done.7.refs_5_.refs_8_.refs_6_ = bf16[384,768]{1,0:T(8,128)(2,1)S(1)} collective-permute-done((bf16[384,768]{1,0:T(8,128)(2,1)}, bf16[384,768]{1,0:T(8,128)(2,1)S(1)}, u32[]{:S(2)}, u32[]{:S(2)}) %collective-permute-start.7) | collective-permute-done | bytes 589856 | tf_op jit(solution)/shard_map/ppermute | solution.py:56
  57.5 5.6 %attention_step.7 = (bf16[256,768]{1,0:T(8,128)(2,1)S(1)}, bf16[256,768]{1,0:T(8,128)(2,1)S(1)}, bf16[1,3,256,512]{3,2,1,0:T(8,128)(2,1)}, bf16[1,3,256,512]{3,2,1,0:T(8,128)(2,1)}, bf16[4,512,192]{2,1,0:T(8,128)(2,1)}) custom-call(s32[3]{0:T(128)S(1)} %pad_add_fusion.core_ref.place_ref, ...), custom_call_target="tpu_custom_call", output_to_operand_aliasing={{4}: (7, {})} | custom-call | bytes 18000000 | tf_op jit(solution)/shard_map/attention_step/pallas_call | solution.py:44
  65.3 5.6 %attention_step.8 = (bf16[256,768]{1,0:T(8,128)(2,1)S(1)}, bf16[256,768]{1,0:T(8,128)(2,1)S(1)}, bf16[1,3,256,512]{3,2,1,0:T(8,128)(2,1)}, bf16[1,3,256,512]{3,2,1,0:T(8,128)(2,1)}, bf16[4,512,192]{2,1,0:T(8,128)(2,1)}) custom-call(s32[3]{0:T(128)S(1)} %pad_add_fusion.core_ref.place_ref, ...), custom_call_target="tpu_custom_call", output_to_operand_aliasing={{4}: (7, {})} | custom-call | bytes 18000000 | tf_op jit(solution)/shard_map/attention_step/pallas_call | solution.py:44
  71.0 6.3 %feed_step.5 = (bf16[4,512,768]{2,1,0:T(8,128)(2,1)}, bf16[4,512,768]{2,1,0:T(8,128)(2,1)}, bf16[4,512,768]{2,1,0:T(8,128)(2,1)}, bf16[512,768]{1,0:T(8,128)(2,1)S(1)}) custom-call(s32[3]{0:T(128)S(1)} %pad_add_fusion.core_ref.place_ref, bf16[4,512,768]{2,1,0:T(8,128)(2,1)} %get-tuple-element.286.rows_any.refs_9_.refs_3_, bf16[4,512,768]{2,1,0:T(8,128)(2,1)} %cot_any.9, ...), custom_call_target="tpu_custom_call" | custom-call | bytes 28800000 | tf_op jit(solution)/shard_map/feed_step/pallas_call | solution.py:44
  84.1 10.0 %feed_step.6 = (bf16[4,512,768]{2,1,0:T(8,128)(2,1)}, bf16[4,512,768]{2,1,0:T(8,128)(2,1)}, bf16[4,512,768]{2,1,0:T(8,128)(2,1)}, bf16[512,768]{1,0:T(8,128)(2,1...) custom-call(s32[3]{0:T(128)S(1)} %pad_add_fusion.core_ref.place_ref,, ...), custom_call_target="tpu_custom_call", output_to_operand_aliasing={{0}: (15, {}), {1}: (16, {}), {2}: (17, {})} | custom-call | bytes 43200000 | tf_op jit(solution)/shard_map/feed_step/pallas_call | solution.py:44
  97.7 10.0 %feed_step.7 = (bf16[4,512,768]{2,1,0:T(8,128)(2,1)}, bf16[4,512,768]{2,1,0:T(8,128)(2,1)}, bf16[4,512,768]{2,1,0:T(8,128)(2,1)}, bf16[512,768]{1,0:T(8,128)(2,1...) custom-call(s32[3]{0:T(128)S(1)} %pad_add_fusion.core_ref.place_ref,, ...), custom_call_target="tpu_custom_call", output_to_operand_aliasing={{0}: (15, {}), {1}: (16, {}), {2}: (17, {}), {7}: (18, {})} | custom-call | bytes 43200000 | tf_op jit(solution)/shard_map/feed_step/pallas_call | solution.py:44
  110.6 7.6 %attention_back_step.5 = (bf16[256,768]{1,0:T(8,128)(2,1)S(1)}, bf16[256,576]{1,0:T(8,128)(2,1)}, bf16[4,512,576]{2,1,0:T(8,128)(2,1)}, bf16[4,3,512,512]{3,2,1,0:T(8,128)(2,1)}, bf16[4,512,768]{2,1,0:T(8,128)(2,1)}) custom-call(s32[3]{0:T(128)S(1)} %pad_add_fusion.core_ref.place_ref, bf16[256,768]{1,0:T(8,128)(2,1)S(1)} %get-tuple-element.320.refs_0_, ...), custom_call_target="tpu_custom_call" | custom-call | bytes 21600000 | tf_op jit(solution)/shard_map/attention_back_step/pallas_call | solution.py:44
  118.2 10.0 %feed_step.8 = (bf16[4,512,768]{2,1,0:T(8,128)(2,1)}, bf16[4,512,768]{2,1,0:T(8,128)(2,1)}, bf16[4,512,768]{2,1,0:T(8,128)(2,1)}, bf16[512,768]{1,0:T(8,128)(2,1...) custom-call(s32[3]{0:T(128)S(1)} %pad_add_fusion.core_ref.place_ref,, ...), custom_call_target="tpu_custom_call", output_to_operand_aliasing={{0}: (15, {}), {1}: (16, {}), {2}: (17, {}), {7}: (18, {})} | custom-call | bytes 43200000 | tf_op jit(solution)/shard_map/feed_step/pallas_call | solution.py:44
  131.8 8.3 %attention_back_step.6 = (bf16[256,768]{1,0:T(8,128)(2,1)S(1)}, f32[1,768]{1,0:T(1,128)S(1)}, f32[128,768]{1,0:T(8,128)}, bf16[256,768]{1,0:T(8,128)(2,1)S(1)}, ...) custom-call(s32[3]{0:T(128)S(1)} %pad_add_fusion.core_ref.place_ref,, ...), custom_call_target="tpu_custom_call", output_to_operand_aliasing={{5}: (15, {}), {6}: (16, {}), {7}: (17, {})} | custom-call | bytes 21600000 | tf_op jit(solution)/shard_map/attention_back_step/pallas_call | solution.py:44
  140.1 7.7 %feed_step.9 = (bf16[4,512,768]{2,1,0:T(8,128)(2,1)}, bf16[4,512,768]{2,1,0:T(8,128)(2,1)}, bf16[4,512,768]{2,1,0:T(8,128)(2,1)}, f32[256,768]{1,0:T(8,128)}, bf...) custom-call(s32[3]{0:T(128)S(1)} %pad_add_fusion.core_ref.place_ref,, ...), custom_call_target="tpu_custom_call", output_to_operand_aliasing={{0}: (13, {}), {1}: (14, {}), {2}: (15, {}), {6}: (16, {})} | custom-call | bytes 28800000 | tf_op jit(solution)/shard_map/feed_step/pallas_call | solution.py:44
  148.0 10.8 %weight_shares.2 = (bf16[4,96,1536]{2,1,0:T(8,128)(2,1)S(1)}, bf16[4,96,1536]{2,1,0:T(8,128)(2,1)}) custom-call(s32[1]{0:T(128)} %bitcast.where_ref, bf16[2048,768]{1,0:T(8,128)(2,1)} %bitcast.43, bf16[2048,768]{1,0:T(8,128)(2,1)} %bitcast.45, bf16[2048,768]{1,0:T(8,128)(2,1)} %bitcast.42, bf16[2048,768]{1,0:T(8,128)(2,1)} %bitcast.44), custom_call_target="tpu_custom_call" | custom-call | bytes 21600000 | tf_op jit(solution)/shard_map/weight_shares/pallas_call | solution.py:44
  161.6 8.4 %attention_back_step.7 = (bf16[256,768]{1,0:T(8,128)(2,1)}, f32[1,768]{1,0:T(1,128)S(1)}, f32[128,768]{1,0:T(8,128)}, bf16[256,768]{1,0:T(8,128)(2,1)S(1)}, bf16...) custom-call(s32[3]{0:T(128)S(1)} %pad_add_fusion.core_ref.place_ref,, ...), custom_call_target="tpu_custom_call", output_to_operand_aliasing={{5}: (15, {}), {6}: (16, {}), {7}: (17, {})} | custom-call | bytes 21600000 | tf_op jit(solution)/shard_map/attention_back_step/pallas_call | solution.py:44
  173.5 9.1 %attention_back_step.8 = (bf16[256,768]{1,0:T(8,128)(2,1)S(1)}, f32[1,768]{1,0:T(1,128)S(1)}, f32[128,768]{1,0:T(8,128)}, bf16[256,768]{1,0:T(8,128)(2,1)}, bf16...) custom-call(s32[3]{0:T(128)S(1)} %pad_add_fusion.core_ref.place_ref,, ...), custom_call_target="tpu_custom_call", output_to_operand_aliasing={{5}: (15, {}), {6}: (16, {}), {7}: (17, {})} | custom-call | bytes 21600000 | tf_op jit(solution)/shard_map/attention_back_step/pallas_call | solution.py:44
  183.3 4.1 %collective-permute-done.38.refs_1_ = bf16[4,96,1536]{2,1,0:T(8,128)(2,1)} collective-permute-done((bf16[4,96,1536]{2,1,0:T(8,128)(2,1)}, bf16[4,96,1536]{2,1,0:T(8,128)(2,1)}, u32[]{:S(2)}, u32[]{:S(2)}) %collective-permute-start.38) | collective-permute-done | bytes 1179680 | tf_op jit(solution)/shard_map/ppermute | solution.py:56
  191.4 6.9 %weight_shares.3 = (bf16[4,96,768]{2,1,0:T(8,128)(2,1)S(1)}, bf16[4,96,768]{2,1,0:T(8,128)(2,1)S(1)}) custom-call(s32[1]{0:T(128)} %bitcast.where_ref, bf16[2048,768]{1,0:T(8,128)(2,1)} %bitcast.50, bf16[2048,576]{1,0:T(8,128)(2,1)} %bitcast.47, bf16[2048,768]{1,0:T(8,128)(2,1)} %bitcast.46, bf16[2048,192]{1,0:T(8,128)(2,1)S(1)} %bitcast.41), custom_call_target="tpu_custom_call" | custom-call | bytes 21600000 | tf_op jit(solution)/shard_map/weight_shares/pallas_call | solution.py:44
  199.2 7.0 %collective-permute-done.39.refs_1_ = bf16[2,96,1536]{2,1,0:T(8,128)(2,1)} collective-permute-done((bf16[2,96,1536]{2,1,0:T(8,128)(2,1)}, bf16[2,96,1536]{2,1,0:T(8,128)(2,1)}, u32[]{:S(2)}, u32[]{:S(2)}) %collective-permute-start.39) | collective-permute-done | bytes 589856 | tf_op jit(solution)/shard_map/ppermute | solution.py:56
  214.9 5.1 %diagonal_sums.1 = f32[3,1,1024]{2,1,0:T(1,128)} custom-call(bf16[4,3,512,512]{3,2,1,0:T(8,128)(2,1)} %get-tuple-element.425.grid_ref), custom_call_target="tpu_custom_call" | custom-call | bytes 10800000 | tf_op jit(solution)/shard_map/diagonal_sums/pallas_call | solution.py:44
  228.2 4.0 %place_halves.1 = bf16[4,512,768]{2,1,0:T(8,128)(2,1)} custom-call(s32[3]{0:T(128)S(1)} %pad_add_fusion.core_ref.place_ref, bf16[4,256,768]{2,1,0:T(8,128)(2,1)} %get-tuple-element.377.own_ref, bf16[4,256,768]{2,1,0:T(8,128)(2,1)} %collective-permute-done.33.far_ref), custom_call_target="tpu_custom_call" | custom-call | bytes 9000000 | tf_op jit(solution)/shard_map/place_halves/pallas_call | solution.py:44
  252.7 7.3 %collective-permute-done.49.refs_2_ = bf16[1,96,768]{2,1,0:T(8,128)(2,1)S(1)} collective-permute-done((bf16[1,96,768]{2,1,0:T(8,128)(2,1)S(1)}, bf16[1,96,768]{2,1,0:T(8,128)(2,1)S(1)}, u32[]{:S(2)}, u32[]{:S(2)}) %collective-permute-start.49) | collective-permute-done | bytes 147488 | tf_op jit(solution)/shard_map/ppermute | solution.py:56
  263.7 5.6 %weave_halves.1 = bf16[412,4,768]{2,1,0:T(4,128)(2,1)} custom-call(s32[3]{0:T(128)S(1)} %pad_add_fusion.core_ref.place_ref, bf16[3,256,768]{2,1,0:T(8,128)(2,1)} %copy-done.5, bf16[3,256,768]{2,1,0:T(8,128)(2,1)} %collective-permute-done.51.refs_1_, bf16[1,256,768]{2,1,0:T(8,128)(2,1)} %copy-done.10, bf16[1,256,768]{2,1,0:T(8,128)(2,1)} %copy-done.40), custom_call_target="tpu_custom_call" | custom-call | bytes 14400000 | tf_op jit(solution)/shard_map/weave_halves/pallas_call | solution.py:44
  (259 shorter events, 100.0 us)
Async XLA Ops:
  12.2 19.5 %collective-permute-start.4 = (bf16[384,768]{1,0:T(8,128)(2,1)}, bf16[384,768]{1,0:T(8,128)(2,1)}, u32[]{:S(2)}, u32[]{:S(2)}) collective-permute-start(bf16[384,768]{1,0:T(8,128)(2,1)} %dynamic-slice_bitcast_fusion), channel_id=1, source_target_pairs={{0,2},{1,3},{2,0},{3,1},{4,6},{5,7},{6,4},{7,5},{8,10},{9,11},{10,... | collective-permute-start | bytes 1769480 | tf_op jit(solution)/shard_map/ppermute | solution.py:56
  14.5 26.4 %collective-permute-start = (bf16[384,768]{1,0:T(8,128)(2,1)}, bf16[384,768]{1,0:T(8,128)(2,1)}, u32[]{:S(2)}, u32[]{:S(2)}) collective-permute-start(bf16[384,768]{1,0:T(8,128)(2,1)} %dynamic-slice_bitcast_fusion.1), channel_id=1, source_target_pairs={{0,2},{1,3},{2,0},{3,1},{4,6},{5,7},{6,4},{7,5},{8,10},{9,11},{10,... | collective-permute-start | bytes 1769480 | tf_op jit(solution)/shard_map/ppermute | solution.py:56
  41.2 16.4 %collective-permute-start.7 = (bf16[384,768]{1,0:T(8,128)(2,1)}, bf16[384,768]{1,0:T(8,128)(2,1)S(1)}, u32[]{:S(2)}, u32[]{:S(2)}) collective-permute-start(bf16[384,768]{1,0:T(8,128)(2,1)} %collective-permute-done.4.refs_4_.refs_7_.refs_5_), channel_id=1, source_target_pairs={{0,4},{4,0},{8,12},{12,8},{16,20},{20,16},{24,28},{28,24},{1,5},{5... | collective-permute-start | bytes 1769480 | tf_op jit(solution)/shard_map/ppermute | solution.py:56
  48.5 15.2 %collective-permute-start.11 = (bf16[256,768]{1,0:T(8,128)(2,1)S(1)}, bf16[256,768]{1,0:T(8,128)(2,1)S(1)}, u32[]{:S(2)}, u32[]{:S(2)}) collective-permute-start(bf16[256,768]{1,0:T(8,128)(2,1)S(1)} %get-tuple-element.284.refs_2_), channel_id=1, source_target_pairs={{0,2},{1,3},{2,0},{3,1},{4,6},{5,7},{6,4},{7,5},{8,10},{9,11},{10,... | collective-permute-start | bytes 1179656 | tf_op jit(solution)/shard_map/ppermute | solution.py:56
  50.0 21.0 %collective-permute-start.10 = (bf16[384,768]{1,0:T(8,128)(2,1)}, bf16[384,768]{1,0:T(8,128)(2,1)S(1)}, u32[]{:S(2)}, u32[]{:S(2)}) collective-permute-start(bf16[384,768]{1,0:T(8,128)(2,1)} %collective-permute-done.refs_6_.refs_9_.refs_7_), channel_id=1, source_target_pairs={{0,4},{4,0},{8,12},{12,8},{16,20},{20,16},{24,28},{28,24},{1,5},{5... | collective-permute-start | bytes 1769480 | tf_op jit(solution)/shard_map/ppermute | solution.py:56
  63.8 14.1 %collective-permute-start.15 = (bf16[256,768]{1,0:T(8,128)(2,1)S(1)}, bf16[256,768]{1,0:T(8,128)(2,1)S(1)}, u32[]{:S(2)}, u32[]{:S(2)}) collective-permute-start(bf16[256,768]{1,0:T(8,128)(2,1)S(1)} %get-tuple-element.297.refs_2_), channel_id=1, source_target_pairs={{0,2},{1,3},{2,0},{3,1},{4,6},{5,7},{6,4},{7,5},{8,10},{9,11},{10,... | collective-permute-start | bytes 1179656 | tf_op jit(solution)/shard_map/ppermute | solution.py:56
  78.4 16.4 %collective-permute-start.19 = (bf16[256,768]{1,0:T(8,128)(2,1)S(1)}, bf16[256,768]{1,0:T(8,128)(2,1)S(1)}, u32[]{:S(2)}, u32[]{:S(2)}) collective-permute-start(bf16[256,768]{1,0:T(8,128)(2,1)S(1)} %get-tuple-element.308.refs_2_), channel_id=1, source_target_pairs={{0,2},{1,3},{2,0},{3,1},{4,6},{5,7},{6,4},{7,5},{8,10},{9,11},{10,... | collective-permute-start | bytes 1179656 | tf_op jit(solution)/shard_map/ppermute | solution.py:56
  94.9 13.5 %collective-permute-start.24 = (bf16[256,768]{1,0:T(8,128)(2,1)S(1)}, bf16[256,768]{1,0:T(8,128)(2,1)S(1)}, u32[]{:S(2)}, u32[]{:S(2)}) collective-permute-start(bf16[256,768]{1,0:T(8,128)(2,1)S(1)} %get-tuple-element.325.refs_0_), channel_id=1, source_target_pairs={{0,2},{1,3},{2,0},{3,1},{4,6},{5,7},{6,4},{7,5},{8,10},{9,11},{10,... | collective-permute-start | bytes 1179656 | tf_op jit(solution)/shard_map/ppermute | solution.py:56
  128.3 11.8 %collective-permute-start.30 = (bf16[512,768]{1,0:T(8,128)(2,1)S(1)}, bf16[512,768]{1,0:T(8,128)(2,1)S(1)}, u32[]{:S(2)}, u32[]{:S(2)}) collective-permute-start(bf16[512,768]{1,0:T(8,128)(2,1)S(1)} %get-tuple-element.349), channel_id=1, source_target_pairs={{0,1},{1,0},{2,3},{3,2},{4,5},{5,4},{6,7},{7,6},{8,9},{9,8},{10,11... | collective-permute-start | bytes 2359304 | tf_op jit(solution)/shard_map/ppermute | solution.py:56
  147.9 24.9 %collective-permute-start.33 = (bf16[4,256,768]{2,1,0:T(8,128)(2,1)}, bf16[4,256,768]{2,1,0:T(8,128)(2,1)}, u32[]{:S(2)}, u32[]{:S(2)}) collective-permute-start(bf16[4,256,768]{2,1,0:T(8,128)(2,1)} %get-tuple-element.377.own_ref), channel_id=1, source_target_pairs={{0,1},{1,0},{2,3},{3,2},{4,5},{5,4},{6,7},{7,6},{8,9},{9,8},{10,11... | collective-permute-start | bytes 4718600 | tf_op jit(solution)/shard_map/ppermute | solution.py:56
  158.8 28.7 %collective-permute-start.38 = (bf16[4,96,1536]{2,1,0:T(8,128)(2,1)}, bf16[4,96,1536]{2,1,0:T(8,128)(2,1)}, u32[]{:S(2)}, u32[]{:S(2)}) collective-permute-start(bf16[4,96,1536]{2,1,0:T(8,128)(2,1)} %get-tuple-element.396), channel_id=1, source_target_pairs={{0,4},{4,0},{8,12},{12,8},{16,20},{20,16},{24,28},{28,24},{1,5},{5... | collective-permute-start | bytes 3538952 | tf_op jit(solution)/shard_map/ppermute | solution.py:56
  159.8 11.2 %collective-permute-start.34 = (bf16[256,768]{1,0:T(8,128)(2,1)S(1)}, bf16[256,768]{1,0:T(8,128)(2,1)S(1)}, u32[]{:S(2)}, u32[]{:S(2)}) collective-permute-start(bf16[256,768]{1,0:T(8,128)(2,1)S(1)} %get-tuple-element.427.refs_0_), channel_id=1, source_target_pairs={{0,2},{1,3},{2,0},{3,1},{4,6},{5,7},{6,4},{7,5},{8,10},{9,11},{10,... | collective-permute-start | bytes 1179656 | tf_op jit(solution)/shard_map/ppermute | solution.py:56
  171.7 11.6 %collective-permute-start.37 = (bf16[256,768]{1,0:T(8,128)(2,1)}, bf16[256,768]{1,0:T(8,128)(2,1)S(1)}, u32[]{:S(2)}, u32[]{:S(2)}) collective-permute-start(bf16[256,768]{1,0:T(8,128)(2,1)} %get-tuple-element.429.refs_3_), channel_id=1, source_target_pairs={{0,2},{1,3},{2,0},{3,1},{4,6},{5,7},{6,4},{7,5},{8,10},{9,11},{10,... | collective-permute-start | bytes 1179656 | tf_op jit(solution)/shard_map/ppermute | solution.py:56
  191.0 15.2 %collective-permute-start.39 = (bf16[2,96,1536]{2,1,0:T(8,128)(2,1)}, bf16[2,96,1536]{2,1,0:T(8,128)(2,1)}, u32[]{:S(2)}, u32[]{:S(2)}) collective-permute-start(bf16[2,96,1536]{2,1,0:T(8,128)(2,1)} %get-tuple-element.410), channel_id=1, source_target_pairs={{0,8},{4,12},{8,0},{12,4},{16,24},{20,28},{24,16},{28,20},{1,9},{5... | collective-permute-start | bytes 1769480 | tf_op jit(solution)/shard_map/ppermute | solution.py:56
  191.4 14.8 %collective-permute-start.40 = (bf16[256,768]{1,0:T(8,128)(2,1)}, bf16[256,768]{1,0:T(8,128)(2,1)}, u32[]{:S(2)}, u32[]{:S(2)}) collective-permute-start(bf16[256,768]{1,0:T(8,128)(2,1)} %get-tuple-element.413), channel_id=1, source_target_pairs={{0,1},{1,0},{2,3},{3,2},{4,5},{5,4},{6,7},{7,6},{8,9},{9,8},{10,11... | collective-permute-start | bytes 1179656 | tf_op jit(solution)/shard_map/ppermute | solution.py:56
  209.5 11.5 %collective-permute-start.44 = (bf16[4,32,768]{2,1,0:T(8,128)(2,1)S(1)}, bf16[4,32,768]{2,1,0:T(8,128)(2,1)}, u32[]{:S(2)}, u32[]{:S(2)}) collective-permute-start(bf16[4,32,768]{2,1,0:T(8,128)(2,1)S(1)} %get-tuple-element.446), channel_id=1, source_target_pairs={{0,1},{1,0},{2,3},{3,2},{4,5},{5,4},{6,7},{7,6},{8,9},{9,8},{10,11... | collective-permute-start | bytes 589832 | tf_op jit(solution)/shard_map/ppermute | solution.py:56
  209.6 15.1 %collective-permute-start.41 = (bf16[256,768]{1,0:T(8,128)(2,1)S(1)}, bf16[256,768]{1,0:T(8,128)(2,1)S(1)}, u32[]{:S(2)}, u32[]{:S(2)}) collective-permute-start(bf16[256,768]{1,0:T(8,128)(2,1)S(1)} %copy-done.23), channel_id=1, source_target_pairs={{0,2},{1,3},{2,0},{3,1},{4,6},{5,7},{6,4},{7,5},{8,10},{9,11},{10,... | collective-permute-start | bytes 1179656 | tf_op jit(solution)/shard_map/ppermute | solution.py:56
  210.7 21.5 %collective-permute-start.42 = (bf16[4,96,768]{2,1,0:T(8,128)(2,1)}, bf16[4,96,768]{2,1,0:T(8,128)(2,1)}, u32[]{:S(2)}, u32[]{:S(2)}) collective-permute-start(bf16[4,96,768]{2,1,0:T(8,128)(2,1)} %copy-done.32), channel_id=1, source_target_pairs={{0,4},{4,0},{8,12},{12,8},{16,20},{20,16},{24,28},{28,24},{1,5},{5... | collective-permute-start | bytes 1769480 | tf_op jit(solution)/shard_map/ppermute | solution.py:56
  213.6 20.0 %collective-permute-start.43 = (bf16[1,96,1536]{2,1,0:T(8,128)(2,1)}, bf16[1,96,1536]{2,1,0:T(8,128)(2,1)}, u32[]{:S(2)}, u32[]{:S(2)}) collective-permute-start(bf16[1,96,1536]{2,1,0:T(8,128)(2,1)} %get-tuple-element.444), channel_id=1, source_target_pairs={{0,16},{4,20},{8,24},{12,28},{16,0},{20,4},{24,8},{28,12},{1,17},{... | collective-permute-start | bytes 884744 | tf_op jit(solution)/shard_map/ppermute | solution.py:56
  220.0 18.3 %collective-permute-start.46 = (bf16[256,768]{1,0:T(8,128)(2,1)}, bf16[256,768]{1,0:T(8,128)(2,1)}, u32[]{:S(2)}, u32[]{:S(2)}) collective-permute-start(bf16[256,768]{1,0:T(8,128)(2,1)} %get-tuple-element.451.refs_0_), channel_id=1, source_target_pairs={{0,2},{1,3},{2,0},{3,1},{4,6},{5,7},{6,4},{7,5},{8,10},{9,11},{10,... | collective-permute-start | bytes 1179656 | tf_op jit(solution)/shard_map/ppermute | solution.py:56
  222.7 12.8 %collective-permute-start.45 = (bf16[4,32,768]{2,1,0:T(8,128)(2,1)}, bf16[4,32,768]{2,1,0:T(8,128)(2,1)}, u32[]{:S(2)}, u32[]{:S(2)}) collective-permute-start(bf16[4,32,768]{2,1,0:T(8,128)(2,1)} %add_convert_fusion.mine_ref), channel_id=1, source_target_pairs={{0,2},{1,3},{2,0},{3,1},{4,6},{5,7},{6,4},{7,5},{8,10},{9,11},{10,... | collective-permute-start | bytes 589832 | tf_op jit(solution)/shard_map/ppermute | solution.py:56
  228.1 34.9 %collective-permute-start.51 = (bf16[3,256,768]{2,1,0:T(8,128)(2,1)S(1)}, bf16[3,256,768]{2,1,0:T(8,128)(2,1)}, u32[]{:S(2)}, u32[]{:S(2)}) collective-permute-start(bf16[3,256,768]{2,1,0:T(8,128)(2,1)S(1)} %finish.2.refs_0_), channel_id=1, source_target_pairs={{0,1},{1,0},{2,3},{3,2},{4,5},{5,4},{6,7},{7,6},{8,9},{9,8},{10,11... | collective-permute-start | bytes 3538952 | tf_op jit(solution)/shard_map/ppermute | solution.py:56
  246.6 13.4 %collective-permute-start.49 = (bf16[1,96,768]{2,1,0:T(8,128)(2,1)S(1)}, bf16[1,96,768]{2,1,0:T(8,128)(2,1)S(1)}, u32[]{:S(2)}, u32[]{:S(2)}) collective-permute-start(bf16[1,96,768]{2,1,0:T(8,128)(2,1)S(1)} %get-tuple-element.459), channel_id=1, source_target_pairs={{0,16},{4,20},{8,24},{12,28},{16,0},{20,4},{24,8},{28,12},{1,17},{... | collective-permute-start | bytes 442376 | tf_op jit(solution)/shard_map/ppermute | solution.py:56
  247.0 13.0 %collective-permute-start.50 = (bf16[1,96,768]{2,1,0:T(8,128)(2,1)S(1)}, bf16[1,96,768]{2,1,0:T(8,128)(2,1)S(1)}, u32[]{:S(2)}, u32[]{:S(2)}) collective-permute-start(bf16[1,96,768]{2,1,0:T(8,128)(2,1)S(1)} %get-tuple-element.460), channel_id=1, source_target_pairs={{0,24},{4,28},{8,16},{12,20},{16,8},{20,12},{24,0},{28,4},{1,25},{... | collective-permute-start | bytes 442376 | tf_op jit(solution)/shard_map/ppermute | solution.py:56
  (81 other events, 586.8 us)
where the time goes:
time: 275 us; the launch traced here: 270 us
  Pallas kernels  173 us (63%)
  waiting for transfers between devices  41 us (15%)
  starting transfers between devices  35 us (13%)
  local copies, waits for them, and re-layouts  13.8 us (5%)
  other arithmetic  3.62 us (1%)
    pallas_call x34, Pallas kernels, run(): call(*[pltpu.with_memory_space_constraint(v, pltpu.HBM) if (v.size >= lea...  173 us
    ppermute x55, waiting for transfers between devices, swap(): return lax.ppermute(value, axis, [(i, i ^ bit) for i in range(count)])  41 us
    ppermute x55, starting transfers between devices, swap(): return lax.ppermute(value, axis, [(i, i ^ bit) for i in range(count)])  35 us
    unnamed x101, local copies, waits for them, and re-layouts  7.72 us
  transfers between devices with their start and end apart: 55, of which 18 were waited for; matrix products, arithmetic and copies ran while one was open for 4% of the time, Pallas kernels for 51%

commit v1 on v0

--- a/solution.py
+++ b/solution.py
@@ -91,8 +91,8 @@
     )(line)
 
 
-def diag_kernel(grid_ref, line_ref):
-    packs, _, rows, _ = grid_ref.shape
+def diagonal_line(grid_ref):
+    packs, rows, _ = grid_ref.shape
     lanes = 128
     count = rows // lanes
     blocks = []
@@ -103,7 +103,7 @@
             if column < count:
                 for pack in range(packs):
                     total = total + grid_ref[
-                        pack, 0, band * lanes : (band + 1) * lanes, column * lanes : (column + 1) * lanes
+                        pack, band * lanes : (band + 1) * lanes, column * lanes : (column + 1) * lanes
                     ].astype(wide)
         blocks.append(total)
     held = jnp.concatenate(blocks, axis=1)
@@ -113,19 +113,7 @@
     line = total[0:1]
     for row in range(1, 8):
         line = line + pltpu.roll(total[row : row + 1], 2 * rows - row, 1)
-    line_ref[0] = line
-
-
-def diagonal_sums(grid):
-    packs, heads, rows, _ = grid.shape
-    return kernel_call(
-        diag_kernel, 3,
-        grid=(heads,),
-        in_specs=[pl.BlockSpec((packs, 1, rows, rows), lambda h: (0, h, 0, 0))],
-        out_specs=pl.BlockSpec((1, 1, 2 * rows), lambda h: (h, 0, 0)),
-        out_shape=in_hbm((heads, 1, 2 * rows), wide),
-        name="diagonal_sums",
-    )(grid)
+    return line
 
 
 def shifted_text_kernel(tokens_ref, gain_ref, weight_ref, *refs):
@@ -776,34 +764,63 @@
     )(core, rows, gain, *[v for part in parts for v in part])
 
 
-def place_kernel(core_ref, own_ref, far_ref, out_ref, sems):
-    packs, half, _ = own_ref.shape
-    copies = []
-    for pack in range(packs):
+def middle_kernel(packs, place_ref, scores_any, rows_any, gain_ref, own_ref, far_ref, *refs):
+    refs, (line_ref, ended_ref, out_any, scores_ref, values_ref, load_sems, save_sems) = refs[:-7], refs[-7:]
+    heads = scores_ref.shape[0]
+    half = values_ref.shape[1]
+    core = place_ref[0]
+    start = pl.multiple_of(core * half, half)
+    value_loads = [
+        pltpu.make_async_copy(rows_any.at[pack, pl.ds(start, half)], values_ref.at[i], load_sems.at[i])
+        for i, pack in enumerate(packs)
+    ]
+    score_loads = [
+        pltpu.make_async_copy(scores_any.at[:, head], scores_ref.at[head], load_sems.at[len(packs) + head])
+        for head in range(heads)
+    ]
+    for copy in value_loads + score_loads:
+        copy.start()
+    saves = []
+    for pack in range(own_ref.shape[0]):
         for side, ref in enumerate((own_ref, far_ref)):
-            start = pl.multiple_of(jnp.bitwise_xor(core_ref[0], side) * half, half)
-            copies.append(
-                pltpu.make_async_copy(
-                    ref.at[pack], out_ref.at[pack, pl.ds(start, half)], sems.at[2 * pack + side]
-                )
-            )
-    for copy in copies:
-        copy.start()
-    for copy in copies:
+            there = pl.ds(pl.multiple_of(jnp.bitwise_xor(core, side) * half, half), half)
+            copy = pltpu.make_async_copy(ref.at[pack], out_any.at[pack, there], save_sems.at[2 * pack + side])
+            copy.start()
+            saves.append(copy)
+    for i, copy in enumerate(value_loads):
         copy.wait()
-
-
-def place_halves(core, own, far):
-    packs, half, model = own.shape
-    inside = pl.BlockSpec(memory_space=pltpu.VMEM)
+        pair_ref, far_pair_ref, grad_ref = refs[3 * i : 3 * i + 3]
+        upstream = pair_ref[...].astype(wide) + far_pair_ref[...].astype(wide)
+        grad, _ = norm_back(upstream, gain_ref[...], values_ref[i].astype(wide))
+        ended_ref[i] = (grad_ref[...] + grad).astype(low)
+    for head, copy in enumerate(score_loads):
+        copy.wait()
+        line_ref[head] = diagonal_line(scores_ref.at[head])
+    for copy in saves:
+        copy.wait()
+
+
+def middle_work(packs, place, scores, rows, gain, own, far, parts):
+    count, heads, row_count, _ = scores.shape
+    _, half, model = own.shape
+    inside, anywhere = pl.BlockSpec(memory_space=pltpu.VMEM), pl.BlockSpec(memory_space=pl.ANY)
     return kernel_call(
-        place_kernel, 2.5, vmem=24, least=1000,
-        in_specs=[pl.BlockSpec(memory_space=pltpu.SMEM), inside, inside],
-        out_specs=pl.BlockSpec(memory_space=pl.ANY),
-        out_shape=in_hbm((packs, 2 * half, model), low),
-        scratch_shapes=[pltpu.SemaphoreType.DMA((2 * packs,))],
-        name="place_halves",
-    )(core, own, far)
+        functools.partial(middle_kernel, packs), 12, vmem=40, least=1000,
+        in_specs=[pl.BlockSpec(memory_space=pltpu.SMEM), anywhere, anywhere] + [inside] * (3 + 3 * len(packs)),
+        out_specs=[inside, inside, anywhere],
+        out_shape=[
+            jax.ShapeDtypeStruct((heads, 1, 2 * row_count), wide),
+            jax.ShapeDtypeStruct((len(packs), half, model), low),
+            in_hbm((count, row_count, model), low),
+        ],
+        scratch_shapes=[
+            pltpu.VMEM((heads, count, row_count, row_count), low),
+            pltpu.VMEM((len(packs), half, model), low),
+            pltpu.SemaphoreType.DMA((len(packs) + heads,)),
+            pltpu.SemaphoreType.DMA((2 * count,)),
+        ],
+        name="middle_work",
+    )(place, scores, rows, gain, own, far, *[v for part in parts for v in part])
 
 
 def weave_kernel(core_ref, *refs):
@@ -938,31 +955,61 @@
     )(*parts)
 
 
-def small_fold_kernel(has_rel, side_ref, mine_ref, got_ref, *refs):
-    keep_ref, send_ref, total_ref = refs[-3:]
-    groups, rows, _ = mine_ref.shape
-    half = groups // 2
-    total_ref[...] = mine_ref[...].astype(wide) + got_ref[...].astype(wide)
-    if has_rel:
-        rel_ref, spot = refs[0], refs[1]
-        for group in range(groups):
-            total_ref[group, spot[0], :] = rel_ref[0, :]
-    keep_ref[...] = total_ref[pl.ds(side_ref[0] * half, half)].astype(low)
-    send_ref[...] = total_ref[pl.ds((1 - side_ref[0]) * half, half)].astype(low)
-
-
-def small_fold(side, mine, got, rel=None, spot=None):
-    groups, rows, model = mine.shape
-    inside, scalar = pl.BlockSpec(memory_space=pltpu.VMEM), pl.BlockSpec(memory_space=pltpu.SMEM)
-    more = [] if rel is None else [rel, jnp.full((1,), spot, jnp.int32)]
+def joint_fold_kernel(spot, where_ref, keep_ref, got_ref, mine_ref, near_ref, rel_ref, *refs):
+    outs, total_ref = refs[:4], refs[4]
+    block = keep_ref.shape[1]
+    group = keep_ref.shape[0] // 4
+    for flip, out_ref in enumerate(outs):
+        chosen = jnp.bitwise_xor(where_ref[0], flip)
+        for piece in range(group):
+            total = keep_ref[chosen * group + piece].astype(wide) + got_ref[chosen * group + piece].astype(wide)
+            out_ref[piece * block : (piece + 1) * block, :] = total.astype(low)
+        total_ref[...] = mine_ref[chosen].astype(wide) + near_ref[chosen].astype(wide)
+        total_ref[spot : spot + 1, :] = rel_ref[...]
+        out_ref[group * block :, :] = total_ref[...].astype(low)
+
+
+def joint_fold(where, parts, smalls, rel, spot):
+    whole, block, width = parts[0].shape
+    rows = smalls[0].shape[1]
+    shape = (whole // 4 * block + rows, width)
+    inside = pl.BlockSpec(memory_space=pltpu.VMEM)
     return kernel_call(
-        functools.partial(small_fold_kernel, rel is not None), 1,
-        in_specs=[scalar, inside, inside] + ([inside, scalar] if more else []),
-        out_specs=[inside] * 2,
-        out_shape=[jax.ShapeDtypeStruct((groups // 2, rows, model), low)] * 2,
-        scratch_shapes=[pltpu.VMEM((groups, rows, model), wide)],
-        name="small_fold",
-    )(side, mine, got, *more)
+        functools.partial(joint_fold_kernel, spot), 2,
+        in_specs=[pl.BlockSpec(memory_space=pltpu.SMEM)] + [inside] * 5,
+        out_specs=[inside] * 4,
+        out_shape=[jax.ShapeDtypeStruct(shape, low)] * 4,
+        scratch_shapes=[pltpu.VMEM((rows, width), wide)],
+        name="joint_fold",
+    )(where, *parts, *smalls, rel)
+
+
+def joint_unfold_kernel(cuts, *refs):
+    ins, outs = refs[:4], refs[4:]
+    total = ins[0][...].astype(wide)
+    for ref in ins[1:]:
+        total = total + ref[...].astype(wide)
+    small = outs[-1].shape[0]
+    outs[-1][...] = total[-small:].astype(low)
+    for (start, width, turned), out_ref in zip(cuts, outs):
+        piece = total[:-small, start : start + width]
+        out_ref[...] = piece.T if turned else piece
+
+
+def joint_unfold(parts, cuts, rows):
+    block = parts[0].shape[0] - rows
+    inside = pl.BlockSpec(memory_space=pltpu.VMEM)
+    return kernel_call(
+        functools.partial(joint_unfold_kernel, cuts), 1.5,
+        in_specs=[inside] * 4,
+        out_specs=[inside] * (len(cuts) + 1),
+        out_shape=[
+            jax.ShapeDtypeStruct((width, block) if turned else (block, width), wide)
+            for _, width, turned in cuts
+        ]
+        + [jax.ShapeDtypeStruct((rows, parts[0].shape[1]), low)],
+        name="joint_unfold",
+    )(*parts)
 
 
 def tie(*values):
@@ -1026,8 +1073,6 @@
     def __init__(self, total, prompt_len):
         self.total, self.share = total, prompt_len // self.groups
         self.mp_bits = bits_of(lax.axis_size("mp"))
-        self.dp_bits = bits_of(lax.axis_size("dp"))[::-1]
-        self.hops = 0
         self.hop_mp()
 
     def hop_mp(self):
@@ -1037,25 +1082,30 @@
     def land(self):
         self.total = (self.keep.astype(wide) + self.got.astype(wide)).astype(low)
 
-    def hop_dp(self, rel=None):
-        bit, self.dp_bits = self.dp_bits[0], self.dp_bits[1:]
-        if self.hops < 2:
-            side = ((lax.axis_index("dp") // bit) % 2).astype(jnp.int32).reshape(1)
-            if rel is not None:
-                self.rel = rel
-                rel = jnp.pad(rel.reshape(1, -1), ((0, 0), (0, self.keep.shape[2] - rel.size)))
-            self.keep, send = small_fold(side, self.keep, self.got, rel, self.share + 2)
-        else:
-            self.land()
-            self.keep = send = self.total
-        self.hops += 1
-        self.got = swap(send, "dp", bit)
+    def join(self, tail, rel):
+        self.rel = rel
+        row = jnp.pad(rel.reshape(1, -1), ((0, 0), (0, self.keep.shape[2] - rel.size)))
+        high, tail.bits = tail.bits[-2], tail.bits[:-2]
+        where = ((lax.axis_index("dp") // high) % 4).astype(jnp.int32).reshape(1)
+        self.block = tail.parts[0].shape[1]
+        own, *sends = joint_fold(where, tail.parts, (self.keep, self.got), row, self.share + 2)
+        self.parts = [own] + [swap(v, "dp", high * (flip + 1)) for flip, v in enumerate(sends)]
+
+    def split(self, tail, cuts):
+        rows = self.keep.shape[1]
+        if not tail.bits:
+            *results, self.total = joint_unfold(self.parts, cuts, rows)
+            return results
+        tail.parts = [v[:-rows].reshape(-1, self.block, v.shape[1]) for v in self.parts]
+        self.total = sum(v[-rows:].astype(wide) for v in self.parts).astype(low)
+        return tail.end(cuts)
 
     def results(self):
-        while self.dp_bits:
-            self.hop_dp()
-        total = self.keep[0].astype(wide) + self.got[0].astype(wide)
         dp_count, dp_index = lax.axis_size("dp"), lax.axis_index("dp")
+        total = self.total
+        for bit in bits_of(dp_count)[:-2]:
+            total = total.astype(low)
+            total = total.astype(wide) + swap(total, "dp", bit).astype(wide)
         share, model = self.share, total.shape[1]
         inside = dp_count // self.groups
         size = share * model // inside
@@ -1189,6 +1239,14 @@
             pair, gain1_sum, head_sum = done
             pairs_back.append([pair, swap(pair, "mp", 2)])
 
+    def near(pack):
+        nonlocal place
+        place, pairs_far[pack] = tie(place, pairs_far[pack])
+
+    def meet(pack):
+        nonlocal place
+        place, grads_low[pack] = tie(place, grads_low[pack])
+
     def end(*ended):
         nonlocal place
         rows_low = finish(ended, place, whole_rows, gain1, [(*pairs_back[p], grads_wide[p]) for p in ended])
@@ -1205,65 +1263,75 @@
     feed(0)
     attend(packs)
     arrive(1)
+    near(2)
     feed(1)
     for step in range(2, packs):
         arrive(step)
+        meet(step - 2)
+        if step + 1 < packs:
+            near(step + 1)
         feed(step)
         back(step - 2)
+    meet(packs - 2)
     feed(packs)
     normed2, active, hidden = kept
     where = lax.axis_index("dp").astype(jnp.int32).reshape(1)
     where, place = tie(where, place)
-    feed_shares = weight_shares(
-        where, groups, [(flat(normed2), flat(hidden)), (flat(cotangent), flat(active))], True
-    )
-    place, *feed_shares = tie(place, *feed_shares)
-    feed_sum = Scatter(*feed_shares, 2)
+    inner_shares = weight_shares(where, groups, [(flat(normed2), flat(hidden))], True)
+    place, inner_shares = tie(place, inner_shares)
+    inner = Scatter(*inner_shares, 2)
+    where, place = tie(where, place)
+    outer_shares = weight_shares(where, groups, [(flat(cotangent), flat(active))], True)
+    place, outer_shares = tie(place, outer_shares)
+    outer = Scatter(*outer_shares, 2)
+    meet(packs - 1)
     back(packs - 2)
     far_results = swap(results, "mp", 1)
-    place, far_results, *pairs_back[0] = tie(place, far_results, *pairs_back[0])
+    place, far_results, pairs_back[0], inner.parts = tie(place, far_results, pairs_back[0], inner.parts)
+    inner.step()
     back(packs - 1)
-    place, *pairs_back[1] = tie(place, *pairs_back[1])
-    place, *feed_sum.parts = tie(place, *feed_sum.parts)
-    feed_sum.step()
+    place, pairs_back[1], inner.parts, outer.parts = tie(place, pairs_back[1], inner.parts, outer.parts)
+    inner.step()
+    outer.step()
+    place, inner.parts[0], outer.parts[0] = tie(place, inner.parts[0], outer.parts[0])
     grad_joined, scores, grad_rows = back_kept
     where, place = tie(where, place)
     tail_shares = weight_shares(
         where, groups, [(flat(normed1), flat(grad_joined)), (flat(grad_rows), flat(mixed))], True
     )
     place, *tail_shares = tie(place, *tail_shares)
-    place, *feed_sum.parts = tie(place, *feed_sum.parts)
-    feed_sum.step()
     tail = Scatter(*tail_shares, 4)
     side_one = (mp_index // 2) % 2 == 1
     gain2_sum = jnp.where(side_one, 0.0, gain2_sum)
     back(packs)
     place, head_sum = tie(place, head_sum)
     small = Small(head_sum, prompt_len)
-    place, scores = tie(place, scores)
-    line = diagonal_sums(scores)[:, 0, :]
-    rel_share = jnp.einsum("ht,tb->bh", line, turned, precision=highest)
+    place, outer.parts = tie(place, outer.parts)
+    outer.step()
+    place, outer.parts[0] = tie(place, outer.parts[0])
     small.land()
     small.hop_mp()
-    place, rel_share = tie(place, rel_share)
-    end(*range(packs - 1))
-    out = place_halves(place, results, far_results)
-    place, out, *tail.parts = tie(place, out, *tail.parts)
-    tail.step()
-    place, tail.parts[0], *feed_sum.parts = tie(place, tail.parts[0], *feed_sum.parts)
-    hidden_width = w_inner.shape[1]
-    inner_grad, outer_grad = feed_sum.end(((0, hidden_width, False), (hidden_width, hidden_width, False)))
-    place, small.got, inner_grad = tie(place, small.got, inner_grad)
-    small.hop_dp(rel_share)
+    early = list(range(packs - 1))
+    line, rows_low, out = middle_work(
+        early, place, scores, whole_rows, gain1, results, far_results,
+        [(*pairs_back[p], grads_wide[p]) for p in early],
+    )
+    place, line, rows_low = tie(place, line, rows_low)
+    text_rows.append((rows_low, swap(rows_low, "mp", 1)))
+    rel_share = jnp.einsum("ht,tb->bh", line[:, 0, :], turned, precision=highest)
+    place, rel_share, tail.parts, small.got = tie(place, rel_share, tail.parts, small.got)
+    small.join(tail, rel_share)
+    place, small.parts[0], inner.parts, outer.parts = tie(place, small.parts[0], inner.parts, outer.parts)
+    whole_width = ((0, w_inner.shape[1], False),)
+    (inner_grad,), (outer_grad,) = inner.end(whole_width), outer.end(whole_width)
+    place, inner_grad, outer_grad = tie(place, inner_grad, outer_grad)
     end(packs - 1)
-    place, small.got = tie(place, small.got)
-    small.hop_dp()
-    text_rows[-1] = tie(*text_rows[-1])
-    place, *tail.parts = tie(place, *tail.parts)
+    place, text_rows[-1] = tie(place, text_rows[-1])
     grad_tokens = weave_halves(place, text_rows, rows - prompt_len)
+    grad_tokens, small.parts = tie(grad_tokens, small.parts)
     grad_tokens = jnp.transpose(grad_tokens, (1, 0, 2))
-    query_grad, key_grad, value_grad, output_grad = tail.end(
-        tuple((i * width, width, i == 3) for i in range(4))
+    query_grad, key_grad, value_grad, output_grad = small.split(
+        tail, tuple((i * width, width, i == 3) for i in range(4))
     )
     prompt_grad, gain1_grad, gain2_grad, rel_grad = small.results()
     return (

time: 275 us -> 268 us (0.975)
  the two profiles are of different devices: /device:TPU:0 before, /device:TPU:8 now
where the time goes in v1:
time: 268 us; the launch traced here: 263 us
  Pallas kernels  170 us (63%)
  starting transfers between devices  38.6 us (14%)
  waiting for transfers between devices  35.7 us (13%)
  local copies, waits for them, and re-layouts  13.7 us (5%)
    pallas_call x34, Pallas kernels, run(): call(*[pltpu.with_memory_space_constraint(v, pltpu.HBM) if (v.size >= lea...  170 us
    ppermute x56, starting transfers between devices, swap(): return lax.ppermute(value, axis, [(i, i ^ bit) for i in range(count)])  38.6 us
    ppermute x56, waiting for transfers between devices, swap(): return lax.ppermute(value, axis, [(i, i ^ bit) for i in range(count)])  35.7 us
    unnamed x77, local copies, waits for them, and re-layouts  7.67 us
  transfers between devices with their start and end apart: 56, of which 14 were waited for; matrix products, arithmetic and copies ran while one was open for 3% of the time, Pallas kernels for 55%

profile of v1, /device:TPU:8, one launch (start us, length us, event | category | flops | bytes accessed | tf_op | source)
XLA Modules:
  0.0 262.7 jit_solution(1074319648665254804)
XLA Ops:
  2.4 5.4 %look_up.1 = bf16[64,768]{1,0:T(8,128)(2,1)S(1)} custom-call(s32[64]{0:T(128)S(1)} %compare_select_fusion.ids_ref, bf16[4016,768]{1,0:T(8,128)(2,1)} %table_any.1, f32[64,768]{1,0:T(8,128)S(1)} %reshape.85.placed_ref), custom_call_target="tpu_custom_call" | custom-call | bytes 9000000 | tf_op jit(solution)/shard_map/look_up/pallas_call | solution.py:44
  18.7 4.2 %text_projections.2 = (bf16[4,512,768]{2,1,0:T(8,128)(2,1)}, bf16[4,512,768]{2,1,0:T(8,128)(2,1)}, bf16[4,512,576]{2,1,0:T(8,128)(2,1)}) custom-call(bf16[4,412,768]{2,1,0:T(8,128)(2,1)} %copy.78.tokens_ref, f32[1,768]{1,0:T(1,128)S(1)} %broadcast_in_dim.25.gain_ref.refs_11_.refs_5_, bf16[576,768]{1,0:T(8,128)(2,1)} %pad_maximum_fusion.weight_ref.refs_6_.refs_0_), custom_call_target="tpu_custom_call" | custom-call | bytes 8640000 | tf_op jit(solution)/shard_map/text_projections/pallas_call | solution.py:44
  24.4 4.5 %text_projections.3 = (bf16[4,512,768]{2,1,0:T(8,128)(2,1)}, bf16[4,512,768]{2,1,0:T(8,128)(2,1)}, bf16[4,512,576]{2,1,0:T(8,128)(2,1)}) custom-call(bf16[4,412,768]{2,1,0:T(8,128)(2,1)} %copy.78.tokens_ref, f32[1,768]{1,0:T(1,128)S(1)} %broadcast_in_dim.25.gain_ref.refs_11_.refs_5_, ...), custom_call_target="tpu_custom_call", output_to_operand_aliasing={{0}: (3, {}), {1}: (4, {}), {2}: (5, {})} | custom-call | bytes 8640000 | tf_op jit(solution)/shard_map/text_projections/pallas_call | solution.py:44
  30.4 3.9 %add_prompt.1 = (bf16[4,512,768]{2,1,0:T(8,128)(2,1)}, bf16[4,512,768]{2,1,0:T(8,128)(2,1)}, bf16[4,512,576]{2,1,0:T(8,128)(2,1)}) custom-call(s32[1]{0:T(128)} %bitcast.1.place_ref, bf16[2,64,768]{2,1,0:T(8,128)(2,1)S(1)} %pad_maximum_fusion.1.pieces_ref, ...), custom_call_target="tpu_custom_call", output_to_operand_aliasing={{0}: (4, {}), {1}: (5, {}), {2}: (6, {})} | custom-call | bytes 9000000 | tf_op jit(solution)/shard_map/add_prompt/pallas_call | solution.py:44
  40.0 5.6 %attention_step.6 = (bf16[256,768]{1,0:T(8,128)(2,1)S(1)}, bf16[256,768]{1,0:T(8,128)(2,1)S(1)}, bf16[1,3,256,512]{3,2,1,0:T(8,128)(2,1)}, bf16[1,3,256,512]{3,2,1,0:T(8,128)(2,1)}, bf16[4,512,192]{2,1,0:T(8,128)(2,1)}) custom-call(s32[3]{0:T(128)S(1)} %pad_add_fusion.core_ref.place_ref, ...), custom_call_target="tpu_custom_call", output_to_operand_aliasing={{4}: (7, {})} | custom-call | bytes 18000000 | tf_op jit(solution)/shard_map/attention_step/pallas_call | solution.py:44
  48.1 6.7 %collective-permute-done.7.refs_5_.refs_8_.refs_6_ = bf16[384,768]{1,0:T(8,128)(2,1)S(1)} collective-permute-done((bf16[384,768]{1,0:T(8,128)(2,1)}, bf16[384,768]{1,0:T(8,128)(2,1)S(1)}, u32[]{:S(2)}, u32[]{:S(2)}) %collective-permute-start.7) | collective-permute-done | bytes 589856 | tf_op jit(solution)/shard_map/ppermute | solution.py:56
  54.8 5.6 %attention_step.7 = (bf16[256,768]{1,0:T(8,128)(2,1)S(1)}, bf16[256,768]{1,0:T(8,128)(2,1)S(1)}, bf16[1,3,256,512]{3,2,1,0:T(8,128)(2,1)}, bf16[1,3,256,512]{3,2,1,0:T(8,128)(2,1)}, bf16[4,512,192]{2,1,0:T(8,128)(2,1)}) custom-call(s32[3]{0:T(128)S(1)} %pad_add_fusion.core_ref.place_ref, ...), custom_call_target="tpu_custom_call", output_to_operand_aliasing={{4}: (7, {})} | custom-call | bytes 18000000 | tf_op jit(solution)/shard_map/attention_step/pallas_call | solution.py:44
  62.5 5.6 %attention_step.8 = (bf16[256,768]{1,0:T(8,128)(2,1)S(1)}, bf16[256,768]{1,0:T(8,128)(2,1)S(1)}, bf16[1,3,256,512]{3,2,1,0:T(8,128)(2,1)}, bf16[1,3,256,512]{3,2,1,0:T(8,128)(2,1)}, bf16[4,512,192]{2,1,0:T(8,128)(2,1)}) custom-call(s32[3]{0:T(128)S(1)} %pad_add_fusion.core_ref.place_ref, ...), custom_call_target="tpu_custom_call", output_to_operand_aliasing={{4}: (7, {})} | custom-call | bytes 18000000 | tf_op jit(solution)/shard_map/attention_step/pallas_call | solution.py:44
  68.1 6.3 %feed_step.5 = (bf16[4,512,768]{2,1,0:T(8,128)(2,1)}, bf16[4,512,768]{2,1,0:T(8,128)(2,1)}, bf16[4,512,768]{2,1,0:T(8,128)(2,1)}, bf16[512,768]{1,0:T(8,128)(2,1)S(1)}) custom-call(s32[3]{0:T(128)S(1)} %pad_add_fusion.core_ref.place_ref, bf16[4,512,768]{2,1,0:T(8,128)(2,1)} %get-tuple-element.318.rows_any.refs_9_.refs_3_, bf16[4,512,768]{2,1,0:T(8,128)(2,1)} %cot_any.9, ...), custom_call_target="tpu_custom_call" | custom-call | bytes 28800000 | tf_op jit(solution)/shard_map/feed_step/pallas_call | solution.py:44
  82.4 10.1 %feed_step.6 = (bf16[4,512,768]{2,1,0:T(8,128)(2,1)}, bf16[4,512,768]{2,1,0:T(8,128)(2,1)}, bf16[4,512,768]{2,1,0:T(8,128)(2,1)}, bf16[512,768]{1,0:T(8,128)(2,1...) custom-call(s32[3]{0:T(128)S(1)} %pad_add_fusion.core_ref.place_ref,, ...), custom_call_target="tpu_custom_call", output_to_operand_aliasing={{0}: (15, {}), {1}: (16, {}), {2}: (17, {})} | custom-call | bytes 43200000 | tf_op jit(solution)/shard_map/feed_step/pallas_call | solution.py:44
  96.5 10.0 %feed_step.7 = (bf16[4,512,768]{2,1,0:T(8,128)(2,1)}, bf16[4,512,768]{2,1,0:T(8,128)(2,1)}, bf16[4,512,768]{2,1,0:T(8,128)(2,1)}, bf16[512,768]{1,0:T(8,128)(2,1...) custom-call(s32[3]{0:T(128)S(1)} %pad_add_fusion.core_ref.place_ref,, ...), custom_call_target="tpu_custom_call", output_to_operand_aliasing={{0}: (15, {}), {1}: (16, {}), {2}: (17, {}), {7}: (18, {})} | custom-call | bytes 43200000 | tf_op jit(solution)/shard_map/feed_step/pallas_call | solution.py:44
  107.3 7.7 %attention_back_step.5 = (bf16[256,768]{1,0:T(8,128)(2,1)S(1)}, bf16[256,576]{1,0:T(8,128)(2,1)}, bf16[4,512,576]{2,1,0:T(8,128)(2,1)}, bf16[4,3,512,512]{3,2,1,0:T(8,128)(2,1)}, bf16[4,512,768]{2,1,0:T(8,128)(2,1)}) custom-call(s32[3]{0:T(128)S(1)} %pad_add_fusion.core_ref.place_ref, bf16[256,768]{1,0:T(8,128)(2,1)S(1)} %get-tuple-element.358.refs_0_, ...), custom_call_target="tpu_custom_call" | custom-call | bytes 21600000 | tf_op jit(solution)/shard_map/attention_back_step/pallas_call | solution.py:44
  115.1 10.1 %feed_step.8 = (bf16[4,512,768]{2,1,0:T(8,128)(2,1)}, bf16[4,512,768]{2,1,0:T(8,128)(2,1)}, bf16[4,512,768]{2,1,0:T(8,128)(2,1)}, bf16[512,768]{1,0:T(8,128)(2,1...) custom-call(s32[3]{0:T(128)S(1)} %pad_add_fusion.core_ref.place_ref,, ...), custom_call_target="tpu_custom_call", output_to_operand_aliasing={{0}: (15, {}), {1}: (16, {}), {2}: (17, {}), {7}: (18, {})} | custom-call | bytes 43200000 | tf_op jit(solution)/shard_map/feed_step/pallas_call | solution.py:44
  128.1 8.4 %attention_back_step.6 = (bf16[256,768]{1,0:T(8,128)(2,1)S(1)}, f32[1,768]{1,0:T(1,128)S(1)}, f32[128,768]{1,0:T(8,128)}, bf16[256,768]{1,0:T(8,128)(2,1)S(1)}, ...) custom-call(s32[3]{0:T(128)S(1)} %pad_add_fusion.core_ref.place_ref,, ...), custom_call_target="tpu_custom_call", output_to_operand_aliasing={{5}: (15, {}), {6}: (16, {}), {7}: (17, {})} | custom-call | bytes 21600000 | tf_op jit(solution)/shard_map/attention_back_step/pallas_call | solution.py:44
  136.5 7.7 %feed_step.9 = (bf16[4,512,768]{2,1,0:T(8,128)(2,1)}, bf16[4,512,768]{2,1,0:T(8,128)(2,1)}, bf16[4,512,768]{2,1,0:T(8,128)(2,1)}, f32[256,768]{1,0:T(8,128)}, bf...) custom-call(s32[3]{0:T(128)S(1)} %pad_add_fusion.core_ref.place_ref,, ...), custom_call_target="tpu_custom_call", output_to_operand_aliasing={{0}: (13, {}), {1}: (14, {}), {2}: (15, {}), {6}: (16, {})} | custom-call | bytes 28800000 | tf_op jit(solution)/shard_map/feed_step/pallas_call | solution.py:44
  145.2 6.3 %weight_shares.3 = (bf16[4,96,768]{2,1,0:T(8,128)(2,1)S(1)}, bf16[4,96,768]{2,1,0:T(8,128)(2,1)}) custom-call(s32[1]{0:T(128)} %bitcast.where_ref, bf16[2048,768]{1,0:T(8,128)(2,1)} %bitcast.43, bf16[2048,768]{1,0:T(8,128)(2,1)} %bitcast.45), custom_call_target="tpu_custom_call" | custom-call | bytes 21600000 | tf_op jit(solution)/shard_map/weight_shares/pallas_call | solution.py:44
  153.2 6.8 %weight_shares.4 = (bf16[4,96,768]{2,1,0:T(8,128)(2,1)S(1)}, bf16[4,96,768]{2,1,0:T(8,128)(2,1)}) custom-call(s32[1]{0:T(128)} %bitcast.where_ref, bf16[2048,768]{1,0:T(8,128)(2,1)} %bitcast.42, bf16[2048,768]{1,0:T(8,128)(2,1)} %bitcast.44), custom_call_target="tpu_custom_call" | custom-call | bytes 21600000 | tf_op jit(solution)/shard_map/weight_shares/pallas_call | solution.py:44
  161.4 8.5 %attention_back_step.7 = (bf16[256,768]{1,0:T(8,128)(2,1)}, f32[1,768]{1,0:T(1,128)S(1)}, f32[128,768]{1,0:T(8,128)}, bf16[256,768]{1,0:T(8,128)(2,1)}, bf16[256...) custom-call(s32[3]{0:T(128)S(1)} %pad_add_fusion.core_ref.place_ref,, ...), custom_call_target="tpu_custom_call", output_to_operand_aliasing={{5}: (15, {}), {6}: (16, {}), {7}: (17, {})} | custom-call | bytes 21600000 | tf_op jit(solution)/shard_map/attention_back_step/pallas_call | solution.py:44
  175.1 9.1 %attention_back_step.8 = (bf16[256,768]{1,0:T(8,128)(2,1)}, f32[1,768]{1,0:T(1,128)S(1)}, f32[128,768]{1,0:T(8,128)}, bf16[256,768]{1,0:T(8,128)(2,1)}, bf16[256...) custom-call(s32[3]{0:T(128)S(1)} %pad_add_fusion.core_ref.place_ref,, ...), custom_call_target="tpu_custom_call", output_to_operand_aliasing={{5}: (15, {}), {6}: (16, {}), {7}: (17, {})} | custom-call | bytes 21600000 | tf_op jit(solution)/shard_map/attention_back_step/pallas_call | solution.py:44
  186.7 8.3 %weight_shares.5 = (bf16[4,96,768]{2,1,0:T(8,128)(2,1)S(1)}, bf16[4,96,768]{2,1,0:T(8,128)(2,1)}) custom-call(s32[1]{0:T(128)} %bitcast.where_ref, bf16[2048,768]{1,0:T(8,128)(2,1)} %bitcast.50, bf16[2048,576]{1,0:T(8,128)(2,1)} %bitcast.47, bf16[2048,768]{1,0:T(8,128)(2,1)} %bitcast.46, bf16[2048,192]{1,0:T(8,128)(2,1)S(1)} %bitcast.41), custom_call_target="tpu_custom_call" | custom-call | bytes 21600000 | tf_op jit(solution)/shard_map/weight_shares/pallas_call | solution.py:44
  199.6 8.2 %middle_work.1 = (f32[3,1,1024]{2,1,0:T(1,128)S(1)}, bf16[3,256,768]{2,1,0:T(8,128)(2,1)S(1)}, bf16[4,512,768]{2,1,0:T(8,128)(2,1)}) custom-call(s32[3]{0:T(128)S(1)} %pad_add_fusion.core_ref.place_ref, bf16[4,3,512,512]{3,2,1,0:T(8,128)(2,1)} %get-tuple-element.490.scores_any, bf16[4,512,768]{2,1,0:T(8,128)(2,1)} %get-tuple-element.318.rows_any.refs_9_.refs_3_, ...), custom_call_target="tpu_custom_call" | custom-call | bytes 43200000 | tf_op jit(solution)/shard_map/middle_work/pallas_call | solution.py:44
  238.4 5.6 %weave_halves.1 = bf16[412,4,768]{2,1,0:T(4,128)(2,1)} custom-call(s32[3]{0:T(128)S(1)} %pad_add_fusion.core_ref.place_ref, bf16[3,256,768]{2,1,0:T(8,128)(2,1)} %copy-done.9, bf16[3,256,768]{2,1,0:T(8,128)(2,1)} %collective-permute-done.51.refs_1_, bf16[1,256,768]{2,1,0:T(8,128)(2,1)} %copy-done.8, bf16[1,256,768]{2,1,0:T(8,128)(2,1)} %copy-done.28), custom_call_target="tpu_custom_call" | custom-call | bytes 14400000 | tf_op jit(solution)/shard_map/weave_halves/pallas_call | solution.py:44
  244.4 5.9 %collective-permute-done.53.refs_2_ = bf16[128,768]{1,0:T(8,128)(2,1)S(1)} collective-permute-done((bf16[128,768]{1,0:T(8,128)(2,1)S(1)}, bf16[128,768]{1,0:T(8,128)(2,1)S(1)}, u32[]{:S(2)}, u32[]{:S(2)}) %collective-permute-start.53) | collective-permute-done | bytes 196640 | tf_op jit(solution)/shard_map/ppermute | solution.py:56
  250.3 5.2 %collective-permute-done.54.refs_3_ = bf16[128,768]{1,0:T(8,128)(2,1)S(1)} collective-permute-done((bf16[128,768]{1,0:T(8,128)(2,1)S(1)}, bf16[128,768]{1,0:T(8,128)(2,1)S(1)}, u32[]{:S(2)}, u32[]{:S(2)}) %collective-permute-start.54) | collective-permute-done | bytes 196640 | tf_op jit(solution)/shard_map/ppermute | solution.py:56
  (236 shorter events, 95.4 us)
Async XLA Ops:
  9.7 19.2 %collective-permute-start.4 = (bf16[384,768]{1,0:T(8,128)(2,1)}, bf16[384,768]{1,0:T(8,128)(2,1)}, u32[]{:S(2)}, u32[]{:S(2)}) collective-permute-start(bf16[384,768]{1,0:T(8,128)(2,1)} %dynamic-slice_bitcast_fusion), channel_id=1, source_target_pairs={{0,2},{1,3},{2,0},{3,1},{4,6},{5,7},{6,4},{7,5},{8,10},{9,11},{10,... | collective-permute-start | bytes 1769480 | tf_op jit(solution)/shard_map/ppermute | solution.py:56
  12.1 26.1 %collective-permute-start = (bf16[384,768]{1,0:T(8,128)(2,1)}, bf16[384,768]{1,0:T(8,128)(2,1)}, u32[]{:S(2)}, u32[]{:S(2)}) collective-permute-start(bf16[384,768]{1,0:T(8,128)(2,1)} %dynamic-slice_bitcast_fusion.1), channel_id=1, source_target_pairs={{0,2},{1,3},{2,0},{3,1},{4,6},{5,7},{6,4},{7,5},{8,10},{9,11},{10,... | collective-permute-start | bytes 1769480 | tf_op jit(solution)/shard_map/ppermute | solution.py:56
  38.4 16.4 %collective-permute-start.7 = (bf16[384,768]{1,0:T(8,128)(2,1)}, bf16[384,768]{1,0:T(8,128)(2,1)S(1)}, u32[]{:S(2)}, u32[]{:S(2)}) collective-permute-start(bf16[384,768]{1,0:T(8,128)(2,1)} %collective-permute-done.4.refs_4_.refs_7_.refs_5_), channel_id=1, source_target_pairs={{0,4},{4,0},{8,12},{12,8},{16,20},{20,16},{24,28},{28,24},{1,5},{5... | collective-permute-start | bytes 1769480 | tf_op jit(solution)/shard_map/ppermute | solution.py:56
  45.8 15.1 %collective-permute-start.11 = (bf16[256,768]{1,0:T(8,128)(2,1)S(1)}, bf16[256,768]{1,0:T(8,128)(2,1)S(1)}, u32[]{:S(2)}, u32[]{:S(2)}) collective-permute-start(bf16[256,768]{1,0:T(8,128)(2,1)S(1)} %get-tuple-element.316.refs_2_), channel_id=1, source_target_pairs={{0,2},{1,3},{2,0},{3,1},{4,6},{5,7},{6,4},{7,5},{8,10},{9,11},{10,... | collective-permute-start | bytes 1179656 | tf_op jit(solution)/shard_map/ppermute | solution.py:56
  47.3 20.8 %collective-permute-start.10 = (bf16[384,768]{1,0:T(8,128)(2,1)}, bf16[384,768]{1,0:T(8,128)(2,1)S(1)}, u32[]{:S(2)}, u32[]{:S(2)}) collective-permute-start(bf16[384,768]{1,0:T(8,128)(2,1)} %collective-permute-done.refs_6_.refs_9_.refs_7_), channel_id=1, source_target_pairs={{0,4},{4,0},{8,12},{12,8},{16,20},{20,16},{24,28},{28,24},{1,5},{5... | collective-permute-start | bytes 1769480 | tf_op jit(solution)/shard_map/ppermute | solution.py:56
  61.0 14.1 %collective-permute-start.15 = (bf16[256,768]{1,0:T(8,128)(2,1)S(1)}, bf16[256,768]{1,0:T(8,128)(2,1)S(1)}, u32[]{:S(2)}, u32[]{:S(2)}) collective-permute-start(bf16[256,768]{1,0:T(8,128)(2,1)S(1)} %get-tuple-element.329.refs_2_), channel_id=1, source_target_pairs={{0,2},{1,3},{2,0},{3,1},{4,6},{5,7},{6,4},{7,5},{8,10},{9,11},{10,... | collective-permute-start | bytes 1179656 | tf_op jit(solution)/shard_map/ppermute | solution.py:56
  77.4 15.2 %collective-permute-start.20 = (bf16[256,768]{1,0:T(8,128)(2,1)S(1)}, bf16[256,768]{1,0:T(8,128)(2,1)S(1)}, u32[]{:S(2)}, u32[]{:S(2)}) collective-permute-start(bf16[256,768]{1,0:T(8,128)(2,1)S(1)} %get-tuple-element.331.refs_2_), channel_id=1, source_target_pairs={{0,2},{1,3},{2,0},{3,1},{4,6},{5,7},{6,4},{7,5},{8,10},{9,11},{10,... | collective-permute-start | bytes 1179656 | tf_op jit(solution)/shard_map/ppermute | solution.py:56
  93.6 13.2 %collective-permute-start.25 = (bf16[256,768]{1,0:T(8,128)(2,1)S(1)}, bf16[256,768]{1,0:T(8,128)(2,1)S(1)}, u32[]{:S(2)}, u32[]{:S(2)}) collective-permute-start(bf16[256,768]{1,0:T(8,128)(2,1)S(1)} %get-tuple-element.346.refs_0_), channel_id=1, source_target_pairs={{0,2},{1,3},{2,0},{3,1},{4,6},{5,7},{6,4},{7,5},{8,10},{9,11},{10,... | collective-permute-start | bytes 1179656 | tf_op jit(solution)/shard_map/ppermute | solution.py:56
  144.2 27.5 %collective-permute-start.34 = (bf16[4,256,768]{2,1,0:T(8,128)(2,1)}, bf16[4,256,768]{2,1,0:T(8,128)(2,1)}, u32[]{:S(2)}, u32[]{:S(2)}) collective-permute-start(bf16[4,256,768]{2,1,0:T(8,128)(2,1)} %get-tuple-element.429.own_ref), channel_id=1, source_target_pairs={{0,1},{1,0},{2,3},{3,2},{4,5},{5,4},{6,7},{7,6},{8,9},{9,8},{10,11... | collective-permute-start | bytes 4718600 | tf_op jit(solution)/shard_map/ppermute | solution.py:56
  144.7 15.4 %collective-permute-start.32 = (bf16[256,768]{1,0:T(8,128)(2,1)}, bf16[256,768]{1,0:T(8,128)(2,1)S(1)}, u32[]{:S(2)}, u32[]{:S(2)}) collective-permute-start(bf16[256,768]{1,0:T(8,128)(2,1)} %get-tuple-element.434.refs_0_), channel_id=1, source_target_pairs={{0,1},{1,0},{2,3},{3,2},{4,5},{5,4},{6,7},{7,6},{8,9},{9,8},{10,11... | collective-permute-start | bytes 1179656 | tf_op jit(solution)/shard_map/ppermute | solution.py:56
  144.8 16.6 %collective-permute-start.33 = (bf16[256,768]{1,0:T(8,128)(2,1)S(1)}, bf16[256,768]{1,0:T(8,128)(2,1)S(1)}, u32[]{:S(2)}, u32[]{:S(2)}) collective-permute-start(bf16[256,768]{1,0:T(8,128)(2,1)S(1)} %get-tuple-element.420), channel_id=1, source_target_pairs={{0,1},{1,0},{2,3},{3,2},{4,5},{5,4},{6,7},{7,6},{8,9},{9,8},{10,11... | collective-permute-start | bytes 1179656 | tf_op jit(solution)/shard_map/ppermute | solution.py:56
  151.5 20.3 %collective-permute-start.36 = (bf16[4,96,768]{2,1,0:T(8,128)(2,1)}, bf16[4,96,768]{2,1,0:T(8,128)(2,1)}, u32[]{:S(2)}, u32[]{:S(2)}) collective-permute-start(bf16[4,96,768]{2,1,0:T(8,128)(2,1)} %get-tuple-element.432), channel_id=1, source_target_pairs={{0,4},{4,0},{8,12},{12,8},{16,20},{20,16},{24,28},{28,24},{1,5},{5... | collective-permute-start | bytes 1769480 | tf_op jit(solution)/shard_map/ppermute | solution.py:56
  152.2 17.7 %collective-permute-start.35 = (bf16[256,768]{1,0:T(8,128)(2,1)S(1)}, bf16[256,768]{1,0:T(8,128)(2,1)S(1)}, u32[]{:S(2)}, u32[]{:S(2)}) collective-permute-start(bf16[256,768]{1,0:T(8,128)(2,1)S(1)} %get-tuple-element.492.refs_0_), channel_id=1, source_target_pairs={{0,2},{1,3},{2,0},{3,1},{4,6},{5,7},{6,4},{7,5},{8,10},{9,11},{10,... | collective-permute-start | bytes 1179656 | tf_op jit(solution)/shard_map/ppermute | solution.py:56
  160.1 25.1 %collective-permute-start.40 = (bf16[4,96,768]{2,1,0:T(8,128)(2,1)}, bf16[4,96,768]{2,1,0:T(8,128)(2,1)S(1)}, u32[]{:S(2)}, u32[]{:S(2)}) collective-permute-start(bf16[4,96,768]{2,1,0:T(8,128)(2,1)} %get-tuple-element.454), channel_id=1, source_target_pairs={{0,4},{4,0},{8,12},{12,8},{16,20},{20,16},{24,28},{28,24},{1,5},{5... | collective-permute-start | bytes 1769480 | tf_op jit(solution)/shard_map/ppermute | solution.py:56
  170.7 14.5 %collective-permute-start.38 = (bf16[256,768]{1,0:T(8,128)(2,1)}, bf16[256,768]{1,0:T(8,128)(2,1)}, u32[]{:S(2)}, u32[]{:S(2)}) collective-permute-start(bf16[256,768]{1,0:T(8,128)(2,1)} %get-tuple-element.494.refs_3_), channel_id=1, source_target_pairs={{0,2},{1,3},{2,0},{3,1},{4,6},{5,7},{6,4},{7,5},{8,10},{9,11},{10,... | collective-permute-start | bytes 1179656 | tf_op jit(solution)/shard_map/ppermute | solution.py:56
  173.6 11.6 %collective-permute-start.39 = (bf16[2,96,768]{2,1,0:T(8,128)(2,1)}, bf16[2,96,768]{2,1,0:T(8,128)(2,1)S(1)}, u32[]{:S(2)}, u32[]{:S(2)}) collective-permute-start(bf16[2,96,768]{2,1,0:T(8,128)(2,1)} %get-tuple-element.452), channel_id=1, source_target_pairs={{0,8},{4,12},{8,0},{12,4},{16,24},{20,28},{24,16},{28,20},{1,9},{5... | collective-permute-start | bytes 884744 | tf_op jit(solution)/shard_map/ppermute | solution.py:56
  184.1 15.5 %collective-permute-start.43 = (bf16[256,768]{1,0:T(8,128)(2,1)}, bf16[256,768]{1,0:T(8,128)(2,1)}, u32[]{:S(2)}, u32[]{:S(2)}) collective-permute-start(bf16[256,768]{1,0:T(8,128)(2,1)} %get-tuple-element.496.refs_6_), channel_id=1, source_target_pairs={{0,2},{1,3},{2,0},{3,1},{4,6},{5,7},{6,4},{7,5},{8,10},{9,11},{10,... | collective-permute-start | bytes 1179656 | tf_op jit(solution)/shard_map/ppermute | solution.py:56
  185.3 12.9 %collective-permute-start.42 = (bf16[2,96,768]{2,1,0:T(8,128)(2,1)S(1)}, bf16[2,96,768]{2,1,0:T(8,128)(2,1)S(1)}, u32[]{:S(2)}, u32[]{:S(2)}) collective-permute-start(bf16[2,96,768]{2,1,0:T(8,128)(2,1)S(1)} %get-tuple-element.484), channel_id=1, source_target_pairs={{0,8},{4,12},{8,0},{12,4},{16,24},{20,28},{24,16},{28,20},{1,9},{5... | collective-permute-start | bytes 884744 | tf_op jit(solution)/shard_map/ppermute | solution.py:56
  207.9 29.7 %collective-permute-start.51 = (bf16[3,256,768]{2,1,0:T(8,128)(2,1)S(1)}, bf16[3,256,768]{2,1,0:T(8,128)(2,1)}, u32[]{:S(2)}, u32[]{:S(2)}) collective-permute-start(bf16[3,256,768]{2,1,0:T(8,128)(2,1)S(1)} %get-tuple-element.525.refs_0_), channel_id=1, source_target_pairs={{0,1},{1,0},{2,3},{3,2},{4,5},{5,4},{6,7},{7,6},{8,9},{9,8},{10,11... | collective-permute-start | bytes 3538952 | tf_op jit(solution)/shard_map/ppermute | solution.py:56
  208.5 15.6 %collective-permute-start.44 = (bf16[4,96,768]{2,1,0:T(8,128)(2,1)}, bf16[4,96,768]{2,1,0:T(8,128)(2,1)}, u32[]{:S(2)}, u32[]{:S(2)}) collective-permute-start(bf16[4,96,768]{2,1,0:T(8,128)(2,1)} %get-tuple-element.503), channel_id=1, source_target_pairs={{0,4},{4,0},{8,12},{12,8},{16,20},{20,16},{24,28},{28,24},{1,5},{5... | collective-permute-start | bytes 1769480 | tf_op jit(solution)/shard_map/ppermute | solution.py:56
  210.4 20.4 %collective-permute-start.49 = (bf16[256,768]{1,0:T(8,128)(2,1)}, bf16[256,768]{1,0:T(8,128)(2,1)S(1)}, u32[]{:S(2)}, u32[]{:S(2)}) collective-permute-start(bf16[256,768]{1,0:T(8,128)(2,1)} %get-tuple-element.521.refs_0_), channel_id=1, source_target_pairs={{0,2},{1,3},{2,0},{3,1},{4,6},{5,7},{6,4},{7,5},{8,10},{9,11},{10,... | collective-permute-start | bytes 1179656 | tf_op jit(solution)/shard_map/ppermute | solution.py:56
  211.4 14.2 %collective-permute-start.47 = (bf16[1,96,768]{2,1,0:T(8,128)(2,1)S(1)}, bf16[1,96,768]{2,1,0:T(8,128)(2,1)}, u32[]{:S(2)}, u32[]{:S(2)}) collective-permute-start(bf16[1,96,768]{2,1,0:T(8,128)(2,1)S(1)} %get-tuple-element.512), channel_id=1, source_target_pairs={{0,16},{4,20},{8,24},{12,28},{16,0},{20,4},{24,8},{28,12},{1,17},{... | collective-permute-start | bytes 442376 | tf_op jit(solution)/shard_map/ppermute | solution.py:56
  236.1 14.2 %collective-permute-start.53 = (bf16[128,768]{1,0:T(8,128)(2,1)S(1)}, bf16[128,768]{1,0:T(8,128)(2,1)S(1)}, u32[]{:S(2)}, u32[]{:S(2)}) collective-permute-start(bf16[128,768]{1,0:T(8,128)(2,1)S(1)} %get-tuple-element.530), channel_id=1, source_target_pairs={{0,16},{4,20},{8,24},{12,28},{16,0},{20,4},{24,8},{28,12},{1,17},{... | collective-permute-start | bytes 589832 | tf_op jit(solution)/shard_map/ppermute | solution.py:56
  236.6 18.9 %collective-permute-start.54 = (bf16[128,768]{1,0:T(8,128)(2,1)S(1)}, bf16[128,768]{1,0:T(8,128)(2,1)S(1)}, u32[]{:S(2)}, u32[]{:S(2)}) collective-permute-start(bf16[128,768]{1,0:T(8,128)(2,1)S(1)} %get-tuple-element.531), channel_id=1, source_target_pairs={{0,24},{4,28},{8,16},{12,20},{16,8},{20,12},{24,0},{28,4},{1,25},{... | collective-permute-start | bytes 589832 | tf_op jit(solution)/shard_map/ppermute | solution.py:56
  (70 other events, 478.0 us)

commit v2 on v1

--- a/solution.py
+++ b/solution.py
@@ -218,45 +218,44 @@
     )(place, pieces, gain, weight, rows, normed, joined)
 
 
-def look_up_kernel(ids_ref, table_any, placed_ref, out_ref, blocks_ref, total_ref, sems):
+def look_up_kernel(ids_ref, table_any, target_ref, placed_ref, out_ref, blocks_ref, sems):
     part = out_ref.shape[0]
     limit = table_any.shape[0]
-    copies, inside = [], []
-    for row in range(part):
-        local = jnp.clip(ids_ref[row], 0, limit - 1)
-        inside.append(local)
-        start = pl.multiple_of(jnp.left_shift(jnp.right_shift(local, 4), 4), 16)
-        copies.append(
-            pltpu.make_async_copy(table_any.at[pl.ds(start, 16)], blocks_ref.at[row], sems.at[row])
-        )
-    for copy in copies:
-        copy.start()
-    for copy in copies:
-        copy.wait()
-    position = lax.broadcasted_iota(jnp.int32, blocks_ref.shape[1:], 0)
-    for row in range(part):
-        own = inside[row] == ids_ref[row]
-        chosen = (position == jnp.bitwise_and(inside[row], 15)) & own
-        found = jnp.sum(jnp.where(chosen, blocks_ref[row].astype(wide), 0.0), axis=0, keepdims=True)
-        total_ref[row : row + 1, :] = placed_ref[row : row + 1, :] + found
-    out_ref[...] = total_ref[...].astype(low)
+
+    def each(act):
+        for row in range(part):
+            local = ids_ref[row]
+
+            @pl.when((local >= 0) & (local < limit))
+            def _():
+                start = pl.multiple_of(jnp.left_shift(jnp.right_shift(local, 4), 4), 16)
+                act(
+                    pltpu.make_async_copy(
+                        table_any.at[pl.ds(start, 16)], blocks_ref.at[pl.ds(16 * row, 16)], sems.at[row]
+                    )
+                )
+
+    blocks_ref[...] = jnp.zeros(blocks_ref.shape, low)
+    each(lambda copy: copy.start())
+    position = lax.broadcasted_iota(jnp.int32, (part, 16 * part), 1)
+    chosen = jnp.where(position == target_ref[...], 1.0, 0.0).astype(low)
+    each(lambda copy: copy.wait())
+    out_ref[...] = (nn(chosen, blocks_ref[...]) + placed_ref[...]).astype(low)
 
 
 def look_up_rows(ids, table, placed):
     part, model = placed.shape
     inside = pl.BlockSpec(memory_space=pltpu.VMEM)
+    own = (ids >= 0) & (ids < table.shape[0])
+    target = jnp.where(own, 16 * jnp.arange(part, dtype=jnp.int32) + ids % 16, -1)[:, None]
     return kernel_call(
         look_up_kernel, 2.5,
-        in_specs=[pl.BlockSpec(memory_space=pltpu.SMEM), pl.BlockSpec(memory_space=pl.ANY), inside],
+        in_specs=[pl.BlockSpec(memory_space=pltpu.SMEM), pl.BlockSpec(memory_space=pl.ANY), inside, inside],
         out_specs=inside,
         out_shape=jax.ShapeDtypeStruct((part, model), low),
-        scratch_shapes=[
-            pltpu.VMEM((part, 16, model), low),
-            pltpu.VMEM((part, model), wide),
-            pltpu.SemaphoreType.DMA((part,)),
-        ],
+        scratch_shapes=[pltpu.VMEM((16 * part, model), low), pltpu.SemaphoreType.DMA((part,))],
         name="look_up",
-    )(ids, table, placed)
+    )(ids, table, target, placed)
 
 
 def attention_step_kernel(
@@ -1321,7 +1320,7 @@
     rel_share = jnp.einsum("ht,tb->bh", line[:, 0, :], turned, precision=highest)
     place, rel_share, tail.parts, small.got = tie(place, rel_share, tail.parts, small.got)
     small.join(tail, rel_share)
-    place, small.parts[0], inner.parts, outer.parts = tie(place, small.parts[0], inner.parts, outer.parts)
+    place, inner.parts, outer.parts = tie(place, inner.parts, outer.parts)
     whole_width = ((0, w_inner.shape[1], False),)
     (inner_grad,), (outer_grad,) = inner.end(whole_width), outer.end(whole_width)
     place, inner_grad, outer_grad = tie(place, inner_grad, outer_grad)

time: 268 us -> 259 us (0.966)
  Pallas kernels: 170 us -> 162 us
  local copies, waits for them, and re-layouts: 13.7 us -> 9.66 us
  waiting for transfers between devices: 35.7 us -> 38.9 us
    pallas_call x34, Pallas kernels: 170 us -> 162 us  [run(): call(*[pltpu.with_memory_space_constraint(v, pltpu.HBM) if (v.size >= lea...]
    unnamed x77 -> x63, local copies, waits for them, and re-layouts: 7.67 us -> 3.5 us
    ppermute x56, waiting for transfers between devices: 35.7 us -> 38.9 us  [swap(): return lax.ppermute(value, axis, [(i, i ^ bit) for i in range(count)])]
  transfers between devices with their start and end apart: 56 -> 56, of which waited for: 14 -> 15; matrix products, arithmetic and copies ran while one was open for 3% -> 3% of each run, Pallas kernels for 55% -> 55%
where the time goes in v2:
time: 259 us; the launch traced here: 255 us
  Pallas kernels  162 us (63%)
  starting transfers between devices  39.4 us (15%)
  waiting for transfers between devices  38.9 us (15%)
  local copies, waits for them, and re-layouts  9.66 us (4%)
    pallas_call x34, Pallas kernels, run(): call(*[pltpu.with_memory_space_constraint(v, pltpu.HBM) if (v.size >= lea...  162 us
    ppermute x56, starting transfers between devices, swap(): return lax.ppermute(value, axis, [(i, i ^ bit) for i in range(count)])  39.4 us
    ppermute x56, waiting for transfers between devices, swap(): return lax.ppermute(value, axis, [(i, i ^ bit) for i in range(count)])  38.9 us
  transfers between devices with their start and end apart: 56, of which 15 were waited for; matrix products, arithmetic and copies ran while one was open for 3% of the time, Pallas kernels for 55%

profile of v2, /device:TPU:8, one launch (start us, length us, event | category | flops | bytes accessed | tf_op | source)
XLA Modules:
  0.0 254.7 jit_solution(10943008075051284689)
XLA Ops:
  15.1 4.2 %text_projections.2 = (bf16[4,512,768]{2,1,0:T(8,128)(2,1)}, bf16[4,512,768]{2,1,0:T(8,128)(2,1)}, bf16[4,512,576]{2,1,0:T(8,128)(2,1)}) custom-call(bf16[4,412,768]{2,1,0:T(8,128)(2,1)} %copy.81.tokens_ref, f32[1,768]{1,0:T(1,128)S(1)} %broadcast_in_dim.31.gain_ref.refs_11_.refs_5_, bf16[576,768]{1,0:T(8,128)(2,1)} %pad_maximum_fusion.weight_ref.refs_6_.refs_0_), custom_call_target="tpu_custom_call" | custom-call | bytes 8640000 | tf_op jit(solution)/shard_map/text_projections/pallas_call | solution.py:44
  21.9 4.4 %text_projections.3 = (bf16[4,512,768]{2,1,0:T(8,128)(2,1)}, bf16[4,512,768]{2,1,0:T(8,128)(2,1)}, bf16[4,512,576]{2,1,0:T(8,128)(2,1)}) custom-call(bf16[4,412,768]{2,1,0:T(8,128)(2,1)} %copy.81.tokens_ref, f32[1,768]{1,0:T(1,128)S(1)} %broadcast_in_dim.31.gain_ref.refs_11_.refs_5_, ...), custom_call_target="tpu_custom_call", output_to_operand_aliasing={{0}: (3, {}), {1}: (4, {}), {2}: (5, {})} | custom-call | bytes 8640000 | tf_op jit(solution)/shard_map/text_projections/pallas_call | solution.py:44
  37.4 5.6 %attention_step.6 = (bf16[256,768]{1,0:T(8,128)(2,1)S(1)}, bf16[256,768]{1,0:T(8,128)(2,1)S(1)}, bf16[1,3,256,512]{3,2,1,0:T(8,128)(2,1)}, bf16[1,3,256,512]{3,2,1,0:T(8,128)(2,1)}, bf16[4,512,192]{2,1,0:T(8,128)(2,1)}) custom-call(s32[3]{0:T(128)S(1)} %pad_add_fusion.core_ref.place_ref, ...), custom_call_target="tpu_custom_call", output_to_operand_aliasing={{4}: (7, {})} | custom-call | bytes 18000000 | tf_op jit(solution)/shard_map/attention_step/pallas_call | solution.py:44
  45.4 6.9 %collective-permute-done.7.refs_5_.refs_8_.refs_6_ = bf16[384,768]{1,0:T(8,128)(2,1)S(1)} collective-permute-done((bf16[384,768]{1,0:T(8,128)(2,1)}, bf16[384,768]{1,0:T(8,128)(2,1)S(1)}, u32[]{:S(2)}, u32[]{:S(2)}) %collective-permute-start.7) | collective-permute-done | bytes 589856 | tf_op jit(solution)/shard_map/ppermute | solution.py:56
  52.2 5.6 %attention_step.7 = (bf16[256,768]{1,0:T(8,128)(2,1)S(1)}, bf16[256,768]{1,0:T(8,128)(2,1)S(1)}, bf16[1,3,256,512]{3,2,1,0:T(8,128)(2,1)}, bf16[1,3,256,512]{3,2,1,0:T(8,128)(2,1)}, bf16[4,512,192]{2,1,0:T(8,128)(2,1)}) custom-call(s32[3]{0:T(128)S(1)} %pad_add_fusion.core_ref.place_ref, ...), custom_call_target="tpu_custom_call", output_to_operand_aliasing={{4}: (7, {})} | custom-call | bytes 18000000 | tf_op jit(solution)/shard_map/attention_step/pallas_call | solution.py:44
  60.0 5.6 %attention_step.8 = (bf16[256,768]{1,0:T(8,128)(2,1)S(1)}, bf16[256,768]{1,0:T(8,128)(2,1)S(1)}, bf16[1,3,256,512]{3,2,1,0:T(8,128)(2,1)}, bf16[1,3,256,512]{3,2,1,0:T(8,128)(2,1)}, bf16[4,512,192]{2,1,0:T(8,128)(2,1)}) custom-call(s32[3]{0:T(128)S(1)} %pad_add_fusion.core_ref.place_ref, ...), custom_call_target="tpu_custom_call", output_to_operand_aliasing={{4}: (7, {})} | custom-call | bytes 18000000 | tf_op jit(solution)/shard_map/attention_step/pallas_call | solution.py:44
  65.6 6.3 %feed_step.5 = (bf16[4,512,768]{2,1,0:T(8,128)(2,1)}, bf16[4,512,768]{2,1,0:T(8,128)(2,1)}, bf16[4,512,768]{2,1,0:T(8,128)(2,1)}, bf16[512,768]{1,0:T(8,128)(2,1)S(1)}) custom-call(s32[3]{0:T(128)S(1)} %pad_add_fusion.core_ref.place_ref, bf16[4,512,768]{2,1,0:T(8,128)(2,1)} %get-tuple-element.317.rows_any.refs_9_.refs_3_, bf16[4,512,768]{2,1,0:T(8,128)(2,1)} %cot_any.9, ...), custom_call_target="tpu_custom_call" | custom-call | bytes 28800000 | tf_op jit(solution)/shard_map/feed_step/pallas_call | solution.py:44
  79.9 10.1 %feed_step.6 = (bf16[4,512,768]{2,1,0:T(8,128)(2,1)}, bf16[4,512,768]{2,1,0:T(8,128)(2,1)}, bf16[4,512,768]{2,1,0:T(8,128)(2,1)}, bf16[512,768]{1,0:T(8,128)(2,1...) custom-call(s32[3]{0:T(128)S(1)} %pad_add_fusion.core_ref.place_ref,, ...), custom_call_target="tpu_custom_call", output_to_operand_aliasing={{0}: (15, {}), {1}: (16, {}), {2}: (17, {})} | custom-call | bytes 43200000 | tf_op jit(solution)/shard_map/feed_step/pallas_call | solution.py:44
  94.0 10.0 %feed_step.7 = (bf16[4,512,768]{2,1,0:T(8,128)(2,1)}, bf16[4,512,768]{2,1,0:T(8,128)(2,1)}, bf16[4,512,768]{2,1,0:T(8,128)(2,1)}, bf16[512,768]{1,0:T(8,128)(2,1...) custom-call(s32[3]{0:T(128)S(1)} %pad_add_fusion.core_ref.place_ref,, ...), custom_call_target="tpu_custom_call", output_to_operand_aliasing={{0}: (15, {}), {1}: (16, {}), {2}: (17, {}), {7}: (18, {})} | custom-call | bytes 43200000 | tf_op jit(solution)/shard_map/feed_step/pallas_call | solution.py:44
  104.8 7.7 %attention_back_step.5 = (bf16[256,768]{1,0:T(8,128)(2,1)S(1)}, bf16[256,576]{1,0:T(8,128)(2,1)}, bf16[4,512,576]{2,1,0:T(8,128)(2,1)}, bf16[4,3,512,512]{3,2,1,0:T(8,128)(2,1)}, bf16[4,512,768]{2,1,0:T(8,128)(2,1)}) custom-call(s32[3]{0:T(128)S(1)} %pad_add_fusion.core_ref.place_ref, bf16[256,768]{1,0:T(8,128)(2,1)S(1)} %get-tuple-element.357.refs_0_, ...), custom_call_target="tpu_custom_call" | custom-call | bytes 21600000 | tf_op jit(solution)/shard_map/attention_back_step/pallas_call | solution.py:44
  112.5 10.0 %feed_step.8 = (bf16[4,512,768]{2,1,0:T(8,128)(2,1)}, bf16[4,512,768]{2,1,0:T(8,128)(2,1)}, bf16[4,512,768]{2,1,0:T(8,128)(2,1)}, bf16[512,768]{1,0:T(8,128)(2,1...) custom-call(s32[3]{0:T(128)S(1)} %pad_add_fusion.core_ref.place_ref,, ...), custom_call_target="tpu_custom_call", output_to_operand_aliasing={{0}: (15, {}), {1}: (16, {}), {2}: (17, {}), {7}: (18, {})} | custom-call | bytes 43200000 | tf_op jit(solution)/shard_map/feed_step/pallas_call | solution.py:44
  125.5 8.3 %attention_back_step.6 = (bf16[256,768]{1,0:T(8,128)(2,1)S(1)}, f32[1,768]{1,0:T(1,128)S(1)}, f32[128,768]{1,0:T(8,128)}, bf16[256,768]{1,0:T(8,128)(2,1)S(1)}, ...) custom-call(s32[3]{0:T(128)S(1)} %pad_add_fusion.core_ref.place_ref,, ...), custom_call_target="tpu_custom_call", output_to_operand_aliasing={{5}: (15, {}), {6}: (16, {}), {7}: (17, {})} | custom-call | bytes 21600000 | tf_op jit(solution)/shard_map/attention_back_step/pallas_call | solution.py:44
  133.8 7.6 %feed_step.9 = (bf16[4,512,768]{2,1,0:T(8,128)(2,1)}, bf16[4,512,768]{2,1,0:T(8,128)(2,1)}, bf16[4,512,768]{2,1,0:T(8,128)(2,1)}, f32[256,768]{1,0:T(8,128)}, bf...) custom-call(s32[3]{0:T(128)S(1)} %pad_add_fusion.core_ref.place_ref,, ...), custom_call_target="tpu_custom_call", output_to_operand_aliasing={{0}: (13, {}), {1}: (14, {}), {2}: (15, {}), {6}: (16, {})} | custom-call | bytes 28800000 | tf_op jit(solution)/shard_map/feed_step/pallas_call | solution.py:44
  142.3 6.3 %weight_shares.3 = (bf16[4,96,768]{2,1,0:T(8,128)(2,1)S(1)}, bf16[4,96,768]{2,1,0:T(8,128)(2,1)}) custom-call(s32[1]{0:T(128)} %bitcast.where_ref, bf16[2048,768]{1,0:T(8,128)(2,1)} %bitcast.45, bf16[2048,768]{1,0:T(8,128)(2,1)} %bitcast.47), custom_call_target="tpu_custom_call" | custom-call | bytes 21600000 | tf_op jit(solution)/shard_map/weight_shares/pallas_call | solution.py:44
  150.2 6.6 %weight_shares.4 = (bf16[4,96,768]{2,1,0:T(8,128)(2,1)S(1)}, bf16[4,96,768]{2,1,0:T(8,128)(2,1)}) custom-call(s32[1]{0:T(128)} %bitcast.where_ref, bf16[2048,768]{1,0:T(8,128)(2,1)} %bitcast.44, bf16[2048,768]{1,0:T(8,128)(2,1)} %bitcast.46), custom_call_target="tpu_custom_call" | custom-call | bytes 21600000 | tf_op jit(solution)/shard_map/weight_shares/pallas_call | solution.py:44
  158.3 8.4 %attention_back_step.7 = (bf16[256,768]{1,0:T(8,128)(2,1)}, f32[1,768]{1,0:T(1,128)S(1)}, f32[128,768]{1,0:T(8,128)}, bf16[256,768]{1,0:T(8,128)(2,1)}, bf16[256...) custom-call(s32[3]{0:T(128)S(1)} %pad_add_fusion.core_ref.place_ref,, ...), custom_call_target="tpu_custom_call", output_to_operand_aliasing={{5}: (15, {}), {6}: (16, {}), {7}: (17, {})} | custom-call | bytes 21600000 | tf_op jit(solution)/shard_map/attention_back_step/pallas_call | solution.py:44
  172.8 9.0 %attention_back_step.8 = (bf16[256,768]{1,0:T(8,128)(2,1)S(1)}, f32[1,768]{1,0:T(1,128)S(1)}, f32[128,768]{1,0:T(8,128)}, bf16[256,768]{1,0:T(8,128)(2,1)}, bf16...) custom-call(s32[3]{0:T(128)S(1)} %pad_add_fusion.core_ref.place_ref,, ...), custom_call_target="tpu_custom_call", output_to_operand_aliasing={{5}: (15, {}), {6}: (16, {}), {7}: (17, {})} | custom-call | bytes 21600000 | tf_op jit(solution)/shard_map/attention_back_step/pallas_call | solution.py:44
  184.7 7.2 %weight_shares.5 = (bf16[4,96,768]{2,1,0:T(8,128)(2,1)S(1)}, bf16[4,96,768]{2,1,0:T(8,128)(2,1)S(1)}) custom-call(s32[1]{0:T(128)} %bitcast.where_ref, bf16[2048,768]{1,0:T(8,128)(2,1)} %bitcast.52, bf16[2048,576]{1,0:T(8,128)(2,1)} %bitcast.49, bf16[2048,768]{1,0:T(8,128)(2,1)} %bitcast.48, bf16[2048,192]{1,0:T(8,128)(2,1)S(1)} %bitcast.43), custom_call_target="tpu_custom_call" | custom-call | bytes 21600000 | tf_op jit(solution)/shard_map/weight_shares/pallas_call | solution.py:44
  195.1 8.2 %middle_work.1 = (f32[3,1,1024]{2,1,0:T(1,128)S(1)}, bf16[3,256,768]{2,1,0:T(8,128)(2,1)S(1)}, bf16[4,512,768]{2,1,0:T(8,128)(2,1)}) custom-call(s32[3]{0:T(128)S(1)} %pad_add_fusion.core_ref.place_ref, bf16[4,3,512,512]{3,2,1,0:T(8,128)(2,1)} %get-tuple-element.489.scores_any, bf16[4,512,768]{2,1,0:T(8,128)(2,1)} %get-tuple-element.317.rows_any.refs_9_.refs_3_, ...), custom_call_target="tpu_custom_call" | custom-call | bytes 43200000 | tf_op jit(solution)/shard_map/middle_work/pallas_call | solution.py:44
  208.5 3.9 %collective-permute-done.46.near_ref = bf16[4,32,768]{2,1,0:T(8,128)(2,1)S(1)} collective-permute-done((bf16[4,32,768]{2,1,0:T(8,128)(2,1)S(1)}, bf16[4,32,768]{2,1,0:T(8,128)(2,1)S(1)}, u32[]{:S(2)}, u32[]{:S(2)}) %collective-permute-start.46) | collective-permute-done | bytes 196640 | tf_op jit(solution)/shard_map/ppermute | solution.py:56
  214.5 4.7 %collective-permute-done.44.got_ref = bf16[4,96,768]{2,1,0:T(8,128)(2,1)S(1)} collective-permute-done((bf16[4,96,768]{2,1,0:T(8,128)(2,1)S(1)}, bf16[4,96,768]{2,1,0:T(8,128)(2,1)S(1)}, u32[]{:S(2)}, u32[]{:S(2)}) %collective-permute-start.44) | collective-permute-done | bytes 589856 | tf_op jit(solution)/shard_map/ppermute | solution.py:56
  229.2 5.6 %weave_halves.1 = bf16[412,4,768]{2,1,0:T(4,128)(2,1)} custom-call(s32[3]{0:T(128)S(1)} %pad_add_fusion.core_ref.place_ref, bf16[3,256,768]{2,1,0:T(8,128)(2,1)} %copy-done.9, bf16[3,256,768]{2,1,0:T(8,128)(2,1)} %collective-permute-done.51.refs_1_, bf16[1,256,768]{2,1,0:T(8,128)(2,1)} %copy-done.8, bf16[1,256,768]{2,1,0:T(8,128)(2,1)} %collective-permute-done.50.refs_3_), custom_call_target="tpu_custom_call" | custom-call | bytes 14400000 | tf_op jit(solution)/shard_map/weave_halves/pallas_call | solution.py:44
  235.8 6.0 %collective-permute-done.53.refs_2_ = bf16[128,768]{1,0:T(8,128)(2,1)S(1)} collective-permute-done((bf16[128,768]{1,0:T(8,128)(2,1)S(1)}, bf16[128,768]{1,0:T(8,128)(2,1)S(1)}, u32[]{:S(2)}, u32[]{:S(2)}) %collective-permute-start.53) | collective-permute-done | bytes 196640 | tf_op jit(solution)/shard_map/ppermute | solution.py:56
  241.8 5.4 %collective-permute-done.54.refs_3_ = bf16[128,768]{1,0:T(8,128)(2,1)S(1)} collective-permute-done((bf16[128,768]{1,0:T(8,128)(2,1)S(1)}, bf16[128,768]{1,0:T(8,128)(2,1)S(1)}, u32[]{:S(2)}, u32[]{:S(2)}) %collective-permute-start.54) | collective-permute-done | bytes 196640 | tf_op jit(solution)/shard_map/ppermute | solution.py:56
  (223 shorter events, 89.1 us)
Async XLA Ops:
  7.6 18.8 %collective-permute-start.4 = (bf16[384,768]{1,0:T(8,128)(2,1)}, bf16[384,768]{1,0:T(8,128)(2,1)}, u32[]{:S(2)}, u32[]{:S(2)}) collective-permute-start(bf16[384,768]{1,0:T(8,128)(2,1)} %dynamic-slice_bitcast_fusion), channel_id=1, source_target_pairs={{0,2},{1,3},{2,0},{3,1},{4,6},{5,7},{6,4},{7,5},{8,10},{9,11},{10,... | collective-permute-start | bytes 1769480 | tf_op jit(solution)/shard_map/ppermute | solution.py:56
  9.9 25.7 %collective-permute-start = (bf16[384,768]{1,0:T(8,128)(2,1)}, bf16[384,768]{1,0:T(8,128)(2,1)}, u32[]{:S(2)}, u32[]{:S(2)}) collective-permute-start(bf16[384,768]{1,0:T(8,128)(2,1)} %dynamic-slice_bitcast_fusion.1), channel_id=1, source_target_pairs={{0,2},{1,3},{2,0},{3,1},{4,6},{5,7},{6,4},{7,5},{8,10},{9,11},{10,... | collective-permute-start | bytes 1769480 | tf_op jit(solution)/shard_map/ppermute | solution.py:56
  35.9 16.4 %collective-permute-start.7 = (bf16[384,768]{1,0:T(8,128)(2,1)}, bf16[384,768]{1,0:T(8,128)(2,1)S(1)}, u32[]{:S(2)}, u32[]{:S(2)}) collective-permute-start(bf16[384,768]{1,0:T(8,128)(2,1)} %collective-permute-done.4.refs_4_.refs_7_.refs_5_), channel_id=1, source_target_pairs={{0,4},{4,0},{8,12},{12,8},{16,20},{20,16},{24,28},{28,24},{1,5},{5... | collective-permute-start | bytes 1769480 | tf_op jit(solution)/shard_map/ppermute | solution.py:56
  43.2 15.2 %collective-permute-start.11 = (bf16[256,768]{1,0:T(8,128)(2,1)S(1)}, bf16[256,768]{1,0:T(8,128)(2,1)S(1)}, u32[]{:S(2)}, u32[]{:S(2)}) collective-permute-start(bf16[256,768]{1,0:T(8,128)(2,1)S(1)} %get-tuple-element.315.refs_2_), channel_id=1, source_target_pairs={{0,2},{1,3},{2,0},{3,1},{4,6},{5,7},{6,4},{7,5},{8,10},{9,11},{10,... | collective-permute-start | bytes 1179656 | tf_op jit(solution)/shard_map/ppermute | solution.py:56
  44.7 20.8 %collective-permute-start.10 = (bf16[384,768]{1,0:T(8,128)(2,1)}, bf16[384,768]{1,0:T(8,128)(2,1)S(1)}, u32[]{:S(2)}, u32[]{:S(2)}) collective-permute-start(bf16[384,768]{1,0:T(8,128)(2,1)} %collective-permute-done.refs_6_.refs_9_.refs_7_), channel_id=1, source_target_pairs={{0,4},{4,0},{8,12},{12,8},{16,20},{20,16},{24,28},{28,24},{1,5},{5... | collective-permute-start | bytes 1769480 | tf_op jit(solution)/shard_map/ppermute | solution.py:56
  58.5 14.1 %collective-permute-start.15 = (bf16[256,768]{1,0:T(8,128)(2,1)S(1)}, bf16[256,768]{1,0:T(8,128)(2,1)S(1)}, u32[]{:S(2)}, u32[]{:S(2)}) collective-permute-start(bf16[256,768]{1,0:T(8,128)(2,1)S(1)} %get-tuple-element.328.refs_2_), channel_id=1, source_target_pairs={{0,2},{1,3},{2,0},{3,1},{4,6},{5,7},{6,4},{7,5},{8,10},{9,11},{10,... | collective-permute-start | bytes 1179656 | tf_op jit(solution)/shard_map/ppermute | solution.py:56
  74.8 15.2 %collective-permute-start.20 = (bf16[256,768]{1,0:T(8,128)(2,1)S(1)}, bf16[256,768]{1,0:T(8,128)(2,1)S(1)}, u32[]{:S(2)}, u32[]{:S(2)}) collective-permute-start(bf16[256,768]{1,0:T(8,128)(2,1)S(1)} %get-tuple-element.330.refs_2_), channel_id=1, source_target_pairs={{0,2},{1,3},{2,0},{3,1},{4,6},{5,7},{6,4},{7,5},{8,10},{9,11},{10,... | collective-permute-start | bytes 1179656 | tf_op jit(solution)/shard_map/ppermute | solution.py:56
  91.1 13.2 %collective-permute-start.25 = (bf16[256,768]{1,0:T(8,128)(2,1)S(1)}, bf16[256,768]{1,0:T(8,128)(2,1)S(1)}, u32[]{:S(2)}, u32[]{:S(2)}) collective-permute-start(bf16[256,768]{1,0:T(8,128)(2,1)S(1)} %get-tuple-element.345.refs_0_), channel_id=1, source_target_pairs={{0,2},{1,3},{2,0},{3,1},{4,6},{5,7},{6,4},{7,5},{8,10},{9,11},{10,... | collective-permute-start | bytes 1179656 | tf_op jit(solution)/shard_map/ppermute | solution.py:56
  141.4 27.2 %collective-permute-start.34 = (bf16[4,256,768]{2,1,0:T(8,128)(2,1)}, bf16[4,256,768]{2,1,0:T(8,128)(2,1)}, u32[]{:S(2)}, u32[]{:S(2)}) collective-permute-start(bf16[4,256,768]{2,1,0:T(8,128)(2,1)} %get-tuple-element.428.own_ref), channel_id=1, source_target_pairs={{0,1},{1,0},{2,3},{3,2},{4,5},{5,4},{6,7},{7,6},{8,9},{9,8},{10,11... | collective-permute-start | bytes 4718600 | tf_op jit(solution)/shard_map/ppermute | solution.py:56
  141.8 15.0 %collective-permute-start.32 = (bf16[256,768]{1,0:T(8,128)(2,1)}, bf16[256,768]{1,0:T(8,128)(2,1)}, u32[]{:S(2)}, u32[]{:S(2)}) collective-permute-start(bf16[256,768]{1,0:T(8,128)(2,1)} %get-tuple-element.433.refs_0_), channel_id=1, source_target_pairs={{0,1},{1,0},{2,3},{3,2},{4,5},{5,4},{6,7},{7,6},{8,9},{9,8},{10,11... | collective-permute-start | bytes 1179656 | tf_op jit(solution)/shard_map/ppermute | solution.py:56
  142.0 16.3 %collective-permute-start.33 = (bf16[256,768]{1,0:T(8,128)(2,1)S(1)}, bf16[256,768]{1,0:T(8,128)(2,1)S(1)}, u32[]{:S(2)}, u32[]{:S(2)}) collective-permute-start(bf16[256,768]{1,0:T(8,128)(2,1)S(1)} %get-tuple-element.419), channel_id=1, source_target_pairs={{0,1},{1,0},{2,3},{3,2},{4,5},{5,4},{6,7},{7,6},{8,9},{9,8},{10,11... | collective-permute-start | bytes 1179656 | tf_op jit(solution)/shard_map/ppermute | solution.py:56
  148.6 20.0 %collective-permute-start.36 = (bf16[4,96,768]{2,1,0:T(8,128)(2,1)}, bf16[4,96,768]{2,1,0:T(8,128)(2,1)}, u32[]{:S(2)}, u32[]{:S(2)}) collective-permute-start(bf16[4,96,768]{2,1,0:T(8,128)(2,1)} %get-tuple-element.431), channel_id=1, source_target_pairs={{0,4},{4,0},{8,12},{12,8},{16,20},{20,16},{24,28},{28,24},{1,5},{5... | collective-permute-start | bytes 1769480 | tf_op jit(solution)/shard_map/ppermute | solution.py:56
  149.2 17.5 %collective-permute-start.35 = (bf16[256,768]{1,0:T(8,128)(2,1)S(1)}, bf16[256,768]{1,0:T(8,128)(2,1)S(1)}, u32[]{:S(2)}, u32[]{:S(2)}) collective-permute-start(bf16[256,768]{1,0:T(8,128)(2,1)S(1)} %get-tuple-element.491.refs_0_), channel_id=1, source_target_pairs={{0,2},{1,3},{2,0},{3,1},{4,6},{5,7},{6,4},{7,5},{8,10},{9,11},{10,... | collective-permute-start | bytes 1179656 | tf_op jit(solution)/shard_map/ppermute | solution.py:56
  156.8 26.1 %collective-permute-start.40 = (bf16[4,96,768]{2,1,0:T(8,128)(2,1)}, bf16[4,96,768]{2,1,0:T(8,128)(2,1)S(1)}, u32[]{:S(2)}, u32[]{:S(2)}) collective-permute-start(bf16[4,96,768]{2,1,0:T(8,128)(2,1)} %get-tuple-element.453), channel_id=1, source_target_pairs={{0,4},{4,0},{8,12},{12,8},{16,20},{20,16},{24,28},{28,24},{1,5},{5... | collective-permute-start | bytes 1769480 | tf_op jit(solution)/shard_map/ppermute | solution.py:56
  167.5 15.4 %collective-permute-start.38 = (bf16[256,768]{1,0:T(8,128)(2,1)}, bf16[256,768]{1,0:T(8,128)(2,1)}, u32[]{:S(2)}, u32[]{:S(2)}) collective-permute-start(bf16[256,768]{1,0:T(8,128)(2,1)} %get-tuple-element.493.refs_3_), channel_id=1, source_target_pairs={{0,2},{1,3},{2,0},{3,1},{4,6},{5,7},{6,4},{7,5},{8,10},{9,11},{10,... | collective-permute-start | bytes 1179656 | tf_op jit(solution)/shard_map/ppermute | solution.py:56
  170.5 12.4 %collective-permute-start.39 = (bf16[2,96,768]{2,1,0:T(8,128)(2,1)}, bf16[2,96,768]{2,1,0:T(8,128)(2,1)}, u32[]{:S(2)}, u32[]{:S(2)}) collective-permute-start(bf16[2,96,768]{2,1,0:T(8,128)(2,1)} %get-tuple-element.451), channel_id=1, source_target_pairs={{0,8},{4,12},{8,0},{12,4},{16,24},{20,28},{24,16},{28,20},{1,9},{5... | collective-permute-start | bytes 884744 | tf_op jit(solution)/shard_map/ppermute | solution.py:56
  181.9 13.2 %collective-permute-start.43 = (bf16[256,768]{1,0:T(8,128)(2,1)S(1)}, bf16[256,768]{1,0:T(8,128)(2,1)}, u32[]{:S(2)}, u32[]{:S(2)}) collective-permute-start(bf16[256,768]{1,0:T(8,128)(2,1)S(1)} %get-tuple-element.495.refs_6_), channel_id=1, source_target_pairs={{0,2},{1,3},{2,0},{3,1},{4,6},{5,7},{6,4},{7,5},{8,10},{9,11},{10,... | collective-permute-start | bytes 1179656 | tf_op jit(solution)/shard_map/ppermute | solution.py:56
  183.1 12.0 %collective-permute-start.42 = (bf16[2,96,768]{2,1,0:T(8,128)(2,1)S(1)}, bf16[2,96,768]{2,1,0:T(8,128)(2,1)S(1)}, u32[]{:S(2)}, u32[]{:S(2)}) collective-permute-start(bf16[2,96,768]{2,1,0:T(8,128)(2,1)S(1)} %get-tuple-element.483), channel_id=1, source_target_pairs={{0,8},{4,12},{8,0},{12,4},{16,24},{20,28},{24,16},{28,20},{1,9},{5... | collective-permute-start | bytes 884744 | tf_op jit(solution)/shard_map/ppermute | solution.py:56
  203.3 25.8 %collective-permute-start.51 = (bf16[3,256,768]{2,1,0:T(8,128)(2,1)S(1)}, bf16[3,256,768]{2,1,0:T(8,128)(2,1)}, u32[]{:S(2)}, u32[]{:S(2)}) collective-permute-start(bf16[3,256,768]{2,1,0:T(8,128)(2,1)S(1)} %get-tuple-element.519.refs_0_), channel_id=1, source_target_pairs={{0,1},{1,0},{2,3},{3,2},{4,5},{5,4},{6,7},{7,6},{8,9},{9,8},{10,11... | collective-permute-start | bytes 3538952 | tf_op jit(solution)/shard_map/ppermute | solution.py:56
  203.9 15.3 %collective-permute-start.44 = (bf16[4,96,768]{2,1,0:T(8,128)(2,1)S(1)}, bf16[4,96,768]{2,1,0:T(8,128)(2,1)S(1)}, u32[]{:S(2)}, u32[]{:S(2)}) collective-permute-start(bf16[4,96,768]{2,1,0:T(8,128)(2,1)S(1)} %get-tuple-element.502), channel_id=1, source_target_pairs={{0,4},{4,0},{8,12},{12,8},{16,20},{20,16},{24,28},{28,24},{1,5},{5... | collective-permute-start | bytes 1769480 | tf_op jit(solution)/shard_map/ppermute | solution.py:56
  205.7 16.2 %collective-permute-start.49 = (bf16[256,768]{1,0:T(8,128)(2,1)S(1)}, bf16[256,768]{1,0:T(8,128)(2,1)S(1)}, u32[]{:S(2)}, u32[]{:S(2)}) collective-permute-start(bf16[256,768]{1,0:T(8,128)(2,1)S(1)} %get-tuple-element.515.refs_0_), channel_id=1, source_target_pairs={{0,2},{1,3},{2,0},{3,1},{4,6},{5,7},{6,4},{7,5},{8,10},{9,11},{10,... | collective-permute-start | bytes 1179656 | tf_op jit(solution)/shard_map/ppermute | solution.py:56
  206.7 12.6 %collective-permute-start.47 = (bf16[1,96,768]{2,1,0:T(8,128)(2,1)S(1)}, bf16[1,96,768]{2,1,0:T(8,128)(2,1)S(1)}, u32[]{:S(2)}, u32[]{:S(2)}) collective-permute-start(bf16[1,96,768]{2,1,0:T(8,128)(2,1)S(1)} %get-tuple-element.506), channel_id=1, source_target_pairs={{0,16},{4,20},{8,24},{12,28},{16,0},{20,4},{24,8},{28,12},{1,17},{... | collective-permute-start | bytes 442376 | tf_op jit(solution)/shard_map/ppermute | solution.py:56
  227.6 14.1 %collective-permute-start.53 = (bf16[128,768]{1,0:T(8,128)(2,1)S(1)}, bf16[128,768]{1,0:T(8,128)(2,1)S(1)}, u32[]{:S(2)}, u32[]{:S(2)}) collective-permute-start(bf16[128,768]{1,0:T(8,128)(2,1)S(1)} %get-tuple-element.528), channel_id=1, source_target_pairs={{0,16},{4,20},{8,24},{12,28},{16,0},{20,4},{24,8},{28,12},{1,17},{... | collective-permute-start | bytes 589832 | tf_op jit(solution)/shard_map/ppermute | solution.py:56
  228.1 19.0 %collective-permute-start.54 = (bf16[128,768]{1,0:T(8,128)(2,1)S(1)}, bf16[128,768]{1,0:T(8,128)(2,1)S(1)}, u32[]{:S(2)}, u32[]{:S(2)}) collective-permute-start(bf16[128,768]{1,0:T(8,128)(2,1)S(1)} %get-tuple-element.529), channel_id=1, source_target_pairs={{0,24},{4,28},{8,16},{12,20},{16,8},{20,12},{24,0},{28,4},{1,25},{... | collective-permute-start | bytes 589832 | tf_op jit(solution)/shard_map/ppermute | solution.py:56
  (63 other events, 454.9 us)

commit v3 on v2

--- a/solution.py
+++ b/solution.py
@@ -939,6 +939,27 @@
         out_ref[...] = piece.T if turned else piece
 
 
+def unfold_both_kernel(*refs):
+    count = (len(refs) - 2) // 2
+    for i in range(2):
+        ins = refs[i * count : (i + 1) * count]
+        total = ins[0][0].astype(wide)
+        for ref in ins[1:]:
+            total = total + ref[0].astype(wide)
+        refs[2 * count + i][...] = total
+
+
+def unfold_both(first, second):
+    inside = pl.BlockSpec(memory_space=pltpu.VMEM)
+    return kernel_call(
+        unfold_both_kernel, 1.5,
+        in_specs=[inside] * (2 * len(first)),
+        out_specs=[inside] * 2,
+        out_shape=[jax.ShapeDtypeStruct(parts[0].shape[1:], wide) for parts in (first, second)],
+        name="unfold_both",
+    )(*first, *second)
+
+
 def unfold(parts, cuts):
     block = parts[0].shape[1]
     inside = pl.BlockSpec(memory_space=pltpu.VMEM)
@@ -1238,10 +1259,6 @@
             pair, gain1_sum, head_sum = done
             pairs_back.append([pair, swap(pair, "mp", 2)])
 
-    def near(pack):
-        nonlocal place
-        place, pairs_far[pack] = tie(place, pairs_far[pack])
-
     def meet(pack):
         nonlocal place
         place, grads_low[pack] = tie(place, grads_low[pack])
@@ -1262,13 +1279,10 @@
     feed(0)
     attend(packs)
     arrive(1)
-    near(2)
     feed(1)
     for step in range(2, packs):
         arrive(step)
         meet(step - 2)
-        if step + 1 < packs:
-            near(step + 1)
         feed(step)
         back(step - 2)
     meet(packs - 2)
@@ -1321,9 +1335,11 @@
     place, rel_share, tail.parts, small.got = tie(place, rel_share, tail.parts, small.got)
     small.join(tail, rel_share)
     place, inner.parts, outer.parts = tie(place, inner.parts, outer.parts)
-    whole_width = ((0, w_inner.shape[1], False),)
-    (inner_grad,), (outer_grad,) = inner.end(whole_width), outer.end(whole_width)
-    place, inner_grad, outer_grad = tie(place, inner_grad, outer_grad)
+    while inner.bits:
+        inner.step()
+    while outer.bits:
+        outer.step()
+    inner_grad, outer_grad = unfold_both(inner.parts, outer.parts)
     end(packs - 1)
     place, text_rows[-1] = tie(place, text_rows[-1])
     grad_tokens = weave_halves(place, text_rows, rows - prompt_len)

time: 259 us -> 258 us (level)
    pallas_call x34 -> x33, Pallas kernels: 162 us -> 162 us  [run(): call(*[pltpu.with_memory_space_constraint(v, pltpu.HBM) if (v.size >= lea...]
  transfers between devices with their start and end apart: 56 -> 56, of which waited for: 15 -> 15; matrix products, arithmetic and copies ran while one was open for 3% -> 3% of each run, Pallas kernels for 55% -> 56%
where the time goes in v3:
time: 258 us; the launch traced here: 253 us
  Pallas kernels  162 us (63%)
  starting transfers between devices  39.9 us (15%)
  waiting for transfers between devices  36.7 us (14%)
  local copies, waits for them, and re-layouts  10.4 us (4%)
    pallas_call x33, Pallas kernels, run(): call(*[pltpu.with_memory_space_constraint(v, pltpu.HBM) if (v.size >= lea...  162 us
    ppermute x56, starting transfers between devices, swap(): return lax.ppermute(value, axis, [(i, i ^ bit) for i in range(count)])  39.9 us
    ppermute x56, waiting for transfers between devices, swap(): return lax.ppermute(value, axis, [(i, i ^ bit) for i in range(count)])  36.7 us
  transfers between devices with their start and end apart: 56, of which 15 were waited for; matrix products, arithmetic and copies ran while one was open for 3% of the time, Pallas kernels for 56%

profile of v3, /device:TPU:8, one launch (start us, length us, event | category | flops | bytes accessed | tf_op | source)
XLA Modules:
  0.0 253.3 jit_solution(9629807560199611355)
XLA Ops:
  15.1 4.2 %text_projections.2 = (bf16[4,512,768]{2,1,0:T(8,128)(2,1)}, bf16[4,512,768]{2,1,0:T(8,128)(2,1)}, bf16[4,512,576]{2,1,0:T(8,128)(2,1)}) custom-call(bf16[4,412,768]{2,1,0:T(8,128)(2,1)} %copy.81.tokens_ref, f32[1,768]{1,0:T(1,128)S(1)} %broadcast_in_dim.31.gain_ref.refs_11_.refs_5_, bf16[576,768]{1,0:T(8,128)(2,1)} %pad_maximum_fusion.weight_ref.refs_6_.refs_0_), custom_call_target="tpu_custom_call" | custom-call | bytes 8640000 | tf_op jit(solution)/shard_map/text_projections/pallas_call | solution.py:44
  22.0 4.4 %text_projections.3 = (bf16[4,512,768]{2,1,0:T(8,128)(2,1)}, bf16[4,512,768]{2,1,0:T(8,128)(2,1)}, bf16[4,512,576]{2,1,0:T(8,128)(2,1)}) custom-call(bf16[4,412,768]{2,1,0:T(8,128)(2,1)} %copy.81.tokens_ref, f32[1,768]{1,0:T(1,128)S(1)} %broadcast_in_dim.31.gain_ref.refs_11_.refs_5_, ...), custom_call_target="tpu_custom_call", output_to_operand_aliasing={{0}: (3, {}), {1}: (4, {}), {2}: (5, {})} | custom-call | bytes 8640000 | tf_op jit(solution)/shard_map/text_projections/pallas_call | solution.py:44
  27.9 4.0 %add_prompt.1 = (bf16[4,512,768]{2,1,0:T(8,128)(2,1)}, bf16[4,512,768]{2,1,0:T(8,128)(2,1)}, bf16[4,512,576]{2,1,0:T(8,128)(2,1)}) custom-call(s32[1]{0:T(128)} %bitcast.1.place_ref, bf16[2,64,768]{2,1,0:T(8,128)(2,1)S(1)} %pad_maximum_fusion.1.pieces_ref, ...), custom_call_target="tpu_custom_call", output_to_operand_aliasing={{0}: (4, {}), {1}: (5, {}), {2}: (6, {})} | custom-call | bytes 9000000 | tf_op jit(solution)/shard_map/add_prompt/pallas_call | solution.py:44
  37.5 5.6 %attention_step.6 = (bf16[256,768]{1,0:T(8,128)(2,1)S(1)}, bf16[256,768]{1,0:T(8,128)(2,1)S(1)}, bf16[1,3,256,512]{3,2,1,0:T(8,128)(2,1)}, bf16[1,3,256,512]{3,2,1,0:T(8,128)(2,1)}, bf16[4,512,192]{2,1,0:T(8,128)(2,1)}) custom-call(s32[3]{0:T(128)S(1)} %pad_add_fusion.core_ref.place_ref, ...), custom_call_target="tpu_custom_call", output_to_operand_aliasing={{4}: (7, {})} | custom-call | bytes 18000000 | tf_op jit(solution)/shard_map/attention_step/pallas_call | solution.py:44
  45.4 6.9 %collective-permute-done.7.refs_5_.refs_8_.refs_6_ = bf16[384,768]{1,0:T(8,128)(2,1)S(1)} collective-permute-done((bf16[384,768]{1,0:T(8,128)(2,1)}, bf16[384,768]{1,0:T(8,128)(2,1)S(1)}, u32[]{:S(2)}, u32[]{:S(2)}) %collective-permute-start.7) | collective-permute-done | bytes 589856 | tf_op jit(solution)/shard_map/ppermute | solution.py:56
  52.3 5.6 %attention_step.7 = (bf16[256,768]{1,0:T(8,128)(2,1)S(1)}, bf16[256,768]{1,0:T(8,128)(2,1)S(1)}, bf16[1,3,256,512]{3,2,1,0:T(8,128)(2,1)}, bf16[1,3,256,512]{3,2,1,0:T(8,128)(2,1)}, bf16[4,512,192]{2,1,0:T(8,128)(2,1)}) custom-call(s32[3]{0:T(128)S(1)} %pad_add_fusion.core_ref.place_ref, ...), custom_call_target="tpu_custom_call", output_to_operand_aliasing={{4}: (7, {})} | custom-call | bytes 18000000 | tf_op jit(solution)/shard_map/attention_step/pallas_call | solution.py:44
  60.1 5.6 %attention_step.8 = (bf16[256,768]{1,0:T(8,128)(2,1)S(1)}, bf16[256,768]{1,0:T(8,128)(2,1)S(1)}, bf16[1,3,256,512]{3,2,1,0:T(8,128)(2,1)}, bf16[1,3,256,512]{3,2,1,0:T(8,128)(2,1)}, bf16[4,512,192]{2,1,0:T(8,128)(2,1)}) custom-call(s32[3]{0:T(128)S(1)} %pad_add_fusion.core_ref.place_ref, ...), custom_call_target="tpu_custom_call", output_to_operand_aliasing={{4}: (7, {})} | custom-call | bytes 18000000 | tf_op jit(solution)/shard_map/attention_step/pallas_call | solution.py:44
  65.7 6.3 %feed_step.5 = (bf16[4,512,768]{2,1,0:T(8,128)(2,1)}, bf16[4,512,768]{2,1,0:T(8,128)(2,1)}, bf16[4,512,768]{2,1,0:T(8,128)(2,1)}, bf16[512,768]{1,0:T(8,128)(2,1)S(1)}) custom-call(s32[3]{0:T(128)S(1)} %pad_add_fusion.core_ref.place_ref, bf16[4,512,768]{2,1,0:T(8,128)(2,1)} %get-tuple-element.312.rows_any.refs_9_.refs_3_, bf16[4,512,768]{2,1,0:T(8,128)(2,1)} %cot_any.9, ...), custom_call_target="tpu_custom_call" | custom-call | bytes 28800000 | tf_op jit(solution)/shard_map/feed_step/pallas_call | solution.py:44
  78.9 10.1 %feed_step.6 = (bf16[4,512,768]{2,1,0:T(8,128)(2,1)}, bf16[4,512,768]{2,1,0:T(8,128)(2,1)}, bf16[4,512,768]{2,1,0:T(8,128)(2,1)}, bf16[512,768]{1,0:T(8,128)(2,1...) custom-call(s32[3]{0:T(128)S(1)} %pad_add_fusion.core_ref.place_ref,, ...), custom_call_target="tpu_custom_call", output_to_operand_aliasing={{0}: (15, {}), {1}: (16, {}), {2}: (17, {})} | custom-call | bytes 43200000 | tf_op jit(solution)/shard_map/feed_step/pallas_call | solution.py:44
  93.0 10.0 %feed_step.7 = (bf16[4,512,768]{2,1,0:T(8,128)(2,1)}, bf16[4,512,768]{2,1,0:T(8,128)(2,1)}, bf16[4,512,768]{2,1,0:T(8,128)(2,1)}, bf16[512,768]{1,0:T(8,128)(2,1...) custom-call(s32[3]{0:T(128)S(1)} %pad_add_fusion.core_ref.place_ref,, ...), custom_call_target="tpu_custom_call", output_to_operand_aliasing={{0}: (15, {}), {1}: (16, {}), {2}: (17, {}), {7}: (18, {})} | custom-call | bytes 43200000 | tf_op jit(solution)/shard_map/feed_step/pallas_call | solution.py:44
  104.1 7.7 %attention_back_step.5 = (bf16[256,768]{1,0:T(8,128)(2,1)S(1)}, bf16[256,576]{1,0:T(8,128)(2,1)}, bf16[4,512,576]{2,1,0:T(8,128)(2,1)}, bf16[4,3,512,512]{3,2,1,0:T(8,128)(2,1)}, bf16[4,512,768]{2,1,0:T(8,128)(2,1)}) custom-call(s32[3]{0:T(128)S(1)} %pad_add_fusion.core_ref.place_ref, bf16[256,768]{1,0:T(8,128)(2,1)S(1)} %get-tuple-element.348.refs_0_, ...), custom_call_target="tpu_custom_call" | custom-call | bytes 21600000 | tf_op jit(solution)/shard_map/attention_back_step/pallas_call | solution.py:44
  111.9 10.0 %feed_step.8 = (bf16[4,512,768]{2,1,0:T(8,128)(2,1)}, bf16[4,512,768]{2,1,0:T(8,128)(2,1)}, bf16[4,512,768]{2,1,0:T(8,128)(2,1)}, bf16[512,768]{1,0:T(8,128)(2,1...) custom-call(s32[3]{0:T(128)S(1)} %pad_add_fusion.core_ref.place_ref,, ...), custom_call_target="tpu_custom_call", output_to_operand_aliasing={{0}: (15, {}), {1}: (16, {}), {2}: (17, {}), {7}: (18, {})} | custom-call | bytes 43200000 | tf_op jit(solution)/shard_map/feed_step/pallas_call | solution.py:44
  124.9 8.3 %attention_back_step.6 = (bf16[256,768]{1,0:T(8,128)(2,1)S(1)}, f32[1,768]{1,0:T(1,128)S(1)}, f32[128,768]{1,0:T(8,128)}, bf16[256,768]{1,0:T(8,128)(2,1)S(1)}, ...) custom-call(s32[3]{0:T(128)S(1)} %pad_add_fusion.core_ref.place_ref,, ...), custom_call_target="tpu_custom_call", output_to_operand_aliasing={{5}: (15, {}), {6}: (16, {}), {7}: (17, {})} | custom-call | bytes 21600000 | tf_op jit(solution)/shard_map/attention_back_step/pallas_call | solution.py:44
  133.2 7.6 %feed_step.9 = (bf16[4,512,768]{2,1,0:T(8,128)(2,1)}, bf16[4,512,768]{2,1,0:T(8,128)(2,1)}, bf16[4,512,768]{2,1,0:T(8,128)(2,1)}, f32[256,768]{1,0:T(8,128)}, bf...) custom-call(s32[3]{0:T(128)S(1)} %pad_add_fusion.core_ref.place_ref,, ...), custom_call_target="tpu_custom_call", output_to_operand_aliasing={{0}: (13, {}), {1}: (14, {}), {2}: (15, {}), {6}: (16, {})} | custom-call | bytes 28800000 | tf_op jit(solution)/shard_map/feed_step/pallas_call | solution.py:44
  141.6 6.3 %weight_shares.3 = (bf16[4,96,768]{2,1,0:T(8,128)(2,1)S(1)}, bf16[4,96,768]{2,1,0:T(8,128)(2,1)}) custom-call(s32[1]{0:T(128)} %bitcast.where_ref, bf16[2048,768]{1,0:T(8,128)(2,1)} %bitcast.45, bf16[2048,768]{1,0:T(8,128)(2,1)} %bitcast.47), custom_call_target="tpu_custom_call" | custom-call | bytes 21600000 | tf_op jit(solution)/shard_map/weight_shares/pallas_call | solution.py:44
  149.6 6.6 %weight_shares.4 = (bf16[4,96,768]{2,1,0:T(8,128)(2,1)S(1)}, bf16[4,96,768]{2,1,0:T(8,128)(2,1)}) custom-call(s32[1]{0:T(128)} %bitcast.where_ref, bf16[2048,768]{1,0:T(8,128)(2,1)} %bitcast.44, bf16[2048,768]{1,0:T(8,128)(2,1)} %bitcast.46), custom_call_target="tpu_custom_call" | custom-call | bytes 21600000 | tf_op jit(solution)/shard_map/weight_shares/pallas_call | solution.py:44
  157.8 8.5 %attention_back_step.7 = (bf16[256,768]{1,0:T(8,128)(2,1)}, f32[1,768]{1,0:T(1,128)S(1)}, f32[128,768]{1,0:T(8,128)}, bf16[256,768]{1,0:T(8,128)(2,1)}, bf16[256...) custom-call(s32[3]{0:T(128)S(1)} %pad_add_fusion.core_ref.place_ref,, ...), custom_call_target="tpu_custom_call", output_to_operand_aliasing={{5}: (15, {}), {6}: (16, {}), {7}: (17, {})} | custom-call | bytes 21600000 | tf_op jit(solution)/shard_map/attention_back_step/pallas_call | solution.py:44
  172.1 9.1 %attention_back_step.8 = (bf16[256,768]{1,0:T(8,128)(2,1)S(1)}, f32[1,768]{1,0:T(1,128)S(1)}, f32[128,768]{1,0:T(8,128)}, bf16[256,768]{1,0:T(8,128)(2,1)}, bf16...) custom-call(s32[3]{0:T(128)S(1)} %pad_add_fusion.core_ref.place_ref,, ...), custom_call_target="tpu_custom_call", output_to_operand_aliasing={{5}: (15, {}), {6}: (16, {}), {7}: (17, {})} | custom-call | bytes 21600000 | tf_op jit(solution)/shard_map/attention_back_step/pallas_call | solution.py:44
  184.8 7.2 %weight_shares.5 = (bf16[4,96,768]{2,1,0:T(8,128)(2,1)S(1)}, bf16[4,96,768]{2,1,0:T(8,128)(2,1)S(1)}) custom-call(s32[1]{0:T(128)} %bitcast.where_ref, bf16[2048,768]{1,0:T(8,128)(2,1)} %bitcast.52, bf16[2048,576]{1,0:T(8,128)(2,1)} %bitcast.49, bf16[2048,768]{1,0:T(8,128)(2,1)} %bitcast.48, bf16[2048,192]{1,0:T(8,128)(2,1)S(1)} %bitcast.43), custom_call_target="tpu_custom_call" | custom-call | bytes 21600000 | tf_op jit(solution)/shard_map/weight_shares/pallas_call | solution.py:44
  195.3 8.2 %middle_work.1 = (f32[3,1,1024]{2,1,0:T(1,128)S(1)}, bf16[3,256,768]{2,1,0:T(8,128)(2,1)S(1)}, bf16[4,512,768]{2,1,0:T(8,128)(2,1)}) custom-call(s32[3]{0:T(128)S(1)} %pad_add_fusion.core_ref.place_ref, bf16[4,3,512,512]{3,2,1,0:T(8,128)(2,1)} %get-tuple-element.480.scores_any, bf16[4,512,768]{2,1,0:T(8,128)(2,1)} %get-tuple-element.312.rows_any.refs_9_.refs_3_, ...), custom_call_target="tpu_custom_call" | custom-call | bytes 43200000 | tf_op jit(solution)/shard_map/middle_work/pallas_call | solution.py:44
  215.0 4.5 %collective-permute-done.44.got_ref = bf16[4,96,768]{2,1,0:T(8,128)(2,1)S(1)} collective-permute-done((bf16[4,96,768]{2,1,0:T(8,128)(2,1)S(1)}, bf16[4,96,768]{2,1,0:T(8,128)(2,1)S(1)}, u32[]{:S(2)}, u32[]{:S(2)}) %collective-permute-start.44) | collective-permute-done | bytes 589856 | tf_op jit(solution)/shard_map/ppermute | solution.py:56
  227.9 5.6 %weave_halves.1 = bf16[412,4,768]{2,1,0:T(4,128)(2,1)} custom-call(s32[3]{0:T(128)S(1)} %pad_add_fusion.core_ref.place_ref, bf16[3,256,768]{2,1,0:T(8,128)(2,1)} %copy-done.9, bf16[3,256,768]{2,1,0:T(8,128)(2,1)} %collective-permute-done.51.refs_1_, bf16[1,256,768]{2,1,0:T(8,128)(2,1)} %copy-done.8, bf16[1,256,768]{2,1,0:T(8,128)(2,1)} %collective-permute-done.50.refs_3_), custom_call_target="tpu_custom_call" | custom-call | bytes 14400000 | tf_op jit(solution)/shard_map/weave_halves/pallas_call | solution.py:44
  234.8 6.0 %collective-permute-done.53.refs_2_ = bf16[128,768]{1,0:T(8,128)(2,1)S(1)} collective-permute-done((bf16[128,768]{1,0:T(8,128)(2,1)S(1)}, bf16[128,768]{1,0:T(8,128)(2,1)S(1)}, u32[]{:S(2)}, u32[]{:S(2)}) %collective-permute-start.53) | collective-permute-done | bytes 196640 | tf_op jit(solution)/shard_map/ppermute | solution.py:56
  240.7 5.1 %collective-permute-done.54.refs_3_ = bf16[128,768]{1,0:T(8,128)(2,1)S(1)} collective-permute-done((bf16[128,768]{1,0:T(8,128)(2,1)S(1)}, bf16[128,768]{1,0:T(8,128)(2,1)S(1)}, u32[]{:S(2)}, u32[]{:S(2)}) %collective-permute-start.54) | collective-permute-done | bytes 196640 | tf_op jit(solution)/shard_map/ppermute | solution.py:56
  (234 shorter events, 88.1 us)
Async XLA Ops:
  7.5 18.9 %collective-permute-start.4 = (bf16[384,768]{1,0:T(8,128)(2,1)}, bf16[384,768]{1,0:T(8,128)(2,1)}, u32[]{:S(2)}, u32[]{:S(2)}) collective-permute-start(bf16[384,768]{1,0:T(8,128)(2,1)} %dynamic-slice_bitcast_fusion), channel_id=1, source_target_pairs={{0,2},{1,3},{2,0},{3,1},{4,6},{5,7},{6,4},{7,5},{8,10},{9,11},{10,... | collective-permute-start | bytes 1769480 | tf_op jit(solution)/shard_map/ppermute | solution.py:56
  9.9 25.8 %collective-permute-start = (bf16[384,768]{1,0:T(8,128)(2,1)}, bf16[384,768]{1,0:T(8,128)(2,1)}, u32[]{:S(2)}, u32[]{:S(2)}) collective-permute-start(bf16[384,768]{1,0:T(8,128)(2,1)} %dynamic-slice_bitcast_fusion.1), channel_id=1, source_target_pairs={{0,2},{1,3},{2,0},{3,1},{4,6},{5,7},{6,4},{7,5},{8,10},{9,11},{10,... | collective-permute-start | bytes 1769480 | tf_op jit(solution)/shard_map/ppermute | solution.py:56
  35.9 16.4 %collective-permute-start.7 = (bf16[384,768]{1,0:T(8,128)(2,1)}, bf16[384,768]{1,0:T(8,128)(2,1)S(1)}, u32[]{:S(2)}, u32[]{:S(2)}) collective-permute-start(bf16[384,768]{1,0:T(8,128)(2,1)} %collective-permute-done.4.refs_4_.refs_7_.refs_5_), channel_id=1, source_target_pairs={{0,4},{4,0},{8,12},{12,8},{16,20},{20,16},{24,28},{28,24},{1,5},{5... | collective-permute-start | bytes 1769480 | tf_op jit(solution)/shard_map/ppermute | solution.py:56
  43.3 15.2 %collective-permute-start.11 = (bf16[256,768]{1,0:T(8,128)(2,1)S(1)}, bf16[256,768]{1,0:T(8,128)(2,1)S(1)}, u32[]{:S(2)}, u32[]{:S(2)}) collective-permute-start(bf16[256,768]{1,0:T(8,128)(2,1)S(1)} %get-tuple-element.310.refs_2_), channel_id=1, source_target_pairs={{0,2},{1,3},{2,0},{3,1},{4,6},{5,7},{6,4},{7,5},{8,10},{9,11},{10,... | collective-permute-start | bytes 1179656 | tf_op jit(solution)/shard_map/ppermute | solution.py:56
  44.8 20.8 %collective-permute-start.10 = (bf16[384,768]{1,0:T(8,128)(2,1)}, bf16[384,768]{1,0:T(8,128)(2,1)S(1)}, u32[]{:S(2)}, u32[]{:S(2)}) collective-permute-start(bf16[384,768]{1,0:T(8,128)(2,1)} %collective-permute-done.refs_6_.refs_9_.refs_7_), channel_id=1, source_target_pairs={{0,4},{4,0},{8,12},{12,8},{16,20},{20,16},{24,28},{28,24},{1,5},{5... | collective-permute-start | bytes 1769480 | tf_op jit(solution)/shard_map/ppermute | solution.py:56
  58.6 14.2 %collective-permute-start.15 = (bf16[256,768]{1,0:T(8,128)(2,1)S(1)}, bf16[256,768]{1,0:T(8,128)(2,1)S(1)}, u32[]{:S(2)}, u32[]{:S(2)}) collective-permute-start(bf16[256,768]{1,0:T(8,128)(2,1)S(1)} %get-tuple-element.323.refs_2_), channel_id=1, source_target_pairs={{0,2},{1,3},{2,0},{3,1},{4,6},{5,7},{6,4},{7,5},{8,10},{9,11},{10,... | collective-permute-start | bytes 1179656 | tf_op jit(solution)/shard_map/ppermute | solution.py:56
  73.1 16.4 %collective-permute-start.19 = (bf16[256,768]{1,0:T(8,128)(2,1)S(1)}, bf16[256,768]{1,0:T(8,128)(2,1)S(1)}, u32[]{:S(2)}, u32[]{:S(2)}) collective-permute-start(bf16[256,768]{1,0:T(8,128)(2,1)S(1)} %get-tuple-element.334.refs_2_), channel_id=1, source_target_pairs={{0,2},{1,3},{2,0},{3,1},{4,6},{5,7},{6,4},{7,5},{8,10},{9,11},{10,... | collective-permute-start | bytes 1179656 | tf_op jit(solution)/shard_map/ppermute | solution.py:56
  90.0 13.6 %collective-permute-start.24 = (bf16[256,768]{1,0:T(8,128)(2,1)S(1)}, bf16[256,768]{1,0:T(8,128)(2,1)S(1)}, u32[]{:S(2)}, u32[]{:S(2)}) collective-permute-start(bf16[256,768]{1,0:T(8,128)(2,1)S(1)} %get-tuple-element.354.refs_0_), channel_id=1, source_target_pairs={{0,2},{1,3},{2,0},{3,1},{4,6},{5,7},{6,4},{7,5},{8,10},{9,11},{10,... | collective-permute-start | bytes 1179656 | tf_op jit(solution)/shard_map/ppermute | solution.py:56
  140.8 27.0 %collective-permute-start.34 = (bf16[4,256,768]{2,1,0:T(8,128)(2,1)}, bf16[4,256,768]{2,1,0:T(8,128)(2,1)}, u32[]{:S(2)}, u32[]{:S(2)}) collective-permute-start(bf16[4,256,768]{2,1,0:T(8,128)(2,1)} %get-tuple-element.419.own_ref), channel_id=1, source_target_pairs={{0,1},{1,0},{2,3},{3,2},{4,5},{5,4},{6,7},{7,6},{8,9},{9,8},{10,11... | collective-permute-start | bytes 4718600 | tf_op jit(solution)/shard_map/ppermute | solution.py:56
  141.1 15.1 %collective-permute-start.32 = (bf16[256,768]{1,0:T(8,128)(2,1)}, bf16[256,768]{1,0:T(8,128)(2,1)}, u32[]{:S(2)}, u32[]{:S(2)}) collective-permute-start(bf16[256,768]{1,0:T(8,128)(2,1)} %get-tuple-element.424.refs_0_), channel_id=1, source_target_pairs={{0,1},{1,0},{2,3},{3,2},{4,5},{5,4},{6,7},{7,6},{8,9},{9,8},{10,11... | collective-permute-start | bytes 1179656 | tf_op jit(solution)/shard_map/ppermute | solution.py:56
  141.4 16.3 %collective-permute-start.33 = (bf16[256,768]{1,0:T(8,128)(2,1)S(1)}, bf16[256,768]{1,0:T(8,128)(2,1)S(1)}, u32[]{:S(2)}, u32[]{:S(2)}) collective-permute-start(bf16[256,768]{1,0:T(8,128)(2,1)S(1)} %get-tuple-element.410), channel_id=1, source_target_pairs={{0,1},{1,0},{2,3},{3,2},{4,5},{5,4},{6,7},{7,6},{8,9},{9,8},{10,11... | collective-permute-start | bytes 1179656 | tf_op jit(solution)/shard_map/ppermute | solution.py:56
  147.9 20.0 %collective-permute-start.36 = (bf16[4,96,768]{2,1,0:T(8,128)(2,1)}, bf16[4,96,768]{2,1,0:T(8,128)(2,1)}, u32[]{:S(2)}, u32[]{:S(2)}) collective-permute-start(bf16[4,96,768]{2,1,0:T(8,128)(2,1)} %get-tuple-element.422), channel_id=1, source_target_pairs={{0,4},{4,0},{8,12},{12,8},{16,20},{20,16},{24,28},{28,24},{1,5},{5... | collective-permute-start | bytes 1769480 | tf_op jit(solution)/shard_map/ppermute | solution.py:56
  148.4 17.8 %collective-permute-start.35 = (bf16[256,768]{1,0:T(8,128)(2,1)S(1)}, bf16[256,768]{1,0:T(8,128)(2,1)S(1)}, u32[]{:S(2)}, u32[]{:S(2)}) collective-permute-start(bf16[256,768]{1,0:T(8,128)(2,1)S(1)} %get-tuple-element.482.refs_0_), channel_id=1, source_target_pairs={{0,2},{1,3},{2,0},{3,1},{4,6},{5,7},{6,4},{7,5},{8,10},{9,11},{10,... | collective-permute-start | bytes 1179656 | tf_op jit(solution)/shard_map/ppermute | solution.py:56
  156.2 26.2 %collective-permute-start.40 = (bf16[4,96,768]{2,1,0:T(8,128)(2,1)}, bf16[4,96,768]{2,1,0:T(8,128)(2,1)S(1)}, u32[]{:S(2)}, u32[]{:S(2)}) collective-permute-start(bf16[4,96,768]{2,1,0:T(8,128)(2,1)} %get-tuple-element.444), channel_id=1, source_target_pairs={{0,4},{4,0},{8,12},{12,8},{16,20},{20,16},{24,28},{28,24},{1,5},{5... | collective-permute-start | bytes 1769480 | tf_op jit(solution)/shard_map/ppermute | solution.py:56
  167.0 15.4 %collective-permute-start.38 = (bf16[256,768]{1,0:T(8,128)(2,1)}, bf16[256,768]{1,0:T(8,128)(2,1)}, u32[]{:S(2)}, u32[]{:S(2)}) collective-permute-start(bf16[256,768]{1,0:T(8,128)(2,1)} %get-tuple-element.484.refs_3_), channel_id=1, source_target_pairs={{0,2},{1,3},{2,0},{3,1},{4,6},{5,7},{6,4},{7,5},{8,10},{9,11},{10,... | collective-permute-start | bytes 1179656 | tf_op jit(solution)/shard_map/ppermute | solution.py:56
  169.7 12.7 %collective-permute-start.39 = (bf16[2,96,768]{2,1,0:T(8,128)(2,1)}, bf16[2,96,768]{2,1,0:T(8,128)(2,1)}, u32[]{:S(2)}, u32[]{:S(2)}) collective-permute-start(bf16[2,96,768]{2,1,0:T(8,128)(2,1)} %get-tuple-element.442), channel_id=1, source_target_pairs={{0,8},{4,12},{8,0},{12,4},{16,24},{20,28},{24,16},{28,20},{1,9},{5... | collective-permute-start | bytes 884744 | tf_op jit(solution)/shard_map/ppermute | solution.py:56
  181.2 14.1 %collective-permute-start.43 = (bf16[256,768]{1,0:T(8,128)(2,1)S(1)}, bf16[256,768]{1,0:T(8,128)(2,1)}, u32[]{:S(2)}, u32[]{:S(2)}) collective-permute-start(bf16[256,768]{1,0:T(8,128)(2,1)S(1)} %get-tuple-element.486.refs_6_), channel_id=1, source_target_pairs={{0,2},{1,3},{2,0},{3,1},{4,6},{5,7},{6,4},{7,5},{8,10},{9,11},{10,... | collective-permute-start | bytes 1179656 | tf_op jit(solution)/shard_map/ppermute | solution.py:56
  182.5 12.6 %collective-permute-start.42 = (bf16[2,96,768]{2,1,0:T(8,128)(2,1)S(1)}, bf16[2,96,768]{2,1,0:T(8,128)(2,1)S(1)}, u32[]{:S(2)}, u32[]{:S(2)}) collective-permute-start(bf16[2,96,768]{2,1,0:T(8,128)(2,1)S(1)} %get-tuple-element.474), channel_id=1, source_target_pairs={{0,8},{4,12},{8,0},{12,4},{16,24},{20,28},{24,16},{28,20},{1,9},{5... | collective-permute-start | bytes 884744 | tf_op jit(solution)/shard_map/ppermute | solution.py:56
  203.5 24.4 %collective-permute-start.51 = (bf16[3,256,768]{2,1,0:T(8,128)(2,1)S(1)}, bf16[3,256,768]{2,1,0:T(8,128)(2,1)}, u32[]{:S(2)}, u32[]{:S(2)}) collective-permute-start(bf16[3,256,768]{2,1,0:T(8,128)(2,1)S(1)} %get-tuple-element.505.refs_0_), channel_id=1, source_target_pairs={{0,1},{1,0},{2,3},{3,2},{4,5},{5,4},{6,7},{7,6},{8,9},{9,8},{10,11... | collective-permute-start | bytes 3538952 | tf_op jit(solution)/shard_map/ppermute | solution.py:56
  204.1 15.3 %collective-permute-start.44 = (bf16[4,96,768]{2,1,0:T(8,128)(2,1)S(1)}, bf16[4,96,768]{2,1,0:T(8,128)(2,1)S(1)}, u32[]{:S(2)}, u32[]{:S(2)}) collective-permute-start(bf16[4,96,768]{2,1,0:T(8,128)(2,1)S(1)} %get-tuple-element.493), channel_id=1, source_target_pairs={{0,4},{4,0},{8,12},{12,8},{16,20},{20,16},{24,28},{28,24},{1,5},{5... | collective-permute-start | bytes 1769480 | tf_op jit(solution)/shard_map/ppermute | solution.py:56
  205.7 15.2 %collective-permute-start.49 = (bf16[256,768]{1,0:T(8,128)(2,1)S(1)}, bf16[256,768]{1,0:T(8,128)(2,1)S(1)}, u32[]{:S(2)}, u32[]{:S(2)}) collective-permute-start(bf16[256,768]{1,0:T(8,128)(2,1)S(1)} %get-tuple-element.501.refs_0_), channel_id=1, source_target_pairs={{0,2},{1,3},{2,0},{3,1},{4,6},{5,7},{6,4},{7,5},{8,10},{9,11},{10,... | collective-permute-start | bytes 1179656 | tf_op jit(solution)/shard_map/ppermute | solution.py:56
  206.8 12.6 %collective-permute-start.47 = (bf16[1,96,768]{2,1,0:T(8,128)(2,1)S(1)}, bf16[1,96,768]{2,1,0:T(8,128)(2,1)S(1)}, u32[]{:S(2)}, u32[]{:S(2)}) collective-permute-start(bf16[1,96,768]{2,1,0:T(8,128)(2,1)S(1)} %get-tuple-element.497), channel_id=1, source_target_pairs={{0,16},{4,20},{8,24},{12,28},{16,0},{20,4},{24,8},{28,12},{1,17},{... | collective-permute-start | bytes 442376 | tf_op jit(solution)/shard_map/ppermute | solution.py:56
  226.3 14.4 %collective-permute-start.53 = (bf16[128,768]{1,0:T(8,128)(2,1)S(1)}, bf16[128,768]{1,0:T(8,128)(2,1)S(1)}, u32[]{:S(2)}, u32[]{:S(2)}) collective-permute-start(bf16[128,768]{1,0:T(8,128)(2,1)S(1)} %get-tuple-element.514), channel_id=1, source_target_pairs={{0,16},{4,20},{8,24},{12,28},{16,0},{20,4},{24,8},{28,12},{1,17},{... | collective-permute-start | bytes 589832 | tf_op jit(solution)/shard_map/ppermute | solution.py:56
  227.0 18.7 %collective-permute-start.54 = (bf16[128,768]{1,0:T(8,128)(2,1)S(1)}, bf16[128,768]{1,0:T(8,128)(2,1)S(1)}, u32[]{:S(2)}, u32[]{:S(2)}) collective-permute-start(bf16[128,768]{1,0:T(8,128)(2,1)S(1)} %get-tuple-element.515), channel_id=1, source_target_pairs={{0,24},{4,28},{8,16},{12,20},{16,8},{20,12},{24,0},{28,4},{1,25},{... | collective-permute-start | bytes 589832 | tf_op jit(solution)/shard_map/ppermute | solution.py:56
  (69 other events, 529.7 us)
